TPU v7x, 256 devices: a whole 4x4x8 slice. The times are simulated.
256 devices in a mesh: seq: 64 (over y, z_hi, x), tp: 4 (over z_lo, core).
Axes of the slice: x: 4, y: 4, z: 8 (z_hi: 4, z_lo: 2; z = z_hi * 2 + z_lo), core: 2. Of those that a mesh axis runs over, the one named last changes fastest.
Arguments:
- sequence_in: bfloat16 [16384, 4096], P('seq'), may hold values from -6 to 6
- value_proj: bfloat16 [4096, 4096], P('seq', 'tp'), may hold values from -0.09375 to 0.09375
- gate_proj: bfloat16 [4096, 4096], P('seq', 'tp'), may hold values from -0.09375 to 0.09375
- filter_response: bfloat16 [2, 256, 64, 4096], P(None, None, 'seq', 'tp'), may hold values from -6 to 6
- skip_weight: float32 [4096], P('tp'), may hold values from -1 to 1
- output_proj: bfloat16 [4096, 4096], P('tp'), may hold values from -0.09375 to 0.09375
Outputs:
- layer_out: bfloat16 [16384, 4096], P('seq', 'tp')
All inputs are finite; a program needn't handle non-finite values.
Results may differ from a plain program's by a relative error of at most 0.024.
Values may be sent and summed in bfloat16 or wider, within the bound.
No kernel may reach another device: no remote copies, remote signals or barrier semaphores. Data moves between devices by JAX's collectives and lax.ppermute only.
A program may use at most 128 MiB of HBM per device.

v0:
```python
import math

import jax
import jax.numpy as jnp
import numpy as np
from jax import lax
from jax.experimental import pallas as pl
from jax.experimental.pallas import tpu as pltpu
from jax.sharding import Mesh
from jax.sharding import PartitionSpec as P

F32 = jnp.float32
BF16 = jnp.bfloat16
SEQ = ("y", "zh", "x")
SLABS = ("y", "zh")
SWAP = [(0, 1), (1, 0)]


def shift(count):
    return [(i, (i + count) % 4) for i in range(4)]


def tie(*arrays):
    return lax.optimization_barrier(arrays)


def in_hbm(arrays):
    return [pltpu.with_memory_space_constraint(a, pltpu.HBM) for a in arrays]


def spread(first, second):
    rows, cols = first.shape
    both = jnp.stack([first, second]).reshape(2, rows, 4, cols // 4).transpose(2, 0, 1, 3)
    both = jnp.broadcast_to(both[None], (4, 4, 2, rows, cols // 4))
    both = lax.all_to_all(
        both.reshape(16, 2, rows, cols // 4), ("zh", "x"), 0, 0, tiled=True
    )
    return tuple(both[:, at].reshape(16 * rows, cols // 4) for at in range(2))


def project_kernel(own_ref, act_ref, *refs):
    w_refs, (out, a_buf, w_buf, sems) = refs[:-4], refs[-4:]
    rows, block = a_buf.shape[1], w_buf.shape[0] // len(w_refs)
    copies = []
    for step, source in enumerate(w_refs):
        row = pl.multiple_of(lax.rem(own_ref[0] + 4 - step, 4) * block, 16)
        copies.append((source, w_buf.at[pl.ds(row, block)]))
    for part in range(4):
        copies.append((act_ref.at[pl.ds(part * rows, rows)], a_buf.at[part]))
    copies = [
        pltpu.make_async_copy(src, dst, sems.at[at]) for at, (src, dst) in enumerate(copies)
    ]
    for copy in copies:
        copy.start()
    for copy in copies[: len(w_refs)]:
        copy.wait()
    for part in range(4):
        copies[len(w_refs) + part].wait()
        prod = jnp.dot(a_buf[part], w_buf[...], preferred_element_type=F32)
        out[:, part] = prod.T.astype(BF16).reshape(16, 16, rows)


def project(own, act, weights):
    rows, depth = act.shape[0] // 4, act.shape[1]
    cols = weights[0].shape[1]
    count = len(weights) + 4
    return pl.pallas_call(
        project_kernel,
        out_shape=jax.ShapeDtypeStruct((16, 4, cols // 16, rows), BF16),
        in_specs=[pl.BlockSpec(memory_space=pltpu.SMEM)]
        + [pl.BlockSpec(memory_space=pltpu.HBM)] * (len(weights) + 1),
        out_specs=pl.BlockSpec(memory_space=pltpu.VMEM),
        scratch_shapes=[
            pltpu.VMEM((4, rows, depth), BF16),
            pltpu.VMEM((depth, cols), BF16),
            pltpu.SemaphoreType.DMA((count,)),
        ],
        compiler_params=pltpu.CompilerParams(vmem_limit_bytes=40 * 1024 * 1024),
    )(own.reshape(1), *in_hbm([act, *weights]))


def give_kernel(at_ref, *refs):
    pieces, (weight_ref, home_ref, give_ref, w_buf, sems) = refs[:4], refs[4:]
    own_x, own_c = at_ref[1], at_ref[2]
    width = w_buf.shape[2]
    copies = []
    for block in range(2):
        col = pl.multiple_of((2 * block + 1 - own_c) * width, 128)
        copies.append(
            pltpu.make_async_copy(
                weight_ref.at[:, pl.ds(col, width)], w_buf.at[block], sems.at[block]
            )
        )
        copies[-1].start()
    for step in range(4):
        src = lax.rem(own_x + 4 - step, 4)
        col = pl.multiple_of(src * 256, 128)
        home_ref[:, pl.ds(col, 256)] = pieces[step][...].astype(F32).T.astype(BF16)
    for block in range(2):
        copies[block].wait()
        give_ref[block] = jnp.dot(
            home_ref[...], w_buf[block], preferred_element_type=F32
        ).astype(BF16)


def home_and_give(at, pieces, weight):
    rows = pieces[0].shape[1]
    inside = pl.BlockSpec(memory_space=pltpu.VMEM)
    return pl.pallas_call(
        give_kernel,
        out_shape=(
            jax.ShapeDtypeStruct((rows, 1024), BF16),
            jax.ShapeDtypeStruct((2, rows, 1024), BF16),
        ),
        in_specs=[pl.BlockSpec(memory_space=pltpu.SMEM)]
        + [inside] * 4
        + [pl.BlockSpec(memory_space=pltpu.HBM)],
        out_specs=(inside, inside),
        scratch_shapes=[pltpu.VMEM((2, 1024, 1024), BF16), pltpu.SemaphoreType.DMA((2,))],
        compiler_params=pltpu.CompilerParams(vmem_limit_bytes=32 * 1024 * 1024),
    )(at, *pieces, *in_hbm([weight]))


def keep_kernel(at_ref, home_ref, weight_ref, away_ref, mine_ref, w_buf, sems):
    own_z, own_c = at_ref[3], at_ref[2]
    width = w_buf.shape[2]
    copies = []
    for block in range(2):
        chip = lax.rem(own_z + 1 + block, 2)
        col = pl.multiple_of((2 * chip + own_c) * width, 128)
        copies.append(
            pltpu.make_async_copy(
                weight_ref.at[:, pl.ds(col, width)], w_buf.at[block], sems.at[block]
            )
        )
        copies[-1].start()
    for block, out_ref in enumerate((away_ref, mine_ref)):
        copies[block].wait()
        out_ref[...] = jnp.dot(home_ref[...], w_buf[block], preferred_element_type=F32)


def keep(at, home, weight):
    rows = home.shape[0]
    inside = pl.BlockSpec(memory_space=pltpu.VMEM)
    one = jax.ShapeDtypeStruct((rows, 1024), F32)
    return pl.pallas_call(
        keep_kernel,
        out_shape=(one, one),
        in_specs=[
            pl.BlockSpec(memory_space=pltpu.SMEM),
            inside,
            pl.BlockSpec(memory_space=pltpu.HBM),
        ],
        out_specs=(inside, inside),
        scratch_shapes=[pltpu.VMEM((2, 1024, 1024), BF16), pltpu.SemaphoreType.DMA((2,))],
        compiler_params=pltpu.CompilerParams(vmem_limit_bytes=32 * 1024 * 1024),
    )(at, home, *in_hbm([weight]))


def inner_tables(count):
    idx = np.arange(count)
    angle = (idx[:, None] * idx[None, :] % count) * (2.0 * math.pi / count)
    cos, sin = np.cos(angle), np.sin(angle)
    ahead = np.block([[cos, -sin], [sin, cos]])
    back = np.block([[cos, sin], [-sin, cos]])
    return jnp.asarray(ahead, BF16), jnp.asarray(back, BF16)


def mm(left, right):
    return jnp.dot(left, right, preferred_element_type=F32)


def body(sequence_in, value_proj, gate_proj, filter_response, skip_weight, output_proj):
    rows = sequence_in.shape[0]
    half = rows // 2
    my_y, my_x, my_zl, my_c = (lax.axis_index(a) for a in ("y", "x", "zl", "c"))
    at = jnp.stack([my_y, my_x, my_c, my_zl])

    act = lax.dynamic_slice(sequence_in, (my_c * half, 0), (half, sequence_in.shape[1]))
    act = lax.all_gather(act, ("x", "c"), axis=0, tiled=True)

    resp = filter_response[:, :, 0, :].reshape(2, rows, 4, 16, 16)
    resp = resp.transpose(3, 2, 4, 0, 1).reshape(64, 16, 2 * rows)

    w_y, g_y = spread(value_proj, gate_proj)
    w_y, resp = tie(w_y, resp)
    w_all = [lax.ppermute(w_y, "y", shift(step)) if step else w_y for step in range(4)]
    resp = lax.all_to_all(resp, SEQ, 0, 0, tiled=True)
    *w_all, resp = tie(*w_all, resp)
    value = project(my_y, act, w_all)
    g_all = lax.all_gather(g_y, "y", axis=0, tiled=True)
    full = rows * 64

    slabs = lax.all_to_all(value, SLABS, 0, 0, tiled=True)
    slabs = slabs.reshape(64, 16, rows)

    resp = resp.astype(F32)
    s_idx = lax.iota(jnp.int32, 64)
    k_idx = lax.iota(jnp.int32, 64)

    def slab_table(order):
        angle = (k_idx[:, None] * order[None, :] % 64).astype(F32) * (2.0 * math.pi / 64)
        return jnp.concatenate([jnp.cos(angle), -jnp.sin(angle)])

    first = slab_table(s_idx).astype(BF16)
    last = (slab_table(s_idx) / full).astype(BF16)
    r_idx = lax.iota(jnp.int32, rows)
    twist = (k_idx[:, None] * r_idx[None, :]).astype(F32) * (2.0 * math.pi / full)
    t_cos, t_sin = jnp.cos(twist)[:, None, :], jnp.sin(twist)[:, None, :]
    ahead, back = inner_tables(rows)

    sect = jnp.einsum("ks,scr->kcr", first, slabs, preferred_element_type=F32)
    re, im = sect[:64], sect[64:]
    turned = jnp.concatenate([re * t_cos + im * t_sin, im * t_cos - re * t_sin], axis=2)
    spec = mm(turned.astype(BF16), ahead)
    re, im = spec[..., :rows], spec[..., rows:]
    h_re, h_im = resp[..., :rows], resp[..., rows:]
    prod = jnp.concatenate([re * h_re - im * h_im, re * h_im + im * h_re], axis=2)
    inv = mm(prod.astype(BF16), back)
    re, im = inv[..., :rows], inv[..., rows:]
    reverted = jnp.concatenate([re * t_cos - im * t_sin, re * t_sin + im * t_cos], axis=0)
    conv = jnp.einsum("ks,kcr->scr", last, reverted.astype(BF16), preferred_element_type=F32)
    conv = lax.all_to_all(
        conv.astype(BF16).reshape(16, 4, 16, rows), SLABS, 0, 0, tiled=True
    )

    gate = project(my_y * 0, act, [g_all])
    skip = lax.dynamic_slice(skip_weight, (my_x * 256,), (256,)).reshape(16, 1, 16, 1)
    mixed = (gate.astype(F32) * (conv.astype(F32) + skip * value.astype(F32))).astype(BF16)

    pieces = []
    for step in range(4):
        piece = lax.dynamic_index_in_dim(mixed, (my_x + step) % 4, 1, keepdims=False)
        piece = piece.reshape(256, rows)
        pieces.append(lax.ppermute(piece, "x", shift(step)) if step else piece)

    home, give = home_and_give(at, pieces, output_proj)
    got = lax.ppermute(give, "c", SWAP)
    away, mine = keep(at, home, output_proj)
    got_away = lax.dynamic_index_in_dim(got, 1 - my_zl, 0, keepdims=False)
    got_mine = lax.dynamic_index_in_dim(got, my_zl, 0, keepdims=False)
    back = lax.ppermute((away + got_away.astype(F32)).astype(BF16), "zl", SWAP)
    return (mine + got_mine.astype(F32) + back.astype(F32)).astype(BF16)


def solution(mesh):
    fine = Mesh(mesh.devices.reshape(4, 4, 4, 2, 2), ("y", "zh", "x", "zl", "c"))
    tp = ("zl", "c")
    placed = (
        P(SEQ, None),
        P(SEQ, tp),
        P(SEQ, tp),
        P(None, None, SEQ, tp),
        P(tp),
        P(tp, None),
    )
    return jax.shard_map(
        body, mesh=fine, in_specs=placed, out_specs=P(SEQ, tp), check_vma=False
    )
```

profile of v0, /device:TPU:1, one launch (start us, length us, event | category | flops | bytes accessed | tf_op | source)
XLA Modules:
  0.0 212.4 jit_solution(5107308159136478251)
XLA Ops:
  7.4 1.6 copy-done
  9.0 1.1 constant_dynamic-slice_fusion.4
  10.1 0.0 all-gather.3.cloned.1.call-update
  10.1 0.1 stack.29
  10.2 0.1 stack.30
  10.3 0.2 maximum_bitcast_fusion
  10.5 1.1 broadcast_in_dim.2
  11.6 11.6 %all-to-all-start = ((bf16[16,2,64,256]{3,2,1,0:T(8,128)(2,1)}), bf16[16,2,64,256]{3,2,1,0:T(8,128)(2,1)S(1)}, u32[]{:S(2)}, u32[]{:S(2)}) async-start(bf16[16,2,64,256]{3,2,1,0:T(8,128)(2,1)} %bitcast.5), calls=%async_computation | async-start | bytes 2097152 | tf_op jit(solution)/shard_map/all_to_all | solution.py:35
  23.2 2.3 %copy.25 = bf16[2,256,1,1024]{1,3,0,2:T(8,128)(2,1)} copy(bf16[2,256,1,1024]{3,1,2,0:T(8,128)(2,1)} %param.11) | data formatting | bytes 2097152 | tf_op args[3]
  25.5 3.4 %copy.26 = bf16[16,4,16,2,256]{4,3,2,1,0:T(2,128)(2,1)} copy(bf16[16,4,16,2,256]{4,2,0,1,3:T(8,128)(2,1)} %bitcast.35) | data formatting | bytes 2097152 | tf_op jit(solution)/shard_map/transpose | solution.py:183
  28.9 2.6 %reshape.65 = bf16[64,16,512]{2,1,0:T(8,128)(2,1)} reshape(bf16[16,4,16,2,256]{4,3,2,1,0:T(2,128)(2,1)} %copy.26) | data formatting | bytes 2097152 | tf_op jit(solution)/shard_map/reshape | solution.py:183
  31.5 17.1 %all-to-all-done = bf16[16,2,64,256]{3,2,1,0:T(8,128)(2,1)S(1)} async-done(((bf16[16,2,64,256]{3,2,1,0:T(8,128)(2,1)}), bf16[16,2,64,256]{3,2,1,0:T(8,128)(2,1)S(1)}, u32[]{:S(2)}, u32[]{:S(2)}) %all-to-all-start) | async-done | bytes 1048608 | tf_op jit(solution)/shard_map/all_to_all | solution.py:35
  48.6 1.0 fusion.30
  49.6 11.4 %all-to-all-start.1 = ((bf16[64,16,512]{2,1,0:T(8,128)(2,1)}), bf16[64,16,512]{2,1,0:T(8,128)(2,1)S(1)}, u32[]{:S(2)}, u32[]{:S(2)}) async-start(bf16[64,16,512]{2,1,0:T(8,128)(2,1)} %reshape.65), calls=%async_computation.1 | async-start | bytes 2097152 | tf_op jit(solution)/shard_map/all_to_all | solution.py:188
  61.0 2.5 %collective-permute-start.2 = (bf16[1024,256]{1,0:T(8,128)(2,1)}, bf16[1024,256]{1,0:T(8,128)(2,1)}, u32[]{:S(2)}, u32[]{:S(2)}) collective-permute-start(bf16[1024,256]{1,0:T(8,128)(2,1)} %bitcast.36), channel_id=1, source_target_pairs={{0,192},{64,0},{128,64},{192,128},{1,193},{65,1},{129,65},{193,129... | collective-permute-start | bytes 1572872 | tf_op jit(solution)/shard_map/ppermute | solution.py:187
  63.5 0.4 collective-permute-start.1
  63.9 0.7 collective-permute-start
  64.6 15.5 %collective-permute-done.2.refs_3_ = bf16[1024,256]{1,0:T(8,128)(2,1)} collective-permute-done((bf16[1024,256]{1,0:T(8,128)(2,1)}, bf16[1024,256]{1,0:T(8,128)(2,1)}, u32[]{:S(2)}, u32[]{:S(2)}) %collective-permute-start.2) | collective-permute-done | bytes 524320 | tf_op jit(solution)/shard_map/ppermute | solution.py:187
  80.1 2.4 %collective-permute-done.1.refs_2_ = bf16[1024,256]{1,0:T(8,128)(2,1)} collective-permute-done((bf16[1024,256]{1,0:T(8,128)(2,1)}, bf16[1024,256]{1,0:T(8,128)(2,1)}, u32[]{:S(2)}, u32[]{:S(2)}) %collective-permute-start.1) | collective-permute-done | bytes 524320 | tf_op jit(solution)/shard_map/ppermute | solution.py:187
  82.5 18.4 %collective-permute-done.refs_1_ = bf16[1024,256]{1,0:T(8,128)(2,1)} collective-permute-done((bf16[1024,256]{1,0:T(8,128)(2,1)}, bf16[1024,256]{1,0:T(8,128)(2,1)}, u32[]{:S(2)}, u32[]{:S(2)}) %collective-permute-start) | collective-permute-done | bytes 524320 | tf_op jit(solution)/shard_map/ppermute | solution.py:187
  100.9 8.3 %shard_map.83 = bf16[16,4,16,256]{3,2,1,0:T(8,128)(2,1)} custom-call(s32[1]{0:T(128)} %bitcast.own_ref, bf16[1024,4096]{1,0:T(8,128)(2,1)} %all-gather.3.cloned.1.call-done.act_ref, bf16[1024,256]{1,0:T(8,128)(2,1)} %bitcast.39, bf16[1024,256]{1,0:T(8,128)(2,1)} %collective-permute-done.refs_1_, bf16[1024,256]{1,0:T(8,128)(2,1)} %collective-permute-done.1.refs_2_, ...), custom_call_target="tpu_custom_call" | custom-call | tf_op jit(solution)/shard_map/pallas_call | solution.py:67
  109.3 6.0 %all-to-all-start.2 = ((bf16[16,4,16,256]{3,2,1,0:T(8,128)(2,1)}), bf16[16,4,16,256]{3,2,1,0:T(8,128)(2,1)}, u32[]{:S(2)}, u32[]{:S(2)}) async-start(bf16[16,4,16,256]{3,2,1,0:T(8,128)(2,1)} %shard_map.83), calls=%async_computation.2 | async-start | bytes 1048576 | tf_op jit(solution)/shard_map/all_to_all | solution.py:194
  115.2 0.2 all-gather.5.cloned.1.call-start
  115.5 0.1 sine_negate_fusion
  115.6 0.2 fusion.12
  115.9 0.0 all-gather.5.cloned.1.call-update
  115.9 1.7 convert_element_type.83
  117.6 14.4 %all-to-all-done.2 = bf16[16,4,16,256]{3,2,1,0:T(8,128)(2,1)} async-done(((bf16[16,4,16,256]{3,2,1,0:T(8,128)(2,1)}), bf16[16,4,16,256]{3,2,1,0:T(8,128)(2,1)}, u32[]{:S(2)}, u32[]{:S(2)}) %all-to-all-start.2) | async-done | bytes 524320 | tf_op jit(solution)/shard_map/all_to_all | solution.py:194
  131.9 1.6 fusion.10
  133.5 0.3 add_convert_fusion.2
  133.9 0.1 pad_maximum_fusion
  134.0 0.6 copy-done.5
  134.6 0.8 fusion.8
  135.4 0.8 copy-done.3
  136.2 0.4 subtract_convert_fusion.1
  136.6 0.1 pad_maximum_fusion.1
  136.7 0.9 copy-done.4
  137.6 0.8 fusion.6
  138.4 0.3 subtract_convert_fusion
  138.7 0.4 convolution_convert_fusion
  139.1 1.1 copy.31
  140.2 5.0 %all-to-all-start.3 = ((bf16[16,4,16,256]{3,2,1,0:T(8,128)(2,1)}), bf16[16,4,16,256]{3,2,1,0:T(8,128)(2,1)S(1)}, u32[]{:S(2)}, u32[]{:S(2)}) async-start(bf16[16,4,16,256]{3,2,1,0:T(8,128)(2,1)} %bitcast.15), calls=%async_computation.3 | async-start | bytes 1048576 | tf_op jit(solution)/shard_map/all_to_all | solution.py:223
  145.2 0.8 dynamic_slice.27
  146.0 0.1 mul.241
  146.1 6.6 %all-gather.5.cloned.1.call-done.refs_0_ = bf16[4096,256]{1,0:T(8,128)(2,1)} async-done(((bf16[1024,256]{1,0:T(8,128)(2,1)}), bf16[4096,256]{1,0:T(8,128)(2,1)}) %all-gather.5.cloned.1.call-update) | async-done | bytes 2097168 | tf_op jit(solution)/shard_map/all_gather | solution.py:191
  152.7 7.5 %shard_map.82 = bf16[16,4,16,256]{3,2,1,0:T(8,128)(2,1)S(1)} custom-call(s32[1]{0:T(128)} %constant.85.clone.1.own_ref, bf16[1024,4096]{1,0:T(8,128)(2,1)} %all-gather.3.cloned.1.call-done.act_ref, bf16[4096,256]{1,0:T(8,128)(2,1)} %all-gather.5.cloned.1.call-done.refs_0_), custom_call_target="tpu_custom_call" | custom-call | tf_op jit(solution)/shard_map/pallas_call | solution.py:67
  160.2 3.2 %all-to-all-done.3 = bf16[16,4,16,256]{3,2,1,0:T(8,128)(2,1)S(1)} async-done(((bf16[16,4,16,256]{3,2,1,0:T(8,128)(2,1)}), bf16[16,4,16,256]{3,2,1,0:T(8,128)(2,1)S(1)}, u32[]{:S(2)}, u32[]{:S(2)}) %all-to-all-start.3) | async-done | bytes 524320 | tf_op jit(solution)/shard_map/all_to_all | solution.py:223
  163.4 1.3 multiply_convert_fusion
  164.8 2.0 collective-permute-start.4
  166.8 0.9 collective-permute-start.5
  167.7 0.5 collective-permute-start.3
  168.3 0.1 pad_add_fusion.at_ref
  168.3 2.3 %collective-permute-done.4.refs_2_ = bf16[256,256]{1,0:T(8,128)(2,1)S(1)} collective-permute-done((bf16[256,256]{1,0:T(8,128)(2,1)S(1)}, bf16[256,256]{1,0:T(8,128)(2,1)S(1)}, u32[]{:S(2)}, u32[]{:S(2)}) %collective-permute-start.4) | collective-permute-done | bytes 131104 | tf_op jit(solution)/shard_map/ppermute | solution.py:235
  170.6 1.9 collective-permute-done.5.refs_3_
  172.5 1.0 collective-permute-done.3.refs_1_
  173.5 4.6 %shard_map.84 = (bf16[256,1024]{1,0:T(8,128)(2,1)S(1)}, bf16[2,256,1024]{2,1,0:T(8,128)(2,1)}) custom-call(s32[4]{0:T(128)S(1)} %pad_add_fusion.at_ref, bf16[256,256]{1,0:T(8,128)(2,1)S(1)} %bitcast.34, bf16[256,256]{1,0:T(8,128)(2,1)S(1)} %collective-permute-done.3.refs_1_, bf16[256,256]{1,0:T(8,128)(2,1)S(1)} %collective-permute-done.4.refs_2_, ...), custom_call_target="tpu_custom_call" | custom-call | tf_op jit(solution)/shard_map/pallas_call | solution.py:109
  178.1 0.8 copy-done.1
  178.9 2.1 collective-permute-start.6
  181.0 1.0 copy-done.2
  182.1 3.6 %shard_map.85 = (f32[256,1024]{1,0:T(8,128)S(1)}, f32[256,1024]{1,0:T(8,128)S(1)}) custom-call(s32[4]{0:T(128)S(1)} %pad_add_fusion.at_ref, bf16[256,1024]{1,0:T(8,128)(2,1)S(1)} %copy-done.2, bf16[1024,4096]{1,0:T(8,128)(2,1)} %weight_ref.1), custom_call_target="tpu_custom_call" | custom-call | tf_op jit(solution)/shard_map/pallas_call | solution.py:146
  185.7 2.0 fusion.3
  187.7 2.4 %collective-permute-start.7 = (bf16[256,1024]{1,0:T(8,128)(2,1)}, bf16[256,1024]{1,0:T(8,128)(2,1)}, u32[]{:S(2)}, u32[]{:S(2)}) collective-permute-start(bf16[256,1024]{1,0:T(8,128)(2,1)} %fusion.3), channel_id=1, source_target_pairs={{0,2},{2,0},{1,3},{3,1},{4,6},{6,4},{5,7},{7,5},{8,10},{10,8},{9,1... | collective-permute-start | bytes 1572872 | tf_op jit(solution)/shard_map/ppermute | solution.py:242
  190.1 12.6 %collective-permute-done.7 = bf16[256,1024]{1,0:T(8,128)(2,1)} collective-permute-done((bf16[256,1024]{1,0:T(8,128)(2,1)}, bf16[256,1024]{1,0:T(8,128)(2,1)}, u32[]{:S(2)}, u32[]{:S(2)}) %collective-permute-start.7) | collective-permute-done | bytes 524320 | tf_op jit(solution)/shard_map/ppermute | solution.py:242
  202.7 2.3 %fusion.5 = bf16[256,1024]{1,0:T(8,128)(2,1)} fusion(f32[256,1024]{1,0:T(8,128)S(1)} %get-tuple-element.24, bf16[256,1024]{1,0:T(8,128)(2,1)} %collective-permute-done.7, bf16[2,256,1024]{2,1,0:T(8,128)(2,1)} %collective-permute-done.6, s32[]{:T(128)S(6)} %select_n.66), kind=kLoop, calls=%fused_computation.10 | loop fusion | flops 1310720 | bytes 2621444 | tf_op jit(solution)/shard_map/convert_element_type | solution.py:243
  (16 shorter events, 0.1 us)
Async XLA Ops:
  7.4 1.6 copy-start
  7.4 2.7 %copy-start.6 = (bf16[64,1024]{1,0:T(8,128)(2,1)S(1)}, bf16[64,1024]{1,0:T(8,128)(2,1)}, u32[]{:S(2)}) copy-start(bf16[64,1024]{1,0:T(8,128)(2,1)} %param.9) | copy-start | bytes 393220
  7.4 2.8 %copy-start.7 = (bf16[64,1024]{1,0:T(8,128)(2,1)S(1)}, bf16[64,1024]{1,0:T(8,128)(2,1)}, u32[]{:S(2)}) copy-start(bf16[64,1024]{1,0:T(8,128)(2,1)} %param.10) | copy-start | bytes 393220
  7.4 93.6 %all-gather.3.cloned.1.call-start = ((), (), s32[]{:S(2)}) async-start(), calls=%async_computation.4 | async-start | bytes 9437184 | tf_op jit(solution)/shard_map/all_gather | solution.py:180
  11.6 37.0 %all-to-all-start = ((bf16[16,2,64,256]{3,2,1,0:T(8,128)(2,1)}), bf16[16,2,64,256]{3,2,1,0:T(8,128)(2,1)S(1)}, u32[]{:S(2)}, u32[]{:S(2)}) async-start(bf16[16,2,64,256]{3,2,1,0:T(8,128)(2,1)} %bitcast.5), calls=%async_computation | async-start | bytes 2097152 | tf_op jit(solution)/shard_map/all_to_all | solution.py:35
  49.6 51.3 %all-to-all-start.1 = ((bf16[64,16,512]{2,1,0:T(8,128)(2,1)}), bf16[64,16,512]{2,1,0:T(8,128)(2,1)S(1)}, u32[]{:S(2)}, u32[]{:S(2)}) async-start(bf16[64,16,512]{2,1,0:T(8,128)(2,1)} %reshape.65), calls=%async_computation.1 | async-start | bytes 2097152 | tf_op jit(solution)/shard_map/all_to_all | solution.py:188
  61.0 19.1 %collective-permute-start.2 = (bf16[1024,256]{1,0:T(8,128)(2,1)}, bf16[1024,256]{1,0:T(8,128)(2,1)}, u32[]{:S(2)}, u32[]{:S(2)}) collective-permute-start(bf16[1024,256]{1,0:T(8,128)(2,1)} %bitcast.36), channel_id=1, source_target_pairs={{0,192},{64,0},{128,64},{192,128},{1,193},{65,1},{129,65},{193,129... | collective-permute-start | bytes 1572872 | tf_op jit(solution)/shard_map/ppermute | solution.py:187
  63.5 19.0 %collective-permute-start.1 = (bf16[1024,256]{1,0:T(8,128)(2,1)}, bf16[1024,256]{1,0:T(8,128)(2,1)}, u32[]{:S(2)}, u32[]{:S(2)}) collective-permute-start(bf16[1024,256]{1,0:T(8,128)(2,1)} %bitcast.37), channel_id=1, source_target_pairs={{0,128},{64,192},{128,0},{192,64},{1,129},{65,193},{129,1},{193,65... | collective-permute-start | bytes 1572872 | tf_op jit(solution)/shard_map/ppermute | solution.py:187
  63.9 37.0 %collective-permute-start = (bf16[1024,256]{1,0:T(8,128)(2,1)}, bf16[1024,256]{1,0:T(8,128)(2,1)}, u32[]{:S(2)}, u32[]{:S(2)}) collective-permute-start(bf16[1024,256]{1,0:T(8,128)(2,1)} %bitcast.38), channel_id=1, source_target_pairs={{0,64},{64,128},{128,192},{192,0},{1,65},{65,129},{129,193},{193,1... | collective-permute-start | bytes 1572872 | tf_op jit(solution)/shard_map/ppermute | solution.py:187
  109.3 22.7 %all-to-all-start.2 = ((bf16[16,4,16,256]{3,2,1,0:T(8,128)(2,1)}), bf16[16,4,16,256]{3,2,1,0:T(8,128)(2,1)}, u32[]{:S(2)}, u32[]{:S(2)}) async-start(bf16[16,4,16,256]{3,2,1,0:T(8,128)(2,1)} %shard_map.83), calls=%async_computation.2 | async-start | bytes 1048576 | tf_op jit(solution)/shard_map/all_to_all | solution.py:194
  115.2 37.5 %all-gather.5.cloned.1.call-start = ((), (), s32[]{:S(2)}) async-start(), calls=%async_computation.5 | async-start | bytes 2621440 | tf_op jit(solution)/shard_map/all_gather | solution.py:191
  133.5 1.0 copy-start.5
  134.6 1.6 copy-start.3
  136.6 1.1 copy-start.4
  140.2 23.2 %all-to-all-start.3 = ((bf16[16,4,16,256]{3,2,1,0:T(8,128)(2,1)}), bf16[16,4,16,256]{3,2,1,0:T(8,128)(2,1)S(1)}, u32[]{:S(2)}, u32[]{:S(2)}) async-start(bf16[16,4,16,256]{3,2,1,0:T(8,128)(2,1)} %bitcast.15), calls=%async_computation.3 | async-start | bytes 1048576 | tf_op jit(solution)/shard_map/all_to_all | solution.py:223
  164.8 5.9 %collective-permute-start.4 = (bf16[256,256]{1,0:T(8,128)(2,1)S(1)}, bf16[256,256]{1,0:T(8,128)(2,1)S(1)}, u32[]{:S(2)}, u32[]{:S(2)}) collective-permute-start(bf16[256,256]{1,0:T(8,128)(2,1)S(1)} %bitcast.43), channel_id=1, source_target_pairs={{0,8},{4,12},{8,0},{12,4},{1,9},{5,13},{9,1},{13,5},{2,10},{6,14},... | collective-permute-start | bytes 393224 | tf_op jit(solution)/shard_map/ppermute | solution.py:235
  166.8 5.7 %collective-permute-start.5 = (bf16[256,256]{1,0:T(8,128)(2,1)S(1)}, bf16[256,256]{1,0:T(8,128)(2,1)S(1)}, u32[]{:S(2)}, u32[]{:S(2)}) collective-permute-start(bf16[256,256]{1,0:T(8,128)(2,1)S(1)} %bitcast.42), channel_id=1, source_target_pairs={{0,12},{4,0},{8,4},{12,8},{1,13},{5,1},{9,5},{13,9},{2,14},{6,2},{... | collective-permute-start | bytes 393224 | tf_op jit(solution)/shard_map/ppermute | solution.py:235
  167.7 5.8 %collective-permute-start.3 = (bf16[256,256]{1,0:T(8,128)(2,1)S(1)}, bf16[256,256]{1,0:T(8,128)(2,1)S(1)}, u32[]{:S(2)}, u32[]{:S(2)}) collective-permute-start(bf16[256,256]{1,0:T(8,128)(2,1)S(1)} %bitcast.41), channel_id=1, source_target_pairs={{0,4},{4,8},{8,12},{12,0},{1,5},{5,9},{9,13},{13,1},{2,6},{6,10},{... | collective-permute-start | bytes 393224 | tf_op jit(solution)/shard_map/ppermute | solution.py:235
  178.1 0.8 copy-start.1
  178.9 6.7 %collective-permute-start.6 = (bf16[2,256,1024]{2,1,0:T(8,128)(2,1)}, bf16[2,256,1024]{2,1,0:T(8,128)(2,1)}, u32[]{:S(2)}, u32[]{:S(2)}) collective-permute-start(bf16[2,256,1024]{2,1,0:T(8,128)(2,1)} %get-tuple-element.25), channel_id=1, source_target_pairs={{0,1},{1,0},{2,3},{3,2},{4,5},{5,4},{6,7},{7,6},{8,9},{9,8},{10,11... | collective-permute-start | bytes 3145736 | tf_op jit(solution)/shard_map/ppermute | solution.py:238
  181.0 1.0 copy-start.2
  187.7 15.0 %collective-permute-start.7 = (bf16[256,1024]{1,0:T(8,128)(2,1)}, bf16[256,1024]{1,0:T(8,128)(2,1)}, u32[]{:S(2)}, u32[]{:S(2)}) collective-permute-start(bf16[256,1024]{1,0:T(8,128)(2,1)} %fusion.3), channel_id=1, source_target_pairs={{0,2},{2,0},{1,3},{3,1},{4,6},{6,4},{5,7},{7,5},{8,10},{10,8},{9,1... | collective-permute-start | bytes 1572872 | tf_op jit(solution)/shard_map/ppermute | solution.py:242
Sparse Core Ops, SparseCore 0:
  10.2 69.2 all-gather.2
Sparse Core Ops, SparseCore 1:
  117.5 35.1 all-gather.4
where the time goes:
time: 213 us; the launch traced here: 212 us
  waiting for transfers between devices  95.4 us (45%)
  starting transfers between devices  45.8 us (22%)
  Pallas kernels  24 us (11%)
  local copies, waits for them, and re-layouts  19.4 us (9%)
  between operations  15.1 us (7%)
  other arithmetic  9.14 us (4%)
  matrix products  3.52 us (2%)
    ppermute x3, waiting for transfers between devices, body(): lax.ppermute(w_y, 'y', shift(step))  36.4 us
    all_to_all x1, waiting for transfers between devices, spread(): lax.all_to_all(both.reshape(16, 2, rows, cols // 4), ('zh', 'x'), 0, 0, t...  17.1 us
    pallas_call x2, Pallas kernels, project(): pl.pallas_call(project_kernel, out_shape=jax.ShapeDtypeStruct((16, 4, col...  15.8 us
    all_to_all x1, waiting for transfers between devices, body(): slabs = lax.all_to_all(value, SLABS, 0, 0, tiled=True)  14.4 us
    ppermute x1, waiting for transfers between devices, body(): back = lax.ppermute((away + got_away.astype(F32)).astype(BF16), 'zl', SWAP)  12.6 us
    all_to_all x1, starting transfers between devices, spread(): lax.all_to_all(both.reshape(16, 2, rows, cols // 4), ('zh', 'x'), 0, 0, t...  11.6 us
    all_to_all x1, starting transfers between devices, body(): resp = lax.all_to_all(resp, SEQ, 0, 0, tiled=True)  11.4 us
    unnamed x17, local copies, waits for them, and re-layouts  8.03 us
  transfers between devices with their start and end apart: 14, of which 11 were waited for; matrix products, arithmetic and copies ran while one was open for 9% of the time, Pallas kernels for 5%

commit v1 on v0

v1 whole, which is shorter than its diff:
```python
import math

import jax
import jax.numpy as jnp
import numpy as np
from jax import lax
from jax.experimental import pallas as pl
from jax.experimental.pallas import tpu as pltpu
from jax.sharding import Mesh
from jax.sharding import PartitionSpec as P

F32 = jnp.float32
BF16 = jnp.bfloat16
SEQ = ("y", "zh", "x")
SLABS = ("y", "zh")
SWAP = [(0, 1), (1, 0)]


def shift(count):
    return [(i, (i + count) % 4) for i in range(4)]


def tie(*arrays):
    return lax.optimization_barrier(arrays)


def in_hbm(arrays):
    return [pltpu.with_memory_space_constraint(a, pltpu.HBM) for a in arrays]


def turn_kernel(source, out):
    for part in range(4):
        block = source[:, part * 256 : (part + 1) * 256].astype(F32).T
        out[:, part] = block.astype(BF16).reshape(16, 16, block.shape[1])


def turn_filter(response):
    inside = pl.BlockSpec(memory_space=pltpu.VMEM)
    return pl.pallas_call(
        turn_kernel,
        out_shape=jax.ShapeDtypeStruct((16, 4, 16, response.shape[0]), BF16),
        in_specs=[inside],
        out_specs=inside,
    )(response)


def split_kernel(own_ref, first, second, *outs):
    rows = first.shape[0]
    for step, out in enumerate(outs):
        col = pl.multiple_of(lax.rem(own_ref[0] + step, 4) * 256, 128)
        out[:rows] = first[:, pl.ds(col, 256)]
        out[rows:] = second[:, pl.ds(col, 256)]


def split_columns(own, first, second):
    inside = pl.BlockSpec(memory_space=pltpu.VMEM)
    one = jax.ShapeDtypeStruct((2 * first.shape[0], 256), first.dtype)
    return pl.pallas_call(
        split_kernel,
        out_shape=(one,) * 4,
        in_specs=[pl.BlockSpec(memory_space=pltpu.SMEM), inside, inside],
        out_specs=(inside,) * 4,
    )(own.reshape(1), first, second)


def place_kernel(own_ref, *refs):
    sources, outs = refs[:4], refs[4:]
    rows = sources[0].shape[0] // len(outs)
    for step, source in enumerate(sources):
        row = pl.multiple_of(lax.rem(own_ref[0] + 4 - step, 4) * rows, 16)
        for at, out in enumerate(outs):
            out[pl.ds(row, rows)] = source[at * rows : (at + 1) * rows]


def place(own, pieces, count):
    inside = pl.BlockSpec(memory_space=pltpu.VMEM)
    rows, cols = pieces[0].shape
    one = jax.ShapeDtypeStruct((4 * rows // count, cols), pieces[0].dtype)
    return pl.pallas_call(
        place_kernel,
        out_shape=(one,) * count,
        in_specs=[pl.BlockSpec(memory_space=pltpu.SMEM)] + [inside] * 4,
        out_specs=(inside,) * count,
    )(own.reshape(1), *pieces)


def to_all(block, axis):
    return [lax.ppermute(block, axis, shift(step)) if step else block for step in range(4)]


def project_kernel(own_ref, act_ref, *refs):
    w_refs, (out, a_buf, w_buf, sems) = refs[:-4], refs[-4:]
    rows, block = a_buf.shape[1], w_buf.shape[0] // len(w_refs)
    copies = []
    for step, source in enumerate(w_refs):
        row = pl.multiple_of(lax.rem(own_ref[0] + 4 - step, 4) * block, 16)
        copies.append((source, w_buf.at[pl.ds(row, block)]))
    for part in range(4):
        copies.append((act_ref.at[pl.ds(part * rows, rows)], a_buf.at[part]))
    copies = [
        pltpu.make_async_copy(src, dst, sems.at[at]) for at, (src, dst) in enumerate(copies)
    ]
    for copy in copies:
        copy.start()
    for copy in copies[: len(w_refs)]:
        copy.wait()
    for part in range(4):
        copies[len(w_refs) + part].wait()
        prod = jnp.dot(a_buf[part], w_buf[...], preferred_element_type=F32)
        out[:, part] = prod.T.astype(BF16).reshape(16, 16, rows)


def project(own, act, weights):
    rows, depth = act.shape[0] // 4, act.shape[1]
    cols = weights[0].shape[1]
    count = len(weights) + 4
    return pl.pallas_call(
        project_kernel,
        out_shape=jax.ShapeDtypeStruct((16, 4, cols // 16, rows), BF16),
        in_specs=[pl.BlockSpec(memory_space=pltpu.SMEM)]
        + [pl.BlockSpec(memory_space=pltpu.HBM)] * (len(weights) + 1),
        out_specs=pl.BlockSpec(memory_space=pltpu.VMEM),
        scratch_shapes=[
            pltpu.VMEM((4, rows, depth), BF16),
            pltpu.VMEM((depth, cols), BF16),
            pltpu.SemaphoreType.DMA((count,)),
        ],
        compiler_params=pltpu.CompilerParams(vmem_limit_bytes=40 * 1024 * 1024),
    )(own.reshape(1), *in_hbm([act, *weights]))


def column_block(weight_ref, block, w_buf, sem):
    col = pl.multiple_of(block * w_buf.shape[1], 128)
    return pltpu.make_async_copy(weight_ref.at[:, pl.ds(col, w_buf.shape[1])], w_buf, sem)


def mix_kernel(at_ref, conv_ref, *refs):
    values, gates, refs = refs[:4], refs[4:8], refs[8:]
    skip_ref, weight_ref, home_ref, give_ref, w_buf, sem = refs
    own_x, own_c, own_z = at_ref[1], at_ref[2], at_ref[3]
    copy = column_block(weight_ref, 2 * (1 - own_z) + 1 - own_c, w_buf, sem)
    copy.start()
    rows = home_ref.shape[0]
    for step in range(4):
        src = lax.rem(own_x + 4 - step, 4)
        conv = conv_ref[:, src].astype(F32).reshape(256, rows)
        value = values[step][...].astype(F32).reshape(256, rows)
        gate = gates[step][...].astype(F32).reshape(256, rows)
        mixed = gate * (conv + skip_ref[src] * value)
        col = pl.multiple_of(src * 256, 128)
        home_ref[:, pl.ds(col, 256)] = mixed.T.astype(BF16)
    copy.wait()
    give_ref[...] = jnp.dot(home_ref[...], w_buf[...], preferred_element_type=F32).astype(BF16)


INSIDE = pl.BlockSpec(memory_space=pltpu.VMEM)
OUTSIDE = pl.BlockSpec(memory_space=pltpu.HBM)
SCALARS = pl.BlockSpec(memory_space=pltpu.SMEM)


def mix_and_give(at, conv, values, gates, skip, weight):
    rows = conv.shape[-1]
    one = jax.ShapeDtypeStruct((rows, 1024), BF16)
    return pl.pallas_call(
        mix_kernel,
        out_shape=(one, one),
        in_specs=[SCALARS] + [INSIDE] * 10 + [OUTSIDE],
        out_specs=(INSIDE, INSIDE),
        scratch_shapes=[pltpu.VMEM((1024, 1024), BF16), pltpu.SemaphoreType.DMA],
        compiler_params=pltpu.CompilerParams(vmem_limit_bytes=32 * 1024 * 1024),
    )(at, conv, *values, *gates, skip, *in_hbm([weight]))


def away_kernel(at_ref, home_ref, weight_ref, away_ref, w_buf, sem):
    copy = column_block(weight_ref, 2 * (1 - at_ref[3]) + at_ref[2], w_buf, sem)
    copy.start()
    copy.wait()
    away_ref[...] = jnp.dot(home_ref[...], w_buf[...], preferred_element_type=F32)


def away_part(at, home, weight):
    return pl.pallas_call(
        away_kernel,
        out_shape=jax.ShapeDtypeStruct((home.shape[0], 1024), F32),
        in_specs=[SCALARS, INSIDE, OUTSIDE],
        out_specs=INSIDE,
        scratch_shapes=[pltpu.VMEM((1024, 1024), BF16), pltpu.SemaphoreType.DMA],
        compiler_params=pltpu.CompilerParams(vmem_limit_bytes=24 * 1024 * 1024),
    )(at, home, *in_hbm([weight]))


def near_kernel(at_ref, home_ref, weight_ref, give_ref, mine_ref, w_buf, sems):
    own_z, own_c = at_ref[3], at_ref[2]
    copies = [
        column_block(weight_ref, 2 * own_z + core, w_buf.at[at], sems.at[at])
        for at, core in enumerate((1 - own_c, own_c))
    ]
    for copy in copies:
        copy.start()
    for at, out_ref in enumerate((give_ref, mine_ref)):
        copies[at].wait()
        out_ref[...] = jnp.dot(
            home_ref[...], w_buf[at], preferred_element_type=F32
        ).astype(out_ref.dtype)


def near_parts(at, home, weight):
    rows = home.shape[0]
    return pl.pallas_call(
        near_kernel,
        out_shape=(
            jax.ShapeDtypeStruct((rows, 1024), BF16),
            jax.ShapeDtypeStruct((rows, 1024), F32),
        ),
        in_specs=[SCALARS, INSIDE, OUTSIDE],
        out_specs=(INSIDE, INSIDE),
        scratch_shapes=[pltpu.VMEM((2, 1024, 1024), BF16), pltpu.SemaphoreType.DMA((2,))],
        compiler_params=pltpu.CompilerParams(vmem_limit_bytes=24 * 1024 * 1024),
    )(at, home, *in_hbm([weight]))


def inner_tables(count):
    idx = np.arange(count)
    angle = (idx[:, None] * idx[None, :] % count) * (2.0 * math.pi / count)
    cos, sin = np.cos(angle), np.sin(angle)
    ahead = np.block([[cos, -sin], [sin, cos]])
    back = np.block([[cos, sin], [-sin, cos]])
    return jnp.asarray(ahead, BF16), jnp.asarray(back, BF16)


def mm(left, right):
    return jnp.dot(left, right, preferred_element_type=F32)


def along_x(parts, own):
    pieces = []
    for step in range(4):
        piece = lax.dynamic_index_in_dim(parts, (own + step) % 4, 1, keepdims=False)
        pieces.append(lax.ppermute(piece, "x", shift(step)) if step else piece)
    return pieces


def body(sequence_in, value_proj, gate_proj, filter_response, skip_weight, output_proj):
    rows = sequence_in.shape[0]
    half = rows // 2
    my_y, my_x, my_zl, my_c = (lax.axis_index(a) for a in ("y", "x", "zl", "c"))
    at = jnp.stack([my_y, my_x, my_c, my_zl])

    act = lax.dynamic_slice(sequence_in, (my_c * half, 0), (half, sequence_in.shape[1]))
    act = lax.all_gather(act, ("x", "c"), axis=0, tiled=True)

    resp = turn_filter(filter_response.reshape(2 * rows, 1024)).reshape(64, 16, 2 * rows)

    wg = split_columns(my_x, value_proj, gate_proj)
    wg = [lax.ppermute(p, "x", shift(step)) if step else p for step, p in enumerate(wg)]
    resp, *wg = tie(resp, *wg)
    resp = lax.all_to_all(resp, SEQ, 0, 0, tiled=True)
    w_x, g_x = place(my_x, wg, 2)
    my_zh = lax.axis_index("zh")
    (w_y,) = place(my_zh, to_all(w_x, "zh"), 1)
    w_y, g_x = tie(w_y, g_x)
    w_all = to_all(w_y, "y")
    g_z = to_all(g_x, "zh")
    *w_all, g_z[1], g_z[2], g_z[3] = tie(*w_all, *g_z[1:])
    (g_y,) = place(my_zh, g_z, 1)
    g_all = lax.all_gather(g_y, "y", axis=0, tiled=True)
    value = project(my_y, act, w_all)
    value, resp = tie(value, resp)
    full = rows * 64

    slabs = lax.all_to_all(value, SLABS, 0, 0, tiled=True)
    values = along_x(value, my_x)
    slabs, g_all, *values = tie(slabs, g_all, *values)
    slabs = slabs.reshape(64, 16, rows)

    s_idx = lax.iota(jnp.int32, 64)
    k_idx = lax.iota(jnp.int32, 64)

    def slab_table(order):
        angle = (k_idx[:, None] * order[None, :] % 64).astype(F32) * (2.0 * math.pi / 64)
        return jnp.concatenate([jnp.cos(angle), -jnp.sin(angle)])

    first = slab_table(s_idx).astype(BF16)
    last = (slab_table(s_idx) / full).astype(BF16)
    r_idx = lax.iota(jnp.int32, rows)
    twist = (k_idx[:, None] * r_idx[None, :]).astype(F32) * (2.0 * math.pi / full)
    t_cos, t_sin = jnp.cos(twist)[:, None, :], jnp.sin(twist)[:, None, :]
    ahead, back = inner_tables(rows)

    sect = jnp.einsum("ks,scr->kcr", first, slabs, preferred_element_type=F32)
    re, im = sect[:64], sect[64:]
    turned = jnp.concatenate([re * t_cos + im * t_sin, im * t_cos - re * t_sin], axis=2)
    spec = mm(turned.astype(BF16), ahead)
    re, im = spec[..., :rows], spec[..., rows:]
    resp = resp.astype(F32)
    h_re, h_im = resp[..., :rows], resp[..., rows:]
    prod = jnp.concatenate([re * h_re - im * h_im, re * h_im + im * h_re], axis=2)
    inv = mm(prod.astype(BF16), back)
    re, im = inv[..., :rows], inv[..., rows:]
    reverted = jnp.concatenate([re * t_cos - im * t_sin, re * t_sin + im * t_cos], axis=0)
    conv = jnp.einsum("ks,kcr->scr", last, reverted.astype(BF16), preferred_element_type=F32)
    conv = lax.all_to_all(conv.astype(BF16), SEQ, 0, 0, tiled=True).reshape(16, 4, 16, rows)
    gate = project(my_y * 0, act, [g_all])
    gates = along_x(gate, my_x)

    home, give = mix_and_give(
        at, conv, values, gates, skip_weight.reshape(4, 256, 1), output_proj
    )
    got = lax.ppermute(give, "c", SWAP)
    away = away_part(at, home, output_proj)
    away = (away + got.astype(F32)).astype(BF16)
    back = lax.ppermute(away, "zl", SWAP)
    home, away = tie(home, away)
    give, mine = near_parts(at, home, output_proj)
    mine = mine + lax.ppermute(give, "c", SWAP).astype(F32)
    return (mine + back.astype(F32)).astype(BF16)


def solution(mesh):
    fine = Mesh(mesh.devices.reshape(4, 4, 4, 2, 2), ("y", "zh", "x", "zl", "c"))
    tp = ("zl", "c")
    placed = (
        P(SEQ, None),
        P(SEQ, tp),
        P(SEQ, tp),
        P(None, None, SEQ, tp),
        P(tp),
        P(tp, None),
    )
    return jax.shard_map(
        body, mesh=fine, in_specs=placed, out_specs=P(SEQ, tp), check_vma=False
    )
```

time: 213 us -> 200 us (0.939)
  waiting for transfers between devices: 95.4 us -> 61.6 us
  starting transfers between devices: 45.8 us -> 67.2 us
  Pallas kernels: 24 us -> 35.8 us
  local copies, waits for them, and re-layouts: 19.4 us -> 11.5 us
  other arithmetic: 9.14 us -> 5.85 us
    ppermute x7 -> x20, starting transfers between devices: 9.48 us -> 37.7 us  [the longest x9 20.2 us: to_all(): lax.ppermute(block, axis, shift(step))]
    all_to_all x2 -> x1, waiting for transfers between devices: 20.3 us -> 0.01 us  [body(): lax.all_to_all(conv.astype(BF16), SEQ, 0, 0, tiled=True)]
    all_to_all x1, waiting for transfers between devices: 0.01 us -> 16.2 us  [body(): resp = lax.all_to_all(resp, SEQ, 0, 0, tiled=True)]
    all_to_all x1, waiting for transfers between devices: 14.4 us -> 2.19 us  [body(): slabs = lax.all_to_all(value, SLABS, 0, 0, tiled=True)]
    pallas_call x2 -> x8, Pallas kernels: 8.21 us -> 20.1 us  [the longest x3 5.56 us: place(): pl.pallas_call(place_kernel, out_shape=(one,) * count, in_specs=[pl.Block...]
    ppermute x7 -> x20, waiting for transfers between devices: 54.1 us -> 43.2 us  [the longest x9 26.2 us: to_all(): lax.ppermute(block, axis, shift(step))]
    all_to_all x2 -> x1, starting transfers between devices: 16.6 us -> 8.59 us  [body(): lax.all_to_all(conv.astype(BF16), SEQ, 0, 0, tiled=True)]
    all_gather x1, waiting for transfers between devices: 6.62 us -> 0.01 us  [body(): g_all = lax.all_gather(g_y, 'y', axis=0, tiled=True)]
  transfers between devices with their start and end apart: 14 -> 26, of which waited for: 11 -> 14; matrix products, arithmetic and copies ran while one was open for 9% -> 3% of each run, Pallas kernels for 5% -> 16%
where the time goes in v1:
time: 200 us; the launch traced here: 199 us
  starting transfers between devices  67.2 us (34%)
  waiting for transfers between devices  61.6 us (31%)
  Pallas kernels  35.8 us (18%)
  between operations  13.7 us (7%)
  local copies, waits for them, and re-layouts  11.5 us (6%)
  other arithmetic  5.85 us (3%)
  matrix products  3.51 us (2%)
    ppermute x9, waiting for transfers between devices, to_all(): lax.ppermute(block, axis, shift(step))  26.2 us
    ppermute x9, starting transfers between devices, to_all(): lax.ppermute(block, axis, shift(step))  20.2 us
    all_to_all x1, waiting for transfers between devices, body(): resp = lax.all_to_all(resp, SEQ, 0, 0, tiled=True)  16.2 us
    pallas_call x2, Pallas kernels, project(): pl.pallas_call(project_kernel, out_shape=jax.ShapeDtypeStruct((16, 4, col...  15.8 us
    all_to_all x1, starting transfers between devices, body(): resp = lax.all_to_all(resp, SEQ, 0, 0, tiled=True)  8.94 us
    ppermute x6, waiting for transfers between devices, along_x(): pieces.append(lax.ppermute(piece, 'x', shift(step)) if step else piece)  8.65 us
    all_to_all x1, starting transfers between devices, body(): lax.all_to_all(conv.astype(BF16), SEQ, 0, 0, tiled=True)  8.59 us
    ppermute x1, waiting for transfers between devices, body(): back = lax.ppermute(away, 'zl', SWAP)  8.32 us
  transfers between devices with their start and end apart: 26, of which 14 were waited for; matrix products, arithmetic and copies ran while one was open for 3% of the time, Pallas kernels for 16%

profile of v1, /device:TPU:1, one launch (start us, length us, event | category | flops | bytes accessed | tf_op | source)
XLA Modules:
  0.0 199.3 jit_solution(14614858927324017348)
XLA Ops:
  6.5 1.6 copy-done
  8.1 1.1 constant_dynamic-slice_fusion
  9.3 1.7 shard_map.83
  11.0 2.0 %collective-permute-start = (bf16[128,256]{1,0:T(8,128)(2,1)}, bf16[128,256]{1,0:T(8,128)(2,1)S(1)}, u32[]{:S(2)}, u32[]{:S(2)}) collective-permute-start(bf16[128,256]{1,0:T(8,128)(2,1)} %get-tuple-element.39), channel_id=1, source_target_pairs={{0,4},{4,8},{8,12},{12,0},{1,5},{5,9},{9,13},{13,1},{2,6},{6,10},{... | collective-permute-start | bytes 196616 | tf_op jit(solution)/shard_map/ppermute | solution.py:255
  13.0 2.5 %collective-permute-start.1 = (bf16[128,256]{1,0:T(8,128)(2,1)}, bf16[128,256]{1,0:T(8,128)(2,1)S(1)}, u32[]{:S(2)}, u32[]{:S(2)}) collective-permute-start(bf16[128,256]{1,0:T(8,128)(2,1)} %get-tuple-element.40), channel_id=1, source_target_pairs={{0,8},{4,12},{8,0},{12,4},{1,9},{5,13},{9,1},{13,5},{2,10},{6,14},... | collective-permute-start | bytes 196616 | tf_op jit(solution)/shard_map/ppermute | solution.py:255
  15.5 1.2 collective-permute-start.2
  16.6 2.6 %shard_map.82 = bf16[16,4,16,512]{3,2,1,0:T(8,128)(2,1)} custom-call(bf16[512,1024]{1,0:T(8,128)(2,1)} %bitcast.37), custom_call_target="tpu_custom_call" | custom-call | tf_op jit(solution)/shard_map/pallas_call | solution.py:39
  19.3 0.6 copy-done.15
  19.9 1.7 shard_map.84
  21.6 6.1 %collective-permute-start.5 = (bf16[256,256]{1,0:T(8,128)(2,1)}, bf16[256,256]{1,0:T(8,128)(2,1)S(1)}, u32[]{:S(2)}, u32[]{:S(2)}) collective-permute-start(bf16[256,256]{1,0:T(8,128)(2,1)} %get-tuple-element.46.refs_0_), channel_id=1, source_target_pairs={{0,48},{16,0},{32,16},{48,32},{1,49},{17,1},{33,17},{49,33},{2,50}... | collective-permute-start | bytes 393224 | tf_op jit(solution)/shard_map/ppermute | solution.py:88
  27.6 0.9 collective-permute-start.4
  28.5 2.4 %collective-permute-start.3 = (bf16[256,256]{1,0:T(8,128)(2,1)}, bf16[256,256]{1,0:T(8,128)(2,1)S(1)}, u32[]{:S(2)}, u32[]{:S(2)}) collective-permute-start(bf16[256,256]{1,0:T(8,128)(2,1)} %get-tuple-element.46.refs_0_), channel_id=1, source_target_pairs={{0,16},{16,32},{32,48},{48,0},{1,17},{17,33},{33,49},{49,1},{2,18}... | collective-permute-start | bytes 393224 | tf_op jit(solution)/shard_map/ppermute | solution.py:88
  30.9 7.1 %collective-permute-done.5.refs_3_ = bf16[256,256]{1,0:T(8,128)(2,1)S(1)} collective-permute-done((bf16[256,256]{1,0:T(8,128)(2,1)}, bf16[256,256]{1,0:T(8,128)(2,1)S(1)}, u32[]{:S(2)}, u32[]{:S(2)}) %collective-permute-start.5) | collective-permute-done | bytes 131104 | tf_op jit(solution)/shard_map/ppermute | solution.py:88
  38.0 0.5 collective-permute-done.3.refs_1_
  38.7 0.4 copy-done.14
  39.1 1.9 shard_map.85.refs_0_
  41.1 2.7 %collective-permute-start.8 = (bf16[1024,256]{1,0:T(8,128)(2,1)}, bf16[1024,256]{1,0:T(8,128)(2,1)}, u32[]{:S(2)}, u32[]{:S(2)}) collective-permute-start(bf16[1024,256]{1,0:T(8,128)(2,1)} %shard_map.85.refs_0_), channel_id=1, source_target_pairs={{0,192},{64,0},{128,64},{192,128},{1,193},{65,1},{129,65},{193,129... | collective-permute-start | bytes 1572872 | tf_op jit(solution)/shard_map/ppermute | solution.py:88
  44.1 0.7 collective-permute-start.6
  44.8 4.3 %collective-permute-start.11 = (bf16[256,256]{1,0:T(8,128)(2,1)}, bf16[256,256]{1,0:T(8,128)(2,1)S(1)}, u32[]{:S(2)}, u32[]{:S(2)}) collective-permute-start(bf16[256,256]{1,0:T(8,128)(2,1)} %get-tuple-element.49.refs_0_), channel_id=1, source_target_pairs={{0,48},{16,0},{32,16},{48,32},{1,49},{17,1},{33,17},{49,33},{2,50}... | collective-permute-start | bytes 393224 | tf_op jit(solution)/shard_map/ppermute | solution.py:88
  49.1 1.0 collective-permute-start.10
  50.1 1.3 collective-permute-done.11.refs_3_
  51.4 1.9 collective-permute-start.9
  53.3 5.1 %collective-permute-done.10.refs_2_ = bf16[256,256]{1,0:T(8,128)(2,1)S(1)} collective-permute-done((bf16[256,256]{1,0:T(8,128)(2,1)}, bf16[256,256]{1,0:T(8,128)(2,1)S(1)}, u32[]{:S(2)}, u32[]{:S(2)}) %collective-permute-start.10) | collective-permute-done | bytes 131104 | tf_op jit(solution)/shard_map/ppermute | solution.py:88
  58.4 4.1 %collective-permute-done.9.refs_1_ = bf16[256,256]{1,0:T(8,128)(2,1)S(1)} collective-permute-done((bf16[256,256]{1,0:T(8,128)(2,1)}, bf16[256,256]{1,0:T(8,128)(2,1)S(1)}, u32[]{:S(2)}, u32[]{:S(2)}) %collective-permute-start.9) | collective-permute-done | bytes 131104 | tf_op jit(solution)/shard_map/ppermute | solution.py:88
  62.5 8.2 %collective-permute-done.6.refs_1_ = bf16[1024,256]{1,0:T(8,128)(2,1)} collective-permute-done((bf16[1024,256]{1,0:T(8,128)(2,1)}, bf16[1024,256]{1,0:T(8,128)(2,1)}, u32[]{:S(2)}, u32[]{:S(2)}) %collective-permute-start.6) | collective-permute-done | bytes 524320 | tf_op jit(solution)/shard_map/ppermute | solution.py:88
  70.7 2.0 shard_map.87
  72.7 8.9 %all-to-all-start = ((bf16[64,16,512]{2,1,0:T(8,128)(2,1)}), bf16[64,16,512]{2,1,0:T(8,128)(2,1)S(1)}, u32[]{:S(2)}, u32[]{:S(2)}) async-start(bf16[64,16,512]{2,1,0:T(8,128)(2,1)} %bitcast.36), calls=%async_computation | async-start | bytes 2097152 | tf_op jit(solution)/shard_map/all_to_all | solution.py:257
  81.7 8.3 %shard_map.86 = bf16[16,4,16,256]{3,2,1,0:T(8,128)(2,1)} custom-call(s32[1]{0:T(128)} %bitcast.own_ref, bf16[1024,4096]{1,0:T(8,128)(2,1)} %all-gather.3.cloned.1.call-done.act_ref, bf16[1024,256]{1,0:T(8,128)(2,1)} %shard_map.85.refs_0_, bf16[1024,256]{1,0:T(8,128)(2,1)} %collective-permute-done.6.refs_1_, ...), custom_call_target="tpu_custom_call" | custom-call | tf_op jit(solution)/shard_map/pallas_call | solution.py:117
  90.0 16.2 %all-to-all-done = bf16[64,16,512]{2,1,0:T(8,128)(2,1)S(1)} async-done(((bf16[64,16,512]{2,1,0:T(8,128)(2,1)}), bf16[64,16,512]{2,1,0:T(8,128)(2,1)S(1)}, u32[]{:S(2)}, u32[]{:S(2)}) %all-to-all-start) | async-done | bytes 1048608 | tf_op jit(solution)/shard_map/all_to_all | solution.py:257
  106.2 4.2 %all-to-all-start.1 = ((bf16[16,4,16,256]{3,2,1,0:T(8,128)(2,1)}), bf16[16,4,16,256]{3,2,1,0:T(8,128)(2,1)}, u32[]{:S(2)}, u32[]{:S(2)}) async-start(bf16[16,4,16,256]{3,2,1,0:T(8,128)(2,1)} %shard_map.86), calls=%async_computation.1 | async-start | bytes 1048576 | tf_op jit(solution)/shard_map/all_to_all | solution.py:271
  110.5 1.2 dynamic-slice_bitcast_fusion.4
  111.6 2.0 collective-permute-start.14
  113.6 0.9 collective-permute-start.13
  114.5 0.8 collective-permute-start.12
  115.7 2.9 %convert_element_type.64 = f32[64,16,512]{2,1,0:T(8,128)} convert(bf16[64,16,512]{2,1,0:T(8,128)(2,1)} %copy-done.6) | non-fusion elementwise | flops 524288 | bytes 3145728 | tf_op jit(solution)/shard_map/convert_element_type | solution.py:295
  119.0 1.7 collective-permute-done.12.refs_1_
  120.7 2.2 %all-to-all-done.1 = bf16[16,4,16,256]{3,2,1,0:T(8,128)(2,1)} async-done(((bf16[16,4,16,256]{3,2,1,0:T(8,128)(2,1)}), bf16[16,4,16,256]{3,2,1,0:T(8,128)(2,1)}, u32[]{:S(2)}, u32[]{:S(2)}) %all-to-all-start.1) | async-done | bytes 524320 | tf_op jit(solution)/shard_map/all_to_all | solution.py:271
  122.9 1.6 fusion.7
  125.0 0.6 copy-done.8
  125.5 0.8 fusion.5
  126.3 0.8 copy-done.5
  127.1 0.4 subtract_convert_fusion.1
  127.7 0.9 copy-done.7
  128.6 0.8 fusion.3
  130.1 1.1 copy.24
  131.1 8.6 %all-to-all-start.2 = ((bf16[64,16,256]{2,1,0:T(8,128)(2,1)}), bf16[64,16,256]{2,1,0:T(8,128)(2,1)S(1)}, u32[]{:S(2)}, u32[]{:S(2)}) async-start(bf16[64,16,256]{2,1,0:T(8,128)(2,1)} %copy.24), calls=%async_computation.2 | async-start | bytes 1048576 | tf_op jit(solution)/shard_map/all_to_all | solution.py:302
  139.7 7.5 %shard_map.88 = bf16[16,4,16,256]{3,2,1,0:T(8,128)(2,1)S(1)} custom-call(s32[1]{0:T(128)} %constant.109.clone.1.own_ref, bf16[1024,4096]{1,0:T(8,128)(2,1)} %all-gather.3.cloned.1.call-done.act_ref, bf16[4096,256]{1,0:T(8,128)(2,1)} %all-gather.5.cloned.1.call-done.refs_0_), custom_call_target="tpu_custom_call" | custom-call | tf_op jit(solution)/shard_map/pallas_call | solution.py:117
  147.2 0.8 dynamic-slice_bitcast_fusion
  148.0 2.0 %collective-permute-start.17 = (bf16[16,16,256]{2,1,0:T(8,128)(2,1)}, bf16[16,16,256]{2,1,0:T(8,128)(2,1)}, u32[]{:S(2)}, u32[]{:S(2)}) collective-permute-start(bf16[16,16,256]{2,1,0:T(8,128)(2,1)} %get-tuple-element.77), channel_id=1, source_target_pairs={{0,12},{4,0},{8,4},{12,8},{1,13},{5,1},{9,5},{13,9},{2,14},{6,2},{... | collective-permute-start | bytes 393224 | tf_op jit(solution)/shard_map/ppermute | solution.py:239
  150.0 0.6 collective-permute-start.16
  150.6 0.6 collective-permute-start.15
  151.6 3.3 %collective-permute-done.17.refs_7_ = bf16[16,16,256]{2,1,0:T(8,128)(2,1)} collective-permute-done((bf16[16,16,256]{2,1,0:T(8,128)(2,1)}, bf16[16,16,256]{2,1,0:T(8,128)(2,1)}, u32[]{:S(2)}, u32[]{:S(2)}) %collective-permute-start.17) | collective-permute-done | bytes 131104 | tf_op jit(solution)/shard_map/ppermute | solution.py:239
  154.9 1.7 collective-permute-done.16.refs_6_
  156.6 1.6 collective-permute-done.15.refs_5_
  158.2 0.9 copy-done.2
  159.1 0.9 copy-done.4
  160.0 3.8 %shard_map.89 = (bf16[256,1024]{1,0:T(8,128)(2,1)S(1)}, bf16[256,1024]{1,0:T(8,128)(2,1)S(1)}) custom-call(s32[4]{0:T(128)S(1)} %pad_add_fusion.at_ref, bf16[16,4,16,256]{3,2,1,0:T(8,128)(2,1)S(1)} %bitcast.35, bf16[16,16,256]{2,1,0:T(8,128)(2,1)S(1)} %get-tuple-element.61.refs_0_, bf16[16,16,256]{2,1,0:T(8,128)(2,1)S(1)} %copy-done.4, ...), custom_call_target="tpu_custom_call" | custom-call | tf_op jit(solution)/shard_map/pallas_call | solution.py:164
  163.8 7.7 %collective-permute-start.18 = (bf16[256,1024]{1,0:T(8,128)(2,1)S(1)}, bf16[256,1024]{1,0:T(8,128)(2,1)S(1)}, u32[]{:S(2)}, u32[]{:S(2)}) collective-permute-start(bf16[256,1024]{1,0:T(8,128)(2,1)S(1)} %get-tuple-element.67), channel_id=1, source_target_pairs={{0,1},{1,0},{2,3},{3,2},{4,5},{5,4},{6,7},{7,6},{8,9},{9,8},{10,11... | collective-permute-start | bytes 1572872 | tf_op jit(solution)/shard_map/ppermute | solution.py:309
  171.4 2.9 %shard_map.90 = f32[256,1024]{1,0:T(8,128)S(1)} custom-call(s32[4]{0:T(128)S(1)} %pad_add_fusion.at_ref, bf16[256,1024]{1,0:T(8,128)(2,1)S(1)} %get-tuple-element.68.home_ref, bf16[1024,4096]{1,0:T(8,128)(2,1)} %weight_ref.3), custom_call_target="tpu_custom_call" | custom-call | tf_op jit(solution)/shard_map/pallas_call | solution.py:182
  174.5 4.6 %collective-permute-start.20 = (bf16[256,1024]{1,0:T(8,128)(2,1)S(1)}, bf16[256,1024]{1,0:T(8,128)(2,1)S(1)}, u32[]{:S(2)}, u32[]{:S(2)}) collective-permute-start(bf16[256,1024]{1,0:T(8,128)(2,1)S(1)} %add_convert_fusion.1), channel_id=1, source_target_pairs={{0,2},{2,0},{1,3},{3,1},{4,6},{6,4},{5,7},{7,5},{8,10},{10,8},{9,1... | collective-permute-start | bytes 1572872 | tf_op jit(solution)/shard_map/ppermute | solution.py:312
  179.1 3.6 %shard_map.91 = (bf16[256,1024]{1,0:T(8,128)(2,1)S(1)}, f32[256,1024]{1,0:T(8,128)S(1)}) custom-call(s32[4]{0:T(128)S(1)} %pad_add_fusion.at_ref, bf16[256,1024]{1,0:T(8,128)(2,1)S(1)} %get-tuple-element.68.home_ref, bf16[1024,4096]{1,0:T(8,128)(2,1)} %weight_ref.3), custom_call_target="tpu_custom_call" | custom-call | tf_op jit(solution)/shard_map/pallas_call | solution.py:209
  182.7 0.4 collective-permute-start.19
  183.1 8.3 %collective-permute-done.20 = bf16[256,1024]{1,0:T(8,128)(2,1)S(1)} collective-permute-done((bf16[256,1024]{1,0:T(8,128)(2,1)S(1)}, bf16[256,1024]{1,0:T(8,128)(2,1)S(1)}, u32[]{:S(2)}, u32[]{:S(2)}) %collective-permute-start.20) | collective-permute-done | bytes 524320 | tf_op jit(solution)/shard_map/ppermute | solution.py:312
  191.4 1.0 add_convert_fusion
  (58 shorter events, 3.3 us)
Async XLA Ops:
  6.5 1.6 copy-start
  6.5 75.1 %all-gather.3.cloned.1.call-start = ((), (), s32[]{:S(2)}) async-start(), calls=%async_computation.3 | async-start | bytes 9437184 | tf_op jit(solution)/shard_map/all_gather | solution.py:250
  9.2 109.4 %all-gather.5.cloned.1.call-start = ((), (), s32[]{:S(2)}) async-start(), calls=%async_computation.4 | async-start | bytes 2621440 | tf_op jit(solution)/shard_map/all_gather | solution.py:266
  11.0 8.3 %collective-permute-start = (bf16[128,256]{1,0:T(8,128)(2,1)}, bf16[128,256]{1,0:T(8,128)(2,1)S(1)}, u32[]{:S(2)}, u32[]{:S(2)}) collective-permute-start(bf16[128,256]{1,0:T(8,128)(2,1)} %get-tuple-element.39), channel_id=1, source_target_pairs={{0,4},{4,8},{8,12},{12,0},{1,5},{5,9},{9,13},{13,1},{2,6},{6,10},{... | collective-permute-start | bytes 196616 | tf_op jit(solution)/shard_map/ppermute | solution.py:255
  13.0 6.2 %collective-permute-start.1 = (bf16[128,256]{1,0:T(8,128)(2,1)}, bf16[128,256]{1,0:T(8,128)(2,1)S(1)}, u32[]{:S(2)}, u32[]{:S(2)}) collective-permute-start(bf16[128,256]{1,0:T(8,128)(2,1)} %get-tuple-element.40), channel_id=1, source_target_pairs={{0,8},{4,12},{8,0},{12,4},{1,9},{5,13},{9,1},{13,5},{2,10},{6,14},... | collective-permute-start | bytes 196616 | tf_op jit(solution)/shard_map/ppermute | solution.py:255
  15.5 3.8 %collective-permute-start.2 = (bf16[128,256]{1,0:T(8,128)(2,1)}, bf16[128,256]{1,0:T(8,128)(2,1)S(1)}, u32[]{:S(2)}, u32[]{:S(2)}) collective-permute-start(bf16[128,256]{1,0:T(8,128)(2,1)} %get-tuple-element.41), channel_id=1, source_target_pairs={{0,12},{4,0},{8,4},{12,8},{1,13},{5,1},{9,5},{13,9},{2,14},{6,2},{... | collective-permute-start | bytes 196616 | tf_op jit(solution)/shard_map/ppermute | solution.py:255
  19.2 0.6 copy-start.15
  19.2 0.6 copy-start.16
  19.3 0.7 copy-start.17
  21.6 16.4 %collective-permute-start.5 = (bf16[256,256]{1,0:T(8,128)(2,1)}, bf16[256,256]{1,0:T(8,128)(2,1)S(1)}, u32[]{:S(2)}, u32[]{:S(2)}) collective-permute-start(bf16[256,256]{1,0:T(8,128)(2,1)} %get-tuple-element.46.refs_0_), channel_id=1, source_target_pairs={{0,48},{16,0},{32,16},{48,32},{1,49},{17,1},{33,17},{49,33},{2,50}... | collective-permute-start | bytes 393224 | tf_op jit(solution)/shard_map/ppermute | solution.py:88
  27.6 10.4 %collective-permute-start.4 = (bf16[256,256]{1,0:T(8,128)(2,1)}, bf16[256,256]{1,0:T(8,128)(2,1)S(1)}, u32[]{:S(2)}, u32[]{:S(2)}) collective-permute-start(bf16[256,256]{1,0:T(8,128)(2,1)} %get-tuple-element.46.refs_0_), channel_id=1, source_target_pairs={{0,32},{16,48},{32,0},{48,16},{1,33},{17,49},{33,1},{49,17},{2,34}... | collective-permute-start | bytes 393224 | tf_op jit(solution)/shard_map/ppermute | solution.py:88
  28.5 10.0 %collective-permute-start.3 = (bf16[256,256]{1,0:T(8,128)(2,1)}, bf16[256,256]{1,0:T(8,128)(2,1)S(1)}, u32[]{:S(2)}, u32[]{:S(2)}) collective-permute-start(bf16[256,256]{1,0:T(8,128)(2,1)} %get-tuple-element.46.refs_0_), channel_id=1, source_target_pairs={{0,16},{16,32},{32,48},{48,0},{1,17},{17,33},{33,49},{49,1},{2,18}... | collective-permute-start | bytes 393224 | tf_op jit(solution)/shard_map/ppermute | solution.py:88
  38.0 0.7 copy-start.11
  38.0 0.7 copy-start.12
  38.5 0.6 copy-start.14
  41.1 21.4 %collective-permute-start.8 = (bf16[1024,256]{1,0:T(8,128)(2,1)}, bf16[1024,256]{1,0:T(8,128)(2,1)}, u32[]{:S(2)}, u32[]{:S(2)}) collective-permute-start(bf16[1024,256]{1,0:T(8,128)(2,1)} %shard_map.85.refs_0_), channel_id=1, source_target_pairs={{0,192},{64,0},{128,64},{192,128},{1,193},{65,1},{129,65},{193,129... | collective-permute-start | bytes 1572872 | tf_op jit(solution)/shard_map/ppermute | solution.py:88
  43.8 18.7 %collective-permute-start.7 = (bf16[1024,256]{1,0:T(8,128)(2,1)}, bf16[1024,256]{1,0:T(8,128)(2,1)}, u32[]{:S(2)}, u32[]{:S(2)}) collective-permute-start(bf16[1024,256]{1,0:T(8,128)(2,1)} %shard_map.85.refs_0_), channel_id=1, source_target_pairs={{0,128},{64,192},{128,0},{192,64},{1,129},{65,193},{129,1},{193,65... | collective-permute-start | bytes 1572872 | tf_op jit(solution)/shard_map/ppermute | solution.py:88
  44.1 26.6 %collective-permute-start.6 = (bf16[1024,256]{1,0:T(8,128)(2,1)}, bf16[1024,256]{1,0:T(8,128)(2,1)}, u32[]{:S(2)}, u32[]{:S(2)}) collective-permute-start(bf16[1024,256]{1,0:T(8,128)(2,1)} %shard_map.85.refs_0_), channel_id=1, source_target_pairs={{0,64},{64,128},{128,192},{192,0},{1,65},{65,129},{129,193},{193,1... | collective-permute-start | bytes 1572872 | tf_op jit(solution)/shard_map/ppermute | solution.py:88
  44.8 6.5 %collective-permute-start.11 = (bf16[256,256]{1,0:T(8,128)(2,1)}, bf16[256,256]{1,0:T(8,128)(2,1)S(1)}, u32[]{:S(2)}, u32[]{:S(2)}) collective-permute-start(bf16[256,256]{1,0:T(8,128)(2,1)} %get-tuple-element.49.refs_0_), channel_id=1, source_target_pairs={{0,48},{16,0},{32,16},{48,32},{1,49},{17,1},{33,17},{49,33},{2,50}... | collective-permute-start | bytes 393224 | tf_op jit(solution)/shard_map/ppermute | solution.py:88
  49.1 9.3 %collective-permute-start.10 = (bf16[256,256]{1,0:T(8,128)(2,1)}, bf16[256,256]{1,0:T(8,128)(2,1)S(1)}, u32[]{:S(2)}, u32[]{:S(2)}) collective-permute-start(bf16[256,256]{1,0:T(8,128)(2,1)} %get-tuple-element.49.refs_0_), channel_id=1, source_target_pairs={{0,32},{16,48},{32,0},{48,16},{1,33},{17,49},{33,1},{49,17},{2,34}... | collective-permute-start | bytes 393224 | tf_op jit(solution)/shard_map/ppermute | solution.py:88
  51.4 19.3 %copy-start.9 = (bf16[256,256]{1,0:T(8,128)(2,1)}, bf16[256,256]{1,0:T(8,128)(2,1)S(1)}, u32[]{:S(2)}) copy-start(bf16[256,256]{1,0:T(8,128)(2,1)S(1)} %collective-permute-done.11.refs_3_) | copy-start | bytes 393220
  51.4 11.1 %collective-permute-start.9 = (bf16[256,256]{1,0:T(8,128)(2,1)}, bf16[256,256]{1,0:T(8,128)(2,1)S(1)}, u32[]{:S(2)}, u32[]{:S(2)}) collective-permute-start(bf16[256,256]{1,0:T(8,128)(2,1)} %get-tuple-element.49.refs_0_), channel_id=1, source_target_pairs={{0,16},{16,32},{32,48},{48,0},{1,17},{17,33},{33,49},{49,1},{2,18}... | collective-permute-start | bytes 393224 | tf_op jit(solution)/shard_map/ppermute | solution.py:88
  58.4 12.3 %copy-start.10 = (bf16[256,256]{1,0:T(8,128)(2,1)}, bf16[256,256]{1,0:T(8,128)(2,1)S(1)}, u32[]{:S(2)}) copy-start(bf16[256,256]{1,0:T(8,128)(2,1)S(1)} %collective-permute-done.10.refs_2_) | copy-start | bytes 393220
  62.5 8.2 %copy-start.13 = (bf16[256,256]{1,0:T(8,128)(2,1)}, bf16[256,256]{1,0:T(8,128)(2,1)S(1)}, u32[]{:S(2)}) copy-start(bf16[256,256]{1,0:T(8,128)(2,1)S(1)} %collective-permute-done.9.refs_1_) | copy-start | bytes 393220
  72.7 33.5 %all-to-all-start = ((bf16[64,16,512]{2,1,0:T(8,128)(2,1)}), bf16[64,16,512]{2,1,0:T(8,128)(2,1)S(1)}, u32[]{:S(2)}, u32[]{:S(2)}) async-start(bf16[64,16,512]{2,1,0:T(8,128)(2,1)} %bitcast.36), calls=%async_computation | async-start | bytes 2097152 | tf_op jit(solution)/shard_map/all_to_all | solution.py:257
  106.1 4.3 %copy-start.6 = (bf16[64,16,512]{2,1,0:T(8,128)(2,1)}, bf16[64,16,512]{2,1,0:T(8,128)(2,1)S(1)}, u32[]{:S(2)}) copy-start(bf16[64,16,512]{2,1,0:T(8,128)(2,1)S(1)} %all-to-all-done) | copy-start | bytes 3145732
  106.2 16.8 %all-to-all-start.1 = ((bf16[16,4,16,256]{3,2,1,0:T(8,128)(2,1)}), bf16[16,4,16,256]{3,2,1,0:T(8,128)(2,1)}, u32[]{:S(2)}, u32[]{:S(2)}) async-start(bf16[16,4,16,256]{3,2,1,0:T(8,128)(2,1)} %shard_map.86), calls=%async_computation.1 | async-start | bytes 1048576 | tf_op jit(solution)/shard_map/all_to_all | solution.py:271
  111.6 7.0 %collective-permute-start.14 = (bf16[16,16,256]{2,1,0:T(8,128)(2,1)S(1)}, bf16[16,16,256]{2,1,0:T(8,128)(2,1)S(1)}, u32[]{:S(2)}, u32[]{:S(2)}) collective-permute-start(bf16[16,16,256]{2,1,0:T(8,128)(2,1)S(1)} %get-tuple-element.81), channel_id=1, source_target_pairs={{0,12},{4,0},{8,4},{12,8},{1,13},{5,1},{9,5},{13,9},{2,14},{6,2},{... | collective-permute-start | bytes 393224 | tf_op jit(solution)/shard_map/ppermute | solution.py:239
  113.6 5.4 %collective-permute-start.13 = (bf16[16,16,256]{2,1,0:T(8,128)(2,1)S(1)}, bf16[16,16,256]{2,1,0:T(8,128)(2,1)S(1)}, u32[]{:S(2)}, u32[]{:S(2)}) collective-permute-start(bf16[16,16,256]{2,1,0:T(8,128)(2,1)S(1)} %get-tuple-element.82), channel_id=1, source_target_pairs={{0,8},{4,12},{8,0},{12,4},{1,9},{5,13},{9,1},{13,5},{2,10},{6,14},... | collective-permute-start | bytes 393224 | tf_op jit(solution)/shard_map/ppermute | solution.py:239
  114.5 6.2 %collective-permute-start.12 = (bf16[16,16,256]{2,1,0:T(8,128)(2,1)S(1)}, bf16[16,16,256]{2,1,0:T(8,128)(2,1)S(1)}, u32[]{:S(2)}, u32[]{:S(2)}) collective-permute-start(bf16[16,16,256]{2,1,0:T(8,128)(2,1)S(1)} %get-tuple-element.83), channel_id=1, source_target_pairs={{0,4},{4,8},{8,12},{12,0},{1,5},{5,9},{9,13},{13,1},{2,6},{6,10},{... | collective-permute-start | bytes 393224 | tf_op jit(solution)/shard_map/ppermute | solution.py:239
  119.0 5.8 %copy-start.1 = (bf16[16,16,256]{2,1,0:T(8,128)(2,1)}, bf16[16,16,256]{2,1,0:T(8,128)(2,1)S(1)}, u32[]{:S(2)}) copy-start(bf16[16,16,256]{2,1,0:T(8,128)(2,1)S(1)} %collective-permute-done.13.refs_2_) | copy-start | bytes 393220
  120.7 4.1 %copy-start.3 = (bf16[16,16,256]{2,1,0:T(8,128)(2,1)}, bf16[16,16,256]{2,1,0:T(8,128)(2,1)S(1)}, u32[]{:S(2)}) copy-start(bf16[16,16,256]{2,1,0:T(8,128)(2,1)S(1)} %collective-permute-done.12.refs_1_) | copy-start | bytes 393220
  124.5 1.0 copy-start.8
  125.5 1.6 copy-start.5
  127.5 1.0 copy-start.7
  131.1 27.1 %all-to-all-start.2 = ((bf16[64,16,256]{2,1,0:T(8,128)(2,1)}), bf16[64,16,256]{2,1,0:T(8,128)(2,1)S(1)}, u32[]{:S(2)}, u32[]{:S(2)}) async-start(bf16[64,16,256]{2,1,0:T(8,128)(2,1)} %copy.24), calls=%async_computation.2 | async-start | bytes 1048576 | tf_op jit(solution)/shard_map/all_to_all | solution.py:302
  139.7 11.4 %copy-start.18 = (f32[1024]{0:T(1024)S(1)}, f32[1024]{0:T(1024)}, u32[]{:S(2)}) copy-start(f32[1024]{0:T(1024)} %param.12) | copy-start | bytes 12292
  148.0 6.9 %collective-permute-start.17 = (bf16[16,16,256]{2,1,0:T(8,128)(2,1)}, bf16[16,16,256]{2,1,0:T(8,128)(2,1)}, u32[]{:S(2)}, u32[]{:S(2)}) collective-permute-start(bf16[16,16,256]{2,1,0:T(8,128)(2,1)} %get-tuple-element.77), channel_id=1, source_target_pairs={{0,12},{4,0},{8,4},{12,8},{1,13},{5,1},{9,5},{13,9},{2,14},{6,2},{... | collective-permute-start | bytes 393224 | tf_op jit(solution)/shard_map/ppermute | solution.py:239
  150.0 6.6 %collective-permute-start.16 = (bf16[16,16,256]{2,1,0:T(8,128)(2,1)}, bf16[16,16,256]{2,1,0:T(8,128)(2,1)}, u32[]{:S(2)}, u32[]{:S(2)}) collective-permute-start(bf16[16,16,256]{2,1,0:T(8,128)(2,1)} %get-tuple-element.78), channel_id=1, source_target_pairs={{0,8},{4,12},{8,0},{12,4},{1,9},{5,13},{9,1},{13,5},{2,10},{6,14},... | collective-permute-start | bytes 393224 | tf_op jit(solution)/shard_map/ppermute | solution.py:239
  150.6 7.6 %collective-permute-start.15 = (bf16[16,16,256]{2,1,0:T(8,128)(2,1)}, bf16[16,16,256]{2,1,0:T(8,128)(2,1)}, u32[]{:S(2)}, u32[]{:S(2)}) collective-permute-start(bf16[16,16,256]{2,1,0:T(8,128)(2,1)} %get-tuple-element.79), channel_id=1, source_target_pairs={{0,4},{4,8},{8,12},{12,0},{1,5},{5,9},{9,13},{13,1},{2,6},{6,10},{... | collective-permute-start | bytes 393224 | tf_op jit(solution)/shard_map/ppermute | solution.py:239
  158.2 0.9 copy-start.2
  159.1 0.9 copy-start.4
  163.8 10.5 %collective-permute-start.18 = (bf16[256,1024]{1,0:T(8,128)(2,1)S(1)}, bf16[256,1024]{1,0:T(8,128)(2,1)S(1)}, u32[]{:S(2)}, u32[]{:S(2)}) collective-permute-start(bf16[256,1024]{1,0:T(8,128)(2,1)S(1)} %get-tuple-element.67), channel_id=1, source_target_pairs={{0,1},{1,0},{2,3},{3,2},{4,5},{5,4},{6,7},{7,6},{8,9},{9,8},{10,11... | collective-permute-start | bytes 1572872 | tf_op jit(solution)/shard_map/ppermute | solution.py:309
  174.5 16.9 %collective-permute-start.20 = (bf16[256,1024]{1,0:T(8,128)(2,1)S(1)}, bf16[256,1024]{1,0:T(8,128)(2,1)S(1)}, u32[]{:S(2)}, u32[]{:S(2)}) collective-permute-start(bf16[256,1024]{1,0:T(8,128)(2,1)S(1)} %add_convert_fusion.1), channel_id=1, source_target_pairs={{0,2},{2,0},{1,3},{3,1},{4,6},{6,4},{5,7},{7,5},{8,10},{10,8},{9,1... | collective-permute-start | bytes 1572872 | tf_op jit(solution)/shard_map/ppermute | solution.py:312
  182.7 8.7 %collective-permute-start.19 = (bf16[256,1024]{1,0:T(8,128)(2,1)S(1)}, bf16[256,1024]{1,0:T(8,128)(2,1)S(1)}, u32[]{:S(2)}, u32[]{:S(2)}) collective-permute-start(bf16[256,1024]{1,0:T(8,128)(2,1)S(1)} %get-tuple-element.70), channel_id=1, source_target_pairs={{0,1},{1,0},{2,3},{3,2},{4,5},{5,4},{6,7},{7,6},{8,9},{9,8},{10,11... | collective-permute-start | bytes 1572872 | tf_op jit(solution)/shard_map/ppermute | solution.py:315
Sparse Core Ops, SparseCore 0:
  9.3 56.4 all-gather.2
  72.8 42.5 all-gather.4

commit v2 on v1

--- a/solution.py
+++ b/solution.py
@@ -14,6 +14,9 @@
 SEQ = ("y", "zh", "x")
 SLABS = ("y", "zh")
 SWAP = [(0, 1), (1, 0)]
+INSIDE = pl.BlockSpec(memory_space=pltpu.VMEM)
+OUTSIDE = pl.BlockSpec(memory_space=pltpu.HBM)
+SCALARS = pl.BlockSpec(memory_space=pltpu.SMEM)
 
 
 def shift(count):
@@ -88,15 +91,20 @@
     return [lax.ppermute(block, axis, shift(step)) if step else block for step in range(4)]
 
 
-def project_kernel(own_ref, act_ref, *refs):
-    w_refs, (out, a_buf, w_buf, sems) = refs[:-4], refs[-4:]
+def project_kernel(whole, at_ref, act_ref, *refs):
+    a_buf, w_buf, sems = refs[-3:]
+    outs = refs[-8:-3] if whole else refs[-7:-3]
+    w_refs = refs[: len(refs) - 3 - len(outs)]
     rows, block = a_buf.shape[1], w_buf.shape[0] // len(w_refs)
+    own_y, own_x = at_ref[0], at_ref[1]
     copies = []
     for step, source in enumerate(w_refs):
-        row = pl.multiple_of(lax.rem(own_ref[0] + 4 - step, 4) * block, 16)
+        row = pl.multiple_of(lax.rem(own_y + 4 - step, 4) * block, 16)
         copies.append((source, w_buf.at[pl.ds(row, block)]))
-    for part in range(4):
-        copies.append((act_ref.at[pl.ds(part * rows, rows)], a_buf.at[part]))
+    parts = [lax.rem(own_x + step, 4) for step in range(4)]
+    for step, part in enumerate(parts):
+        row = pl.multiple_of(part * rows, 16)
+        copies.append((act_ref.at[pl.ds(row, rows)], a_buf.at[step]))
     copies = [
         pltpu.make_async_copy(src, dst, sems.at[at]) for at, (src, dst) in enumerate(copies)
     ]
@@ -104,29 +112,41 @@
         copy.start()
     for copy in copies[: len(w_refs)]:
         copy.wait()
-    for part in range(4):
-        copies[len(w_refs) + part].wait()
-        prod = jnp.dot(a_buf[part], w_buf[...], preferred_element_type=F32)
-        out[:, part] = prod.T.astype(BF16).reshape(16, 16, rows)
-
-
-def project(own, act, weights):
+    for step, part in enumerate(parts):
+        copies[len(w_refs) + step].wait()
+        prod = jnp.dot(a_buf[step], w_buf[...], preferred_element_type=F32).T.astype(BF16)
+        outs[step][...] = prod
+        if whole:
+            outs[4][:, part] = prod.reshape(16, 16, rows)
+
+
+def project(at, act, weights, whole):
     rows, depth = act.shape[0] // 4, act.shape[1]
     cols = weights[0].shape[1]
     count = len(weights) + 4
-    return pl.pallas_call(
-        project_kernel,
-        out_shape=jax.ShapeDtypeStruct((16, 4, cols // 16, rows), BF16),
-        in_specs=[pl.BlockSpec(memory_space=pltpu.SMEM)]
-        + [pl.BlockSpec(memory_space=pltpu.HBM)] * (len(weights) + 1),
-        out_specs=pl.BlockSpec(memory_space=pltpu.VMEM),
+    shapes = [(cols, rows)] * 4 + [(16, 4, cols // 16, rows)] * whole
+    return pl.pallas_call(
+        lambda *refs: project_kernel(whole, *refs),
+        out_shape=[jax.ShapeDtypeStruct(shape, BF16) for shape in shapes],
+        in_specs=[SCALARS] + [OUTSIDE] * (len(weights) + 1),
+        out_specs=[INSIDE] * len(shapes),
         scratch_shapes=[
             pltpu.VMEM((4, rows, depth), BF16),
             pltpu.VMEM((depth, cols), BF16),
             pltpu.SemaphoreType.DMA((count,)),
         ],
         compiler_params=pltpu.CompilerParams(vmem_limit_bytes=40 * 1024 * 1024),
-    )(own.reshape(1), *in_hbm([act, *weights]))
+    )(at, *in_hbm([act, *weights]))
+
+
+def fetch(sources, buffers, sems):
+    copies = [
+        pltpu.make_async_copy(src, dst, sems.at[at])
+        for at, (src, dst) in enumerate(zip(sources, buffers))
+    ]
+    for copy in copies:
+        copy.start()
+    return copies
 
 
 def column_block(weight_ref, block, w_buf, sem):
@@ -134,18 +154,20 @@
     return pltpu.make_async_copy(weight_ref.at[:, pl.ds(col, w_buf.shape[1])], w_buf, sem)
 
 
-def mix_kernel(at_ref, conv_ref, *refs):
-    values, gates, refs = refs[:4], refs[4:8], refs[8:]
-    skip_ref, weight_ref, home_ref, give_ref, w_buf, sem = refs
+def mix_kernel(at_ref, skip_ref, conv_hbm, *refs):
+    sources, weight_ref = (conv_hbm,) + refs[:8], refs[8]
+    home_ref, give_ref, conv_buf, vg_buf, w_buf, sem, sems = refs[9:]
     own_x, own_c, own_z = at_ref[1], at_ref[2], at_ref[3]
+    copies = fetch(sources, [conv_buf] + [vg_buf.at[at] for at in range(8)], sems)
     copy = column_block(weight_ref, 2 * (1 - own_z) + 1 - own_c, w_buf, sem)
     copy.start()
     rows = home_ref.shape[0]
+    for other in copies:
+        other.wait()
     for step in range(4):
         src = lax.rem(own_x + 4 - step, 4)
-        conv = conv_ref[:, src].astype(F32).reshape(256, rows)
-        value = values[step][...].astype(F32).reshape(256, rows)
-        gate = gates[step][...].astype(F32).reshape(256, rows)
+        conv = conv_buf[:, src].astype(F32).reshape(256, rows)
+        value, gate = vg_buf[step].astype(F32), vg_buf[4 + step].astype(F32)
         mixed = gate * (conv + skip_ref[src] * value)
         col = pl.multiple_of(src * 256, 128)
         home_ref[:, pl.ds(col, 256)] = mixed.T.astype(BF16)
@@ -153,22 +175,23 @@
     give_ref[...] = jnp.dot(home_ref[...], w_buf[...], preferred_element_type=F32).astype(BF16)
 
 
-INSIDE = pl.BlockSpec(memory_space=pltpu.VMEM)
-OUTSIDE = pl.BlockSpec(memory_space=pltpu.HBM)
-SCALARS = pl.BlockSpec(memory_space=pltpu.SMEM)
-
-
 def mix_and_give(at, conv, values, gates, skip, weight):
     rows = conv.shape[-1]
     one = jax.ShapeDtypeStruct((rows, 1024), BF16)
     return pl.pallas_call(
         mix_kernel,
         out_shape=(one, one),
-        in_specs=[SCALARS] + [INSIDE] * 10 + [OUTSIDE],
+        in_specs=[SCALARS, INSIDE] + [OUTSIDE] * 10,
         out_specs=(INSIDE, INSIDE),
-        scratch_shapes=[pltpu.VMEM((1024, 1024), BF16), pltpu.SemaphoreType.DMA],
+        scratch_shapes=[
+            pltpu.VMEM(conv.shape, BF16),
+            pltpu.VMEM((8, 256, rows), BF16),
+            pltpu.VMEM((1024, 1024), BF16),
+            pltpu.SemaphoreType.DMA,
+            pltpu.SemaphoreType.DMA((9,)),
+        ],
         compiler_params=pltpu.CompilerParams(vmem_limit_bytes=32 * 1024 * 1024),
-    )(at, conv, *values, *gates, skip, *in_hbm([weight]))
+    )(at, skip, *in_hbm([conv, *values, *gates, weight]))
 
 
 def away_kernel(at_ref, home_ref, weight_ref, away_ref, w_buf, sem):
@@ -219,25 +242,99 @@
     )(at, home, *in_hbm([weight]))
 
 
-def inner_tables(count):
-    idx = np.arange(count)
-    angle = (idx[:, None] * idx[None, :] % count) * (2.0 * math.pi / count)
+def tables(rows):
+    slab = np.arange(64)
+    angle = (slab[:, None] * slab[None, :] % 64) * (2.0 * math.pi / 64)
+    first = np.concatenate([np.cos(angle), -np.sin(angle)])
+    idx = np.arange(rows)
+    angle = slab[:, None] * idx[None, :] * (2.0 * math.pi / (64 * rows))
+    turn = np.stack([np.cos(angle), np.sin(angle)])
+    angle = (idx[:, None] * idx[None, :] % rows) * (2.0 * math.pi / rows)
     cos, sin = np.cos(angle), np.sin(angle)
     ahead = np.block([[cos, -sin], [sin, cos]])
     back = np.block([[cos, sin], [-sin, cos]])
-    return jnp.asarray(ahead, BF16), jnp.asarray(back, BF16)
+    last = first.T / (64 * rows)
+    return (
+        jnp.asarray(first, BF16),
+        jnp.asarray(last, BF16),
+        jnp.asarray(turn, F32),
+        jnp.asarray(ahead, BF16),
+        jnp.asarray(back, BF16),
+    )
 
 
 def mm(left, right):
     return jnp.dot(left, right, preferred_element_type=F32)
 
 
-def along_x(parts, own):
-    pieces = []
-    for step in range(4):
-        piece = lax.dynamic_index_in_dim(parts, (own + step) % 4, 1, keepdims=False)
-        pieces.append(lax.ppermute(piece, "x", shift(step)) if step else piece)
-    return pieces
+def filter_kernel(first, last, turn, *refs):
+    sources, out_ref, x_buf, h_buf = refs[:4], refs[4], refs[5], refs[6]
+    buffers, sems = refs[7:11], refs[11]
+    slab_ref, resp_ref, ahead, back = buffers
+    for copy in fetch(sources, buffers, sems):
+        copy.wait()
+    rows = slab_ref.shape[1]
+    for ref, buf in ((slab_ref, x_buf), (resp_ref, h_buf)):
+        for part in range(buf.shape[0]):
+            buf[part] = ref[:, part * 128 : (part + 1) * 128].astype(F32)
+
+    def pick_rows(buf, pick):
+        return jnp.concatenate([buf[part, pick, :] for part in range(buf.shape[0])], axis=1)
+
+    t_cos, t_sin = turn[0], turn[1]
+    group = 4
+    for start in range(0, 16, group):
+        picks = [pl.ds(start + at, 64, stride=16) for at in range(group)]
+        turned = []
+        for pick in picks:
+            sect = mm(first[...], pick_rows(x_buf, pick).astype(BF16))
+            re, im = sect[:64], sect[64:]
+            turned.append(
+                jnp.concatenate([re * t_cos + im * t_sin, im * t_cos - re * t_sin], axis=1)
+            )
+        spec = mm(jnp.concatenate(turned).astype(BF16), ahead[...])
+        prods = []
+        for at, pick in enumerate(picks):
+            re, im = spec[at * 64 : (at + 1) * 64, :rows], spec[at * 64 : (at + 1) * 64, rows:]
+            resp = pick_rows(h_buf, pick)
+            h_re, h_im = resp[:, :rows], resp[:, rows:]
+            prods.append(
+                jnp.concatenate([re * h_re - im * h_im, re * h_im + im * h_re], axis=1)
+            )
+        inv = mm(jnp.concatenate(prods).astype(BF16), back[...])
+        for at, pick in enumerate(picks):
+            re, im = inv[at * 64 : (at + 1) * 64, :rows], inv[at * 64 : (at + 1) * 64, rows:]
+            reverted = jnp.concatenate([re * t_cos - im * t_sin, re * t_sin + im * t_cos])
+            conv = mm(last[...], reverted.astype(BF16))
+            for part in range(x_buf.shape[0]):
+                x_buf[part, pick, :] = conv[:, part * 128 : (part + 1) * 128]
+    for part in range(x_buf.shape[0]):
+        out_ref[:, part * 128 : (part + 1) * 128] = x_buf[part].astype(BF16)
+
+
+def filtered(slabs, resp):
+    count, rows = slabs.shape
+    first, last, turn, ahead, back = tables(rows)
+    return pl.pallas_call(
+        filter_kernel,
+        out_shape=jax.ShapeDtypeStruct((count, rows), BF16),
+        in_specs=[INSIDE] * 3 + [OUTSIDE] * 4,
+        out_specs=INSIDE,
+        scratch_shapes=[
+            pltpu.VMEM((rows // 128, count, 128), F32),
+            pltpu.VMEM((2 * rows // 128, count, 128), F32),
+            pltpu.VMEM((count, rows), BF16),
+            pltpu.VMEM((count, 2 * rows), BF16),
+            pltpu.VMEM((2 * rows, 2 * rows), BF16),
+            pltpu.VMEM((2 * rows, 2 * rows), BF16),
+            pltpu.SemaphoreType.DMA((4,)),
+        ],
+        compiler_params=pltpu.CompilerParams(vmem_limit_bytes=32 * 1024 * 1024),
+    )(first, last, turn, *in_hbm([slabs, resp, ahead, back]))
+
+
+def along_x(pieces):
+    return [lax.ppermute(p, "x", shift(step)) if step else p for step, p in enumerate(pieces)]
 
 
 def body(sequence_in, value_proj, gate_proj, filter_response, skip_weight, output_proj):
@@ -246,62 +343,32 @@
     my_y, my_x, my_zl, my_c = (lax.axis_index(a) for a in ("y", "x", "zl", "c"))
     at = jnp.stack([my_y, my_x, my_c, my_zl])
 
-    act = lax.dynamic_slice(sequence_in, (my_c * half, 0), (half, sequence_in.shape[1]))
-    act = lax.all_gather(act, ("x", "c"), axis=0, tiled=True)
-
-    resp = turn_filter(filter_response.reshape(2 * rows, 1024)).reshape(64, 16, 2 * rows)
-
-    wg = split_columns(my_x, value_proj, gate_proj)
+    resp = turn_filter(filter_response.reshape(2 * rows, 1024))
+    resp, ahead_x, ahead_c = tie(resp, my_x, my_c)
+    resp = lax.all_to_all(resp.reshape(64, 16, 2 * rows), SEQ, 0, 0, tiled=True)
+
+    wg = split_columns(ahead_x, value_proj, gate_proj)
     wg = [lax.ppermute(p, "x", shift(step)) if step else p for step, p in enumerate(wg)]
-    resp, *wg = tie(resp, *wg)
-    resp = lax.all_to_all(resp, SEQ, 0, 0, tiled=True)
     w_x, g_x = place(my_x, wg, 2)
     my_zh = lax.axis_index("zh")
+
+    act = lax.dynamic_slice(sequence_in, (ahead_c * half, 0), (half, sequence_in.shape[1]))
+    act = lax.all_gather(act, ("x", "c"), axis=0, tiled=True)
+
     (w_y,) = place(my_zh, to_all(w_x, "zh"), 1)
     w_y, g_x = tie(w_y, g_x)
     w_all = to_all(w_y, "y")
-    g_z = to_all(g_x, "zh")
-    *w_all, g_z[1], g_z[2], g_z[3] = tie(*w_all, *g_z[1:])
-    (g_y,) = place(my_zh, g_z, 1)
+    (g_y,) = place(my_zh, to_all(g_x, "zh"), 1)
+    *w_all, resp, g_y = tie(*w_all, resp, g_y)
     g_all = lax.all_gather(g_y, "y", axis=0, tiled=True)
-    value = project(my_y, act, w_all)
-    value, resp = tie(value, resp)
-    full = rows * 64
-
+    *values, value = project(at, act, w_all, True)
     slabs = lax.all_to_all(value, SLABS, 0, 0, tiled=True)
-    values = along_x(value, my_x)
-    slabs, g_all, *values = tie(slabs, g_all, *values)
-    slabs = slabs.reshape(64, 16, rows)
-
-    s_idx = lax.iota(jnp.int32, 64)
-    k_idx = lax.iota(jnp.int32, 64)
-
-    def slab_table(order):
-        angle = (k_idx[:, None] * order[None, :] % 64).astype(F32) * (2.0 * math.pi / 64)
-        return jnp.concatenate([jnp.cos(angle), -jnp.sin(angle)])
-
-    first = slab_table(s_idx).astype(BF16)
-    last = (slab_table(s_idx) / full).astype(BF16)
-    r_idx = lax.iota(jnp.int32, rows)
-    twist = (k_idx[:, None] * r_idx[None, :]).astype(F32) * (2.0 * math.pi / full)
-    t_cos, t_sin = jnp.cos(twist)[:, None, :], jnp.sin(twist)[:, None, :]
-    ahead, back = inner_tables(rows)
-
-    sect = jnp.einsum("ks,scr->kcr", first, slabs, preferred_element_type=F32)
-    re, im = sect[:64], sect[64:]
-    turned = jnp.concatenate([re * t_cos + im * t_sin, im * t_cos - re * t_sin], axis=2)
-    spec = mm(turned.astype(BF16), ahead)
-    re, im = spec[..., :rows], spec[..., rows:]
-    resp = resp.astype(F32)
-    h_re, h_im = resp[..., :rows], resp[..., rows:]
-    prod = jnp.concatenate([re * h_re - im * h_im, re * h_im + im * h_re], axis=2)
-    inv = mm(prod.astype(BF16), back)
-    re, im = inv[..., :rows], inv[..., rows:]
-    reverted = jnp.concatenate([re * t_cos - im * t_sin, re * t_sin + im * t_cos], axis=0)
-    conv = jnp.einsum("ks,kcr->scr", last, reverted.astype(BF16), preferred_element_type=F32)
-    conv = lax.all_to_all(conv.astype(BF16), SEQ, 0, 0, tiled=True).reshape(16, 4, 16, rows)
-    gate = project(my_y * 0, act, [g_all])
-    gates = along_x(gate, my_x)
+    values = along_x(values)
+    slabs, *values = tie(slabs, *values)
+    conv = filtered(slabs.reshape(1024, rows), resp.reshape(1024, 2 * rows))
+    conv = conv.reshape(64, 16, rows)
+    conv = lax.all_to_all(conv, SEQ, 0, 0, tiled=True).reshape(16, 4, 16, rows)
+    gates = along_x(project(at * jnp.array([0, 1, 0, 0], jnp.int32), act, [g_all], False))
 
     home, give = mix_and_give(
         at, conv, values, gates, skip_weight.reshape(4, 256, 1), output_proj

time: 200 us -> 192 us (0.960)
  waiting for transfers between devices: 61.6 us -> 40.9 us
  starting transfers between devices: 67.2 us -> 85.2 us
  Pallas kernels: 35.8 us -> 42.9 us
  other arithmetic: 5.85 us -> 1.25 us
  local copies, waits for them, and re-layouts: 11.5 us -> 7.91 us
  matrix products: 3.51 us -> 0 us
    all_to_all x2, waiting for transfers between devices: 16.2 us -> 0.01 us  [the longest x1 0.01 us: body(): resp = lax.all_to_all(resp.reshape(64, 16, 2 * rows), SEQ, 0, 0, tiled=True)]
    ppermute x9, waiting for transfers between devices: 26.2 us -> 10.1 us  [to_all(): lax.ppermute(block, axis, shift(step))]
    all_to_all x2, starting transfers between devices: 17.5 us -> 29.7 us  [the longest x1 15.1 us: body(): resp = lax.all_to_all(resp.reshape(64, 16, 2 * rows), SEQ, 0, 0, tiled=True)]
    ppermute x3, waiting for transfers between devices: 0.01 us -> 8.33 us  [body(): lax.ppermute(p, 'x', shift(step))]
    pallas_call x3 -> x4, Pallas kernels: 19.5 us -> 26.6 us  [the longest x2 16.9 us: project(): pl.pallas_call(lambda *refs: project_kernel(whole, *refs), out_shape=[jax...]
    ppermute x1, starting transfers between devices: 7.66 us -> 1.1 us  [body(): got = lax.ppermute(give, 'c', SWAP)]
    ppermute x6, starting transfers between devices: 6.83 us -> 13.4 us  [along_x(): lax.ppermute(p, 'x', shift(step))]
    all_to_all x1, starting transfers between devices: 4.24 us -> 10.5 us  [body(): slabs = lax.all_to_all(value, SLABS, 0, 0, tiled=True)]
  transfers between devices with their start and end apart: 26 -> 26, of which waited for: 14 -> 14; matrix products, arithmetic and copies ran while one was open for 3% -> 0% of each run, Pallas kernels for 16% -> 19%
where the time goes in v2:
time: 192 us
  starting transfers between devices  85.2 us (44%)
  Pallas kernels  42.9 us (22%)
  waiting for transfers between devices  40.9 us (21%)
  between operations  13.6 us (7%)
  local copies, waits for them, and re-layouts  7.91 us (4%)
    ppermute x9, starting transfers between devices, to_all(): lax.ppermute(block, axis, shift(step))  25.6 us
    pallas_call x2, Pallas kernels, project(): pl.pallas_call(lambda *refs: project_kernel(whole, *refs), out_shape=[jax...  16.9 us
    all_to_all x1, starting transfers between devices, body(): resp = lax.all_to_all(resp.reshape(64, 16, 2 * rows), SEQ, 0, 0, tiled=True)  15.1 us
    all_to_all x1, starting transfers between devices, body(): conv = lax.all_to_all(conv, SEQ, 0, 0, tiled=True).reshape(16, 4, 16, rows)  14.6 us
    ppermute x6, starting transfers between devices, along_x(): lax.ppermute(p, 'x', shift(step))  13.4 us
    ppermute x6, waiting for transfers between devices, along_x(): lax.ppermute(p, 'x', shift(step))  12.6 us
    all_to_all x1, starting transfers between devices, body(): slabs = lax.all_to_all(value, SLABS, 0, 0, tiled=True)  10.5 us
    ppermute x9, waiting for transfers between devices, to_all(): lax.ppermute(block, axis, shift(step))  10.1 us
  transfers between devices with their start and end apart: 26, of which 14 were waited for; matrix products, arithmetic and copies ran while one was open for 0% of the time, Pallas kernels for 19%

profile of v2, /device:TPU:1, one launch (start us, length us, event | category | flops | bytes accessed | tf_op | source)
XLA Modules:
  0.0 191.8 jit_solution(3200576342647043345)
XLA Ops:
  6.5 2.7 %shard_map.118 = bf16[16,4,16,512]{3,2,1,0:T(8,128)(2,1)} custom-call(bf16[512,1024]{1,0:T(8,128)(2,1)} %bitcast.16), custom_call_target="tpu_custom_call" | custom-call | tf_op jit(solution)/shard_map/pallas_call | solution.py:42
  9.2 1.1 constant_dynamic-slice_fusion
  10.3 15.1 %all-to-all-start = ((bf16[64,16,512]{2,1,0:T(8,128)(2,1)}), bf16[64,16,512]{2,1,0:T(8,128)(2,1)S(1)}, u32[]{:S(2)}, u32[]{:S(2)}) async-start(bf16[64,16,512]{2,1,0:T(8,128)(2,1)} %bitcast.13), calls=%async_computation | async-start | bytes 2097152 | tf_op jit(solution)/shard_map/all_to_all | solution.py:348
  25.5 1.7 shard_map.119
  27.3 1.0 collective-permute-start
  28.3 2.4 %collective-permute-start.1 = (bf16[128,256]{1,0:T(8,128)(2,1)}, bf16[128,256]{1,0:T(8,128)(2,1)S(1)}, u32[]{:S(2)}, u32[]{:S(2)}) collective-permute-start(bf16[128,256]{1,0:T(8,128)(2,1)} %get-tuple-element.45), channel_id=1, source_target_pairs={{0,8},{4,12},{8,0},{12,4},{1,9},{5,13},{9,1},{13,5},{2,10},{6,14},... | collective-permute-start | bytes 196616 | tf_op jit(solution)/shard_map/ppermute | solution.py:351
  30.7 1.2 collective-permute-start.2
  31.9 4.7 %collective-permute-done.refs_1_ = bf16[128,256]{1,0:T(8,128)(2,1)S(1)} collective-permute-done((bf16[128,256]{1,0:T(8,128)(2,1)}, bf16[128,256]{1,0:T(8,128)(2,1)S(1)}, u32[]{:S(2)}, u32[]{:S(2)}) %collective-permute-start) | collective-permute-done | bytes 65568 | tf_op jit(solution)/shard_map/ppermute | solution.py:351
  36.6 2.9 %collective-permute-done.1.refs_2_ = bf16[128,256]{1,0:T(8,128)(2,1)S(1)} collective-permute-done((bf16[128,256]{1,0:T(8,128)(2,1)}, bf16[128,256]{1,0:T(8,128)(2,1)S(1)}, u32[]{:S(2)}, u32[]{:S(2)}) %collective-permute-start.1) | collective-permute-done | bytes 65568 | tf_op jit(solution)/shard_map/ppermute | solution.py:351
  39.5 0.7 collective-permute-done.2.refs_3_
  40.2 0.6 copy-done.19
  40.8 1.7 shard_map.120
  42.5 2.8 %collective-permute-start.3 = (bf16[256,256]{1,0:T(8,128)(2,1)}, bf16[256,256]{1,0:T(8,128)(2,1)S(1)}, u32[]{:S(2)}, u32[]{:S(2)}) collective-permute-start(bf16[256,256]{1,0:T(8,128)(2,1)} %get-tuple-element.47.refs_0_), channel_id=1, source_target_pairs={{0,16},{16,32},{32,48},{48,0},{1,17},{17,33},{33,49},{49,1},{2,18}... | collective-permute-start | bytes 393224 | tf_op jit(solution)/shard_map/ppermute | solution.py:91
  45.3 4.6 %collective-permute-start.4 = (bf16[256,256]{1,0:T(8,128)(2,1)}, bf16[256,256]{1,0:T(8,128)(2,1)S(1)}, u32[]{:S(2)}, u32[]{:S(2)}) collective-permute-start(bf16[256,256]{1,0:T(8,128)(2,1)} %get-tuple-element.47.refs_0_), channel_id=1, source_target_pairs={{0,32},{16,48},{32,0},{48,16},{1,33},{17,49},{33,1},{49,17},{2,34}... | collective-permute-start | bytes 393224 | tf_op jit(solution)/shard_map/ppermute | solution.py:91
  49.9 3.6 %collective-permute-start.5 = (bf16[256,256]{1,0:T(8,128)(2,1)}, bf16[256,256]{1,0:T(8,128)(2,1)S(1)}, u32[]{:S(2)}, u32[]{:S(2)}) collective-permute-start(bf16[256,256]{1,0:T(8,128)(2,1)} %get-tuple-element.47.refs_0_), channel_id=1, source_target_pairs={{0,48},{16,0},{32,16},{48,32},{1,49},{17,1},{33,17},{49,33},{2,50}... | collective-permute-start | bytes 393224 | tf_op jit(solution)/shard_map/ppermute | solution.py:91
  53.5 4.1 %collective-permute-done.4.refs_2_ = bf16[256,256]{1,0:T(8,128)(2,1)S(1)} collective-permute-done((bf16[256,256]{1,0:T(8,128)(2,1)}, bf16[256,256]{1,0:T(8,128)(2,1)S(1)}, u32[]{:S(2)}, u32[]{:S(2)}) %collective-permute-start.4) | collective-permute-done | bytes 131104 | tf_op jit(solution)/shard_map/ppermute | solution.py:91
  57.6 0.2 collective-permute-done.5.refs_3_
  57.8 0.4 copy-done.12
  58.2 0.2 copy-done.14
  58.5 1.9 %shard_map.121.refs_2_ = bf16[1024,256]{1,0:T(8,128)(2,1)} custom-call(s32[1]{0:T(128)} %bitcast.5.own_ref, bf16[256,256]{1,0:T(8,128)(2,1)} %get-tuple-element.47.refs_0_, bf16[256,256]{1,0:T(8,128)(2,1)} %copy-done.11, bf16[256,256]{1,0:T(8,128)(2,1)} %copy-done.12, bf16[256,256]{1,0:T(8,128)(2,1)} %copy-done.14), custom_call_target="tpu_custom_call" | custom-call | tf_op jit(solution)/shard_map/pallas_call | solution.py:82
  60.4 2.8 %collective-permute-start.6 = (bf16[1024,256]{1,0:T(8,128)(2,1)}, bf16[1024,256]{1,0:T(8,128)(2,1)}, u32[]{:S(2)}, u32[]{:S(2)}) collective-permute-start(bf16[1024,256]{1,0:T(8,128)(2,1)} %shard_map.121.refs_2_), channel_id=1, source_target_pairs={{0,64},{64,128},{128,192},{192,0},{1,65},{65,129},{129,193},{193,1... | collective-permute-start | bytes 1572872 | tf_op jit(solution)/shard_map/ppermute | solution.py:91
  63.3 1.4 collective-permute-start.7
  64.6 1.0 collective-permute-start.8
  65.6 3.0 %collective-permute-start.9 = (bf16[256,256]{1,0:T(8,128)(2,1)}, bf16[256,256]{1,0:T(8,128)(2,1)S(1)}, u32[]{:S(2)}, u32[]{:S(2)}) collective-permute-start(bf16[256,256]{1,0:T(8,128)(2,1)} %get-tuple-element.51.refs_0_), channel_id=1, source_target_pairs={{0,16},{16,32},{32,48},{48,0},{1,17},{17,33},{33,49},{49,1},{2,18}... | collective-permute-start | bytes 393224 | tf_op jit(solution)/shard_map/ppermute | solution.py:91
  68.6 3.7 %collective-permute-start.10 = (bf16[256,256]{1,0:T(8,128)(2,1)}, bf16[256,256]{1,0:T(8,128)(2,1)S(1)}, u32[]{:S(2)}, u32[]{:S(2)}) collective-permute-start(bf16[256,256]{1,0:T(8,128)(2,1)} %get-tuple-element.51.refs_0_), channel_id=1, source_target_pairs={{0,32},{16,48},{32,0},{48,16},{1,33},{17,49},{33,1},{49,17},{2,34}... | collective-permute-start | bytes 393224 | tf_op jit(solution)/shard_map/ppermute | solution.py:91
  72.3 0.5 collective-permute-done.9.refs_1_
  72.8 2.7 %collective-permute-start.11 = (bf16[256,256]{1,0:T(8,128)(2,1)}, bf16[256,256]{1,0:T(8,128)(2,1)S(1)}, u32[]{:S(2)}, u32[]{:S(2)}) collective-permute-start(bf16[256,256]{1,0:T(8,128)(2,1)} %get-tuple-element.51.refs_0_), channel_id=1, source_target_pairs={{0,48},{16,0},{32,16},{48,32},{1,49},{17,1},{33,17},{49,33},{2,50}... | collective-permute-start | bytes 393224 | tf_op jit(solution)/shard_map/ppermute | solution.py:91
  75.5 1.1 collective-permute-done.10.refs_2_
  76.6 2.7 %collective-permute-done.11.refs_3_ = bf16[256,256]{1,0:T(8,128)(2,1)S(1)} collective-permute-done((bf16[256,256]{1,0:T(8,128)(2,1)}, bf16[256,256]{1,0:T(8,128)(2,1)S(1)}, u32[]{:S(2)}, u32[]{:S(2)}) %collective-permute-start.11) | collective-permute-done | bytes 131104 | tf_op jit(solution)/shard_map/ppermute | solution.py:91
  79.3 0.6 copy-done.16
  80.0 1.9 %shard_map.122 = bf16[1024,256]{1,0:T(8,128)(2,1)} custom-call(s32[1]{0:T(128)} %bitcast.5.own_ref, bf16[256,256]{1,0:T(8,128)(2,1)} %get-tuple-element.51.refs_0_, bf16[256,256]{1,0:T(8,128)(2,1)} %copy-done.13, bf16[256,256]{1,0:T(8,128)(2,1)} %copy-done.15, bf16[256,256]{1,0:T(8,128)(2,1)} %copy-done.16), custom_call_target="tpu_custom_call" | custom-call | tf_op jit(solution)/shard_map/pallas_call | solution.py:82
  81.9 1.5 collective-permute-done.8.refs_5_
  83.4 1.0 copy-done.6
  84.4 0.1 fusion
  84.5 8.8 %shard_map.123 = (bf16[256,256]{1,0:T(8,128)(2,1)S(1)}, bf16[256,256]{1,0:T(8,128)(2,1)S(1)}, bf16[256,256]{1,0:T(8,128)(2,1)S(1)}, bf16[256,256]{1,0:T(8,128)(2,1)S(1)}, bf16[16,4,16,256]{3,2,1,0:T(8,128)(2,1)}) custom-call(s32[4]{0:T(128)S(1)} %get-tuple-element.78.refs_0_.at_ref, bf16[1024,4096]{1,0:T(8,128)(2,1)} %all-gather.3.cloned.1.call-done.refs_1_, ...), custom_call_target="tpu_custom_call" | custom-call | tf_op jit(solution)/shard_map/pallas_call | solution.py:128
  93.4 0.6 copy-done.1
  94.0 10.5 %all-to-all-start.1 = ((bf16[16,4,16,256]{3,2,1,0:T(8,128)(2,1)}), bf16[16,4,16,256]{3,2,1,0:T(8,128)(2,1)S(1)}, u32[]{:S(2)}, u32[]{:S(2)}) async-start(bf16[16,4,16,256]{3,2,1,0:T(8,128)(2,1)} %get-tuple-element.56), calls=%async_computation.1 | async-start | bytes 1048576 | tf_op jit(solution)/shard_map/all_to_all | solution.py:365
  104.6 5.5 %collective-permute-start.12 = (bf16[256,256]{1,0:T(8,128)(2,1)S(1)}, bf16[256,256]{1,0:T(8,128)(2,1)S(1)}, u32[]{:S(2)}, u32[]{:S(2)}) collective-permute-start(bf16[256,256]{1,0:T(8,128)(2,1)S(1)} %get-tuple-element.58), channel_id=1, source_target_pairs={{0,4},{4,8},{8,12},{12,0},{1,5},{5,9},{9,13},{13,1},{2,6},{6,10},{... | collective-permute-start | bytes 393224 | tf_op jit(solution)/shard_map/ppermute | solution.py:337
  110.1 3.0 %collective-permute-start.13 = (bf16[256,256]{1,0:T(8,128)(2,1)S(1)}, bf16[256,256]{1,0:T(8,128)(2,1)S(1)}, u32[]{:S(2)}, u32[]{:S(2)}) collective-permute-start(bf16[256,256]{1,0:T(8,128)(2,1)S(1)} %get-tuple-element.59), channel_id=1, source_target_pairs={{0,8},{4,12},{8,0},{12,4},{1,9},{5,13},{9,1},{13,5},{2,10},{6,14},... | collective-permute-start | bytes 393224 | tf_op jit(solution)/shard_map/ppermute | solution.py:337
  113.1 0.3 collective-permute-start.14
  113.4 1.8 collective-permute-done.12.refs_1_
  115.1 3.6 %collective-permute-done.13.refs_2_ = bf16[256,256]{1,0:T(8,128)(2,1)S(1)} collective-permute-done((bf16[256,256]{1,0:T(8,128)(2,1)S(1)}, bf16[256,256]{1,0:T(8,128)(2,1)S(1)}, u32[]{:S(2)}, u32[]{:S(2)}) %collective-permute-start.13) | collective-permute-done | bytes 131104 | tf_op jit(solution)/shard_map/ppermute | solution.py:337
  118.7 0.7 copy-done.10
  119.4 0.8 copy-done.7
  120.2 6.3 %shard_map.124 = bf16[1024,256]{1,0:T(8,128)(2,1)} custom-call(bf16[128,64]{1,0:T(8,128)(2,1)S(1)} %copy-done.4, bf16[64,128]{1,0:T(8,128)(2,1)S(1)} %copy-done.5, f32[2,64,256]{2,1,0:T(8,128)S(1)} %copy-done.3, bf16[1024,256]{1,0:T(8,128)(2,1)} %bitcast.14, bf16[1024,512]{1,0:T(8,128)(2,1)} %bitcast.12, bf16[512,512]{1,0:T(8,128)(2,1)} %constant.40.clone.refs_2_, ...), custom_call_target="tpu_custom_call" | custom-call | tf_op jit(solution)/shard_map/pallas_call | solution.py:318
  126.5 14.6 %all-to-all-start.2 = ((bf16[64,16,256]{2,1,0:T(8,128)(2,1)}), bf16[64,16,256]{2,1,0:T(8,128)(2,1)S(1)}, u32[]{:S(2)}, u32[]{:S(2)}) async-start(bf16[64,16,256]{2,1,0:T(8,128)(2,1)} %bitcast.10), calls=%async_computation.2 | async-start | bytes 1048576 | tf_op jit(solution)/shard_map/all_to_all | solution.py:370
  141.1 8.0 %shard_map.125 = (bf16[256,256]{1,0:T(8,128)(2,1)S(1)}, bf16[256,256]{1,0:T(8,128)(2,1)S(1)}, bf16[256,256]{1,0:T(8,128)(2,1)S(1)}, bf16[256,256]{1,0:T(8,128)(2,1)S(1)}) custom-call(s32[4]{0:T(128)S(1)} %get-tuple-element.77.refs_0_, bf16[1024,4096]{1,0:T(8,128)(2,1)} %all-gather.3.cloned.1.call-done.refs_1_, ...), custom_call_target="tpu_custom_call" | custom-call | tf_op jit(solution)/shard_map/pallas_call | solution.py:128
  149.1 0.6 copy-done.2
  149.8 1.0 collective-permute-start.15
  150.8 2.4 %collective-permute-start.16 = (bf16[256,256]{1,0:T(8,128)(2,1)S(1)}, bf16[256,256]{1,0:T(8,128)(2,1)}, u32[]{:S(2)}, u32[]{:S(2)}) collective-permute-start(bf16[256,256]{1,0:T(8,128)(2,1)S(1)} %get-tuple-element.70), channel_id=1, source_target_pairs={{0,8},{4,12},{8,0},{12,4},{1,9},{5,13},{9,1},{13,5},{2,10},{6,14},... | collective-permute-start | bytes 393224 | tf_op jit(solution)/shard_map/ppermute | solution.py:337
  153.2 1.2 collective-permute-start.17
  154.4 0.3 reshape.38.skip_ref
  154.7 3.3 %collective-permute-done.15.refs_5_ = bf16[256,256]{1,0:T(8,128)(2,1)} collective-permute-done((bf16[256,256]{1,0:T(8,128)(2,1)S(1)}, bf16[256,256]{1,0:T(8,128)(2,1)}, u32[]{:S(2)}, u32[]{:S(2)}) %collective-permute-start.15) | collective-permute-done | bytes 131104 | tf_op jit(solution)/shard_map/ppermute | solution.py:337
  158.0 4.0 %collective-permute-done.16.refs_6_ = bf16[256,256]{1,0:T(8,128)(2,1)} collective-permute-done((bf16[256,256]{1,0:T(8,128)(2,1)S(1)}, bf16[256,256]{1,0:T(8,128)(2,1)}, u32[]{:S(2)}, u32[]{:S(2)}) %collective-permute-start.16) | collective-permute-done | bytes 131104 | tf_op jit(solution)/shard_map/ppermute | solution.py:337
  162.0 0.8 copy-done.8
  162.7 3.4 %shard_map.126 = (bf16[256,1024]{1,0:T(8,128)(2,1)S(1)}, bf16[256,1024]{1,0:T(8,128)(2,1)S(1)}) custom-call(s32[4]{0:T(128)S(1)} %get-tuple-element.78.refs_0_.at_ref, f32[4,256,1]{2,1,0:T(8,128)S(1)} %reshape.38.skip_ref, bf16[16,4,16,256]{3,2,1,0:T(8,128)(2,1)} %bitcast.15, bf16[256,256]{1,0:T(8,128)(2,1)} %copy-done.1, bf16[256,256]{1,0:T(8,128)(2,1)} %copy-done.9, ...), custom_call_target="tpu_custom_call" | custom-call | tf_op jit(solution)/shard_map/pallas_call | solution.py:181
  166.2 1.1 collective-permute-start.18
  167.3 2.9 %shard_map.127 = f32[256,1024]{1,0:T(8,128)S(1)} custom-call(s32[4]{0:T(128)S(1)} %get-tuple-element.78.refs_0_.at_ref, bf16[256,1024]{1,0:T(8,128)(2,1)S(1)} %get-tuple-element.74.home_ref, bf16[1024,4096]{1,0:T(8,128)(2,1)} %weight_ref.3), custom_call_target="tpu_custom_call" | custom-call | tf_op jit(solution)/shard_map/pallas_call | solution.py:205
  170.1 0.1 add_convert_fusion.1
  170.3 0.1 collective-permute-start.20
  170.4 3.6 %shard_map.128 = (bf16[256,1024]{1,0:T(8,128)(2,1)S(1)}, f32[256,1024]{1,0:T(8,128)S(1)}) custom-call(s32[4]{0:T(128)S(1)} %get-tuple-element.78.refs_0_.at_ref, bf16[256,1024]{1,0:T(8,128)(2,1)S(1)} %get-tuple-element.74.home_ref, bf16[1024,4096]{1,0:T(8,128)(2,1)} %weight_ref.3), custom_call_target="tpu_custom_call" | custom-call | tf_op jit(solution)/shard_map/pallas_call | solution.py:232
  174.0 0.1 collective-permute-start.19
  174.1 9.8 %collective-permute-done.20 = bf16[256,1024]{1,0:T(8,128)(2,1)S(1)} collective-permute-done((bf16[256,1024]{1,0:T(8,128)(2,1)S(1)}, bf16[256,1024]{1,0:T(8,128)(2,1)S(1)}, u32[]{:S(2)}, u32[]{:S(2)}) %collective-permute-start.20) | collective-permute-done | bytes 524320 | tf_op jit(solution)/shard_map/ppermute | solution.py:379
  183.9 1.0 add_convert_fusion
  (50 shorter events, 0.2 us)
Async XLA Ops:
  6.5 2.7 %copy-start = (bf16[256,4096]{1,0:T(8,128)(2,1)S(1)}, bf16[256,4096]{1,0:T(8,128)(2,1)}, u32[]{:S(2)}) copy-start(bf16[256,4096]{1,0:T(8,128)(2,1)} %param.12) | copy-start | bytes 6291460
  6.5 78.0 %all-gather.3.cloned.1.call-start = ((), (), s32[]{:S(2)}) async-start(), calls=%async_computation.3 | async-start | bytes 9437184 | tf_op jit(solution)/shard_map/all_gather | solution.py:356
  10.3 73.1 %all-to-all-start = ((bf16[64,16,512]{2,1,0:T(8,128)(2,1)}), bf16[64,16,512]{2,1,0:T(8,128)(2,1)S(1)}, u32[]{:S(2)}, u32[]{:S(2)}) async-start(bf16[64,16,512]{2,1,0:T(8,128)(2,1)} %bitcast.13), calls=%async_computation | async-start | bytes 2097152 | tf_op jit(solution)/shard_map/all_to_all | solution.py:348
  25.5 59.0 %copy-start.21 = (s32[4]{0:T(128)S(1)}, s32[4]{0:T(128)}, u32[]{:S(2)}) copy-start(s32[4]{0:T(128)} %constant.42.clone) | copy-start | bytes 52
  25.5 115.6 %all-gather.5.cloned.1.call-start = ((), (), s32[]{:S(2)}) async-start(), calls=%async_computation.4 | async-start | bytes 2621440 | tf_op jit(solution)/shard_map/all_gather | solution.py:363
  27.3 9.3 %collective-permute-start = (bf16[128,256]{1,0:T(8,128)(2,1)}, bf16[128,256]{1,0:T(8,128)(2,1)S(1)}, u32[]{:S(2)}, u32[]{:S(2)}) collective-permute-start(bf16[128,256]{1,0:T(8,128)(2,1)} %get-tuple-element.44), channel_id=1, source_target_pairs={{0,4},{4,8},{8,12},{12,0},{1,5},{5,9},{9,13},{13,1},{2,6},{6,10},{... | collective-permute-start | bytes 196616 | tf_op jit(solution)/shard_map/ppermute | solution.py:351
  28.3 11.2 %collective-permute-start.1 = (bf16[128,256]{1,0:T(8,128)(2,1)}, bf16[128,256]{1,0:T(8,128)(2,1)S(1)}, u32[]{:S(2)}, u32[]{:S(2)}) collective-permute-start(bf16[128,256]{1,0:T(8,128)(2,1)} %get-tuple-element.45), channel_id=1, source_target_pairs={{0,8},{4,12},{8,0},{12,4},{1,9},{5,13},{9,1},{13,5},{2,10},{6,14},... | collective-permute-start | bytes 196616 | tf_op jit(solution)/shard_map/ppermute | solution.py:351
  30.7 9.5 %collective-permute-start.2 = (bf16[128,256]{1,0:T(8,128)(2,1)}, bf16[128,256]{1,0:T(8,128)(2,1)S(1)}, u32[]{:S(2)}, u32[]{:S(2)}) collective-permute-start(bf16[128,256]{1,0:T(8,128)(2,1)} %get-tuple-element.46), channel_id=1, source_target_pairs={{0,12},{4,0},{8,4},{12,8},{1,13},{5,1},{9,5},{13,9},{2,14},{6,2},{... | collective-permute-start | bytes 196616 | tf_op jit(solution)/shard_map/ppermute | solution.py:351
  36.6 3.6 %copy-start.17 = (bf16[128,256]{1,0:T(8,128)(2,1)}, bf16[128,256]{1,0:T(8,128)(2,1)S(1)}, u32[]{:S(2)}) copy-start(bf16[128,256]{1,0:T(8,128)(2,1)S(1)} %collective-permute-done.refs_1_) | copy-start | bytes 196612
  39.5 0.7 copy-start.18
  40.2 0.6 copy-start.19
  42.5 11.0 %collective-permute-start.3 = (bf16[256,256]{1,0:T(8,128)(2,1)}, bf16[256,256]{1,0:T(8,128)(2,1)S(1)}, u32[]{:S(2)}, u32[]{:S(2)}) collective-permute-start(bf16[256,256]{1,0:T(8,128)(2,1)} %get-tuple-element.47.refs_0_), channel_id=1, source_target_pairs={{0,16},{16,32},{32,48},{48,0},{1,17},{17,33},{33,49},{49,1},{2,18}... | collective-permute-start | bytes 393224 | tf_op jit(solution)/shard_map/ppermute | solution.py:91
  45.3 12.3 %collective-permute-start.4 = (bf16[256,256]{1,0:T(8,128)(2,1)}, bf16[256,256]{1,0:T(8,128)(2,1)S(1)}, u32[]{:S(2)}, u32[]{:S(2)}) collective-permute-start(bf16[256,256]{1,0:T(8,128)(2,1)} %get-tuple-element.47.refs_0_), channel_id=1, source_target_pairs={{0,32},{16,48},{32,0},{48,16},{1,33},{17,49},{33,1},{49,17},{2,34}... | collective-permute-start | bytes 393224 | tf_op jit(solution)/shard_map/ppermute | solution.py:91
  49.9 7.9 %collective-permute-start.5 = (bf16[256,256]{1,0:T(8,128)(2,1)}, bf16[256,256]{1,0:T(8,128)(2,1)S(1)}, u32[]{:S(2)}, u32[]{:S(2)}) collective-permute-start(bf16[256,256]{1,0:T(8,128)(2,1)} %get-tuple-element.47.refs_0_), channel_id=1, source_target_pairs={{0,48},{16,0},{32,16},{48,32},{1,49},{17,1},{33,17},{49,33},{2,50}... | collective-permute-start | bytes 393224 | tf_op jit(solution)/shard_map/ppermute | solution.py:91
  53.5 4.3 %copy-start.11 = (bf16[256,256]{1,0:T(8,128)(2,1)}, bf16[256,256]{1,0:T(8,128)(2,1)S(1)}, u32[]{:S(2)}) copy-start(bf16[256,256]{1,0:T(8,128)(2,1)S(1)} %collective-permute-done.3.refs_1_) | copy-start | bytes 393220
  57.6 0.7 copy-start.12
  57.8 0.6 copy-start.14
  60.4 21.5 %collective-permute-start.6 = (bf16[1024,256]{1,0:T(8,128)(2,1)}, bf16[1024,256]{1,0:T(8,128)(2,1)}, u32[]{:S(2)}, u32[]{:S(2)}) collective-permute-start(bf16[1024,256]{1,0:T(8,128)(2,1)} %shard_map.121.refs_2_), channel_id=1, source_target_pairs={{0,64},{64,128},{128,192},{192,0},{1,65},{65,129},{129,193},{193,1... | collective-permute-start | bytes 1572872 | tf_op jit(solution)/shard_map/ppermute | solution.py:91
  63.3 18.6 %collective-permute-start.7 = (bf16[1024,256]{1,0:T(8,128)(2,1)}, bf16[1024,256]{1,0:T(8,128)(2,1)}, u32[]{:S(2)}, u32[]{:S(2)}) collective-permute-start(bf16[1024,256]{1,0:T(8,128)(2,1)} %shard_map.121.refs_2_), channel_id=1, source_target_pairs={{0,128},{64,192},{128,0},{192,64},{1,129},{65,193},{129,1},{193,65... | collective-permute-start | bytes 1572872 | tf_op jit(solution)/shard_map/ppermute | solution.py:91
  64.6 18.8 %collective-permute-start.8 = (bf16[1024,256]{1,0:T(8,128)(2,1)}, bf16[1024,256]{1,0:T(8,128)(2,1)}, u32[]{:S(2)}, u32[]{:S(2)}) collective-permute-start(bf16[1024,256]{1,0:T(8,128)(2,1)} %shard_map.121.refs_2_), channel_id=1, source_target_pairs={{0,192},{64,0},{128,64},{192,128},{1,193},{65,1},{129,65},{193,129... | collective-permute-start | bytes 1572872 | tf_op jit(solution)/shard_map/ppermute | solution.py:91
  65.6 7.2 %collective-permute-start.9 = (bf16[256,256]{1,0:T(8,128)(2,1)}, bf16[256,256]{1,0:T(8,128)(2,1)S(1)}, u32[]{:S(2)}, u32[]{:S(2)}) collective-permute-start(bf16[256,256]{1,0:T(8,128)(2,1)} %get-tuple-element.51.refs_0_), channel_id=1, source_target_pairs={{0,16},{16,32},{32,48},{48,0},{1,17},{17,33},{33,49},{49,1},{2,18}... | collective-permute-start | bytes 393224 | tf_op jit(solution)/shard_map/ppermute | solution.py:91
  68.6 8.0 %collective-permute-start.10 = (bf16[256,256]{1,0:T(8,128)(2,1)}, bf16[256,256]{1,0:T(8,128)(2,1)S(1)}, u32[]{:S(2)}, u32[]{:S(2)}) collective-permute-start(bf16[256,256]{1,0:T(8,128)(2,1)} %get-tuple-element.51.refs_0_), channel_id=1, source_target_pairs={{0,32},{16,48},{32,0},{48,16},{1,33},{17,49},{33,1},{49,17},{2,34}... | collective-permute-start | bytes 393224 | tf_op jit(solution)/shard_map/ppermute | solution.py:91
  72.8 6.5 %copy-start.13 = (bf16[256,256]{1,0:T(8,128)(2,1)}, bf16[256,256]{1,0:T(8,128)(2,1)S(1)}, u32[]{:S(2)}) copy-start(bf16[256,256]{1,0:T(8,128)(2,1)S(1)} %collective-permute-done.9.refs_1_) | copy-start | bytes 393220
  72.8 6.5 %collective-permute-start.11 = (bf16[256,256]{1,0:T(8,128)(2,1)}, bf16[256,256]{1,0:T(8,128)(2,1)S(1)}, u32[]{:S(2)}, u32[]{:S(2)}) collective-permute-start(bf16[256,256]{1,0:T(8,128)(2,1)} %get-tuple-element.51.refs_0_), channel_id=1, source_target_pairs={{0,48},{16,0},{32,16},{48,32},{1,49},{17,1},{33,17},{49,33},{2,50}... | collective-permute-start | bytes 393224 | tf_op jit(solution)/shard_map/ppermute | solution.py:91
  76.6 2.7 %copy-start.15 = (bf16[256,256]{1,0:T(8,128)(2,1)}, bf16[256,256]{1,0:T(8,128)(2,1)S(1)}, u32[]{:S(2)}) copy-start(bf16[256,256]{1,0:T(8,128)(2,1)S(1)} %collective-permute-done.10.refs_2_) | copy-start | bytes 393220
  79.3 0.7 copy-start.16
  83.4 1.0 copy-start.6
  84.5 35.6 %copy-start.3 = (f32[2,64,256]{2,1,0:T(8,128)S(1)}, f32[2,64,256]{2,1,0:T(8,128)}, u32[]{:S(2)}) copy-start(f32[2,64,256]{2,1,0:T(8,128)} %constant.39.clone.turn) | copy-start | bytes 393220
  84.5 35.6 %copy-start.4 = (bf16[128,64]{1,0:T(8,128)(2,1)S(1)}, bf16[128,64]{1,0:T(8,128)(2,1)}, u32[]{:S(2)}) copy-start(bf16[128,64]{1,0:T(8,128)(2,1)} %constant.37.clone.first) | copy-start | bytes 49156
  84.5 35.6 %copy-start.5 = (bf16[64,128]{1,0:T(8,128)(2,1)S(1)}, bf16[64,128]{1,0:T(8,128)(2,1)}, u32[]{:S(2)}) copy-start(bf16[64,128]{1,0:T(8,128)(2,1)} %constant.38.clone.last) | copy-start | bytes 49156
  93.4 0.6 copy-start.1
  94.0 25.3 %all-to-all-start.1 = ((bf16[16,4,16,256]{3,2,1,0:T(8,128)(2,1)}), bf16[16,4,16,256]{3,2,1,0:T(8,128)(2,1)S(1)}, u32[]{:S(2)}, u32[]{:S(2)}) async-start(bf16[16,4,16,256]{3,2,1,0:T(8,128)(2,1)} %get-tuple-element.56), calls=%async_computation.1 | async-start | bytes 1048576 | tf_op jit(solution)/shard_map/all_to_all | solution.py:365
  104.6 10.5 %collective-permute-start.12 = (bf16[256,256]{1,0:T(8,128)(2,1)S(1)}, bf16[256,256]{1,0:T(8,128)(2,1)S(1)}, u32[]{:S(2)}, u32[]{:S(2)}) collective-permute-start(bf16[256,256]{1,0:T(8,128)(2,1)S(1)} %get-tuple-element.58), channel_id=1, source_target_pairs={{0,4},{4,8},{8,12},{12,0},{1,5},{5,9},{9,13},{13,1},{2,6},{6,10},{... | collective-permute-start | bytes 393224 | tf_op jit(solution)/shard_map/ppermute | solution.py:337
  110.1 8.6 %collective-permute-start.13 = (bf16[256,256]{1,0:T(8,128)(2,1)S(1)}, bf16[256,256]{1,0:T(8,128)(2,1)S(1)}, u32[]{:S(2)}, u32[]{:S(2)}) collective-permute-start(bf16[256,256]{1,0:T(8,128)(2,1)S(1)} %get-tuple-element.59), channel_id=1, source_target_pairs={{0,8},{4,12},{8,0},{12,4},{1,9},{5,13},{9,1},{13,5},{2,10},{6,14},... | collective-permute-start | bytes 393224 | tf_op jit(solution)/shard_map/ppermute | solution.py:337
  113.1 6.3 %collective-permute-start.14 = (bf16[256,256]{1,0:T(8,128)(2,1)S(1)}, bf16[256,256]{1,0:T(8,128)(2,1)}, u32[]{:S(2)}, u32[]{:S(2)}) collective-permute-start(bf16[256,256]{1,0:T(8,128)(2,1)S(1)} %get-tuple-element.60), channel_id=1, source_target_pairs={{0,12},{4,0},{8,4},{12,8},{1,13},{5,1},{9,5},{13,9},{2,14},{6,2},{... | collective-permute-start | bytes 393224 | tf_op jit(solution)/shard_map/ppermute | solution.py:337
  115.1 3.6 %copy-start.9 = (bf16[256,256]{1,0:T(8,128)(2,1)}, bf16[256,256]{1,0:T(8,128)(2,1)S(1)}, u32[]{:S(2)}) copy-start(bf16[256,256]{1,0:T(8,128)(2,1)S(1)} %collective-permute-done.12.refs_1_) | copy-start | bytes 393220
  118.7 0.7 copy-start.10
  119.4 0.8 copy-start.7
  126.5 35.5 %all-to-all-start.2 = ((bf16[64,16,256]{2,1,0:T(8,128)(2,1)}), bf16[64,16,256]{2,1,0:T(8,128)(2,1)S(1)}, u32[]{:S(2)}, u32[]{:S(2)}) async-start(bf16[64,16,256]{2,1,0:T(8,128)(2,1)} %bitcast.10), calls=%async_computation.2 | async-start | bytes 1048576 | tf_op jit(solution)/shard_map/all_to_all | solution.py:370
  141.1 13.3 %copy-start.20 = (f32[1024]{0:T(1024)S(1)}, f32[1024]{0:T(1024)}, u32[]{:S(2)}) copy-start(f32[1024]{0:T(1024)} %param.16) | copy-start | bytes 12292
  149.1 0.7 copy-start.2
  149.8 8.2 %collective-permute-start.15 = (bf16[256,256]{1,0:T(8,128)(2,1)S(1)}, bf16[256,256]{1,0:T(8,128)(2,1)}, u32[]{:S(2)}, u32[]{:S(2)}) collective-permute-start(bf16[256,256]{1,0:T(8,128)(2,1)S(1)} %get-tuple-element.69), channel_id=1, source_target_pairs={{0,4},{4,8},{8,12},{12,0},{1,5},{5,9},{9,13},{13,1},{2,6},{6,10},{... | collective-permute-start | bytes 393224 | tf_op jit(solution)/shard_map/ppermute | solution.py:337
  150.8 11.2 %collective-permute-start.16 = (bf16[256,256]{1,0:T(8,128)(2,1)S(1)}, bf16[256,256]{1,0:T(8,128)(2,1)}, u32[]{:S(2)}, u32[]{:S(2)}) collective-permute-start(bf16[256,256]{1,0:T(8,128)(2,1)S(1)} %get-tuple-element.70), channel_id=1, source_target_pairs={{0,8},{4,12},{8,0},{12,4},{1,9},{5,13},{9,1},{13,5},{2,10},{6,14},... | collective-permute-start | bytes 393224 | tf_op jit(solution)/shard_map/ppermute | solution.py:337
  153.2 8.8 %collective-permute-start.17 = (bf16[256,256]{1,0:T(8,128)(2,1)S(1)}, bf16[256,256]{1,0:T(8,128)(2,1)}, u32[]{:S(2)}, u32[]{:S(2)}) collective-permute-start(bf16[256,256]{1,0:T(8,128)(2,1)S(1)} %get-tuple-element.71), channel_id=1, source_target_pairs={{0,12},{4,0},{8,4},{12,8},{1,13},{5,1},{9,5},{13,9},{2,14},{6,2},{... | collective-permute-start | bytes 393224 | tf_op jit(solution)/shard_map/ppermute | solution.py:337
  162.0 0.8 copy-start.8
  166.2 4.0 %collective-permute-start.18 = (bf16[256,1024]{1,0:T(8,128)(2,1)S(1)}, bf16[256,1024]{1,0:T(8,128)(2,1)S(1)}, u32[]{:S(2)}, u32[]{:S(2)}) collective-permute-start(bf16[256,1024]{1,0:T(8,128)(2,1)S(1)} %get-tuple-element.73), channel_id=1, source_target_pairs={{0,1},{1,0},{2,3},{3,2},{4,5},{5,4},{6,7},{7,6},{8,9},{9,8},{10,11... | collective-permute-start | bytes 1572872 | tf_op jit(solution)/shard_map/ppermute | solution.py:376
  170.3 13.6 %collective-permute-start.20 = (bf16[256,1024]{1,0:T(8,128)(2,1)S(1)}, bf16[256,1024]{1,0:T(8,128)(2,1)S(1)}, u32[]{:S(2)}, u32[]{:S(2)}) collective-permute-start(bf16[256,1024]{1,0:T(8,128)(2,1)S(1)} %add_convert_fusion.1), channel_id=1, source_target_pairs={{0,2},{2,0},{1,3},{3,1},{4,6},{6,4},{5,7},{7,5},{8,10},{10,8},{9,1... | collective-permute-start | bytes 1572872 | tf_op jit(solution)/shard_map/ppermute | solution.py:379
  174.0 9.9 %collective-permute-start.19 = (bf16[256,1024]{1,0:T(8,128)(2,1)S(1)}, bf16[256,1024]{1,0:T(8,128)(2,1)S(1)}, u32[]{:S(2)}, u32[]{:S(2)}) collective-permute-start(bf16[256,1024]{1,0:T(8,128)(2,1)S(1)} %get-tuple-element.76), channel_id=1, source_target_pairs={{0,1},{1,0},{2,3},{3,2},{4,5},{5,4},{6,7},{7,6},{8,9},{9,8},{10,11... | collective-permute-start | bytes 1572872 | tf_op jit(solution)/shard_map/ppermute | solution.py:382
Sparse Core Ops, SparseCore 0:
  10.4 68.1 all-gather.2
  83.5 45.9 all-gather.4

commit v3 on v2

--- a/solution.py
+++ b/solution.py
@@ -31,6 +31,10 @@
     return [pltpu.with_memory_space_constraint(a, pltpu.HBM) for a in arrays]
 
 
+def in_vmem(arrays):
+    return [pltpu.with_memory_space_constraint(a, pltpu.VMEM) for a in arrays]
+
+
 def turn_kernel(source, out):
     for part in range(4):
         block = source[:, part * 256 : (part + 1) * 256].astype(F32).T
@@ -84,59 +88,90 @@
         out_shape=(one,) * count,
         in_specs=[pl.BlockSpec(memory_space=pltpu.SMEM)] + [inside] * 4,
         out_specs=(inside,) * count,
-    )(own.reshape(1), *pieces)
+    )(own.reshape(1), *in_vmem(pieces))
 
 
 def to_all(block, axis):
     return [lax.ppermute(block, axis, shift(step)) if step else block for step in range(4)]
 
 
-def project_kernel(whole, at_ref, act_ref, *refs):
-    a_buf, w_buf, sems = refs[-3:]
-    outs = refs[-8:-3] if whole else refs[-7:-3]
-    w_refs = refs[: len(refs) - 3 - len(outs)]
-    rows, block = a_buf.shape[1], w_buf.shape[0] // len(w_refs)
-    own_y, own_x = at_ref[0], at_ref[1]
+def sum_kernel(steps, at_ref, act_ref, *refs):
+    w_refs, (total, a_buf, w_buf, sems) = refs[: len(steps)], refs[len(steps) :]
+    depth = w_buf.shape[1]
     copies = []
-    for step, source in enumerate(w_refs):
-        row = pl.multiple_of(lax.rem(own_y + 4 - step, 4) * block, 16)
-        copies.append((source, w_buf.at[pl.ds(row, block)]))
-    parts = [lax.rem(own_x + step, 4) for step in range(4)]
-    for step, part in enumerate(parts):
-        row = pl.multiple_of(part * rows, 16)
-        copies.append((act_ref.at[pl.ds(row, rows)], a_buf.at[step]))
-    copies = [
-        pltpu.make_async_copy(src, dst, sems.at[at]) for at, (src, dst) in enumerate(copies)
-    ]
-    for copy in copies:
-        copy.start()
-    for copy in copies[: len(w_refs)]:
-        copy.wait()
-    for step, part in enumerate(parts):
-        copies[len(w_refs) + step].wait()
-        prod = jnp.dot(a_buf[step], w_buf[...], preferred_element_type=F32).T.astype(BF16)
-        outs[step][...] = prod
-        if whole:
-            outs[4][:, part] = prod.reshape(16, 16, rows)
-
-
-def project(at, act, weights, whole):
-    rows, depth = act.shape[0] // 4, act.shape[1]
+    for at, step in enumerate(steps):
+        first = pl.multiple_of(lax.rem(at_ref[0] + 4 - step, 4) * depth, depth)
+        pair = (w_refs[at], act_ref.at[:, pl.ds(first, depth)])
+        copies.append(fetch(pair, (w_buf.at[at], a_buf.at[at]), sems.at[at]))
+    for at, pair in enumerate(copies):
+        for copy in pair:
+            copy.wait()
+        prod = jnp.dot(a_buf[at], w_buf[at], preferred_element_type=F32)
+        total[...] = prod if at == 0 else total[...] + prod
+
+
+def part_sum(at, act, weights, steps):
+    rows, depth = act.shape[0], act.shape[1] // 4
     cols = weights[0].shape[1]
-    count = len(weights) + 4
-    shapes = [(cols, rows)] * 4 + [(16, 4, cols // 16, rows)] * whole
-    return pl.pallas_call(
-        lambda *refs: project_kernel(whole, *refs),
-        out_shape=[jax.ShapeDtypeStruct(shape, BF16) for shape in shapes],
-        in_specs=[SCALARS] + [OUTSIDE] * (len(weights) + 1),
-        out_specs=[INSIDE] * len(shapes),
+    return pl.pallas_call(
+        lambda *refs: sum_kernel(steps, *refs),
+        out_shape=jax.ShapeDtypeStruct((rows, cols), F32),
+        in_specs=[SCALARS] + [OUTSIDE] * (len(steps) + 1),
+        out_specs=INSIDE,
         scratch_shapes=[
-            pltpu.VMEM((4, rows, depth), BF16),
-            pltpu.VMEM((depth, cols), BF16),
-            pltpu.SemaphoreType.DMA((count,)),
+            pltpu.VMEM((len(steps), rows, depth), BF16),
+            pltpu.VMEM((len(steps), depth, cols), BF16),
+            pltpu.SemaphoreType.DMA((len(steps), 2)),
         ],
         compiler_params=pltpu.CompilerParams(vmem_limit_bytes=40 * 1024 * 1024),
     )(at, *in_hbm([act, *weights]))
+
+
+def finish_kernel(steps, whole, at_ref, act_ref, w_ref, *refs):
+    a_buf, w_buf, total, sems = refs[-4:]
+    outs = refs[-9:-4] if whole else refs[-8:-4]
+    depth, rows = w_buf.shape[1], total.shape[0] // 4
+    own_y, own_x = at_ref[0], at_ref[1]
+    copies = []
+    for at, step in enumerate(steps):
+        first = pl.multiple_of(lax.rem(own_y + 4 - step, 4) * depth, depth)
+        source = w_ref if len(steps) == 1 else w_ref.at[pl.ds(first, depth)]
+        pair = (source, act_ref.at[:, pl.ds(first, depth)])
+        copies.append(fetch(pair, (w_buf.at[at], a_buf.at[at]), sems.at[at]))
+    has_sum = len(refs) > len(outs) + 4
+    if has_sum:
+        copies[0] += fetch(refs[:1], (total,), sems.at[len(steps)])
+    for at, pair in enumerate(copies):
+        for copy in pair:
+            copy.wait()
+        prod = jnp.dot(a_buf[at], w_buf[at], preferred_element_type=F32)
+        total[...] = total[...] + prod if at or has_sum else prod
+    for step in range(4):
+        part = lax.rem(own_x + step, 4)
+        row = pl.multiple_of(part * rows, 8)
+        block = total[pl.ds(row, rows), :].T.astype(BF16)
+        outs[step][...] = block
+        if whole:
+            outs[4][:, part] = block.reshape(16, 16, rows)
+
+
+def project(at, act, weight, steps, before, whole):
+    rows, depth = act.shape[0] // 4, act.shape[1] // 4
+    cols = weight.shape[1]
+    shapes = [(cols, rows)] * 4 + [(16, 4, cols // 16, rows)] * whole
+    return pl.pallas_call(
+        lambda *refs: finish_kernel(steps, whole, *refs),
+        out_shape=[jax.ShapeDtypeStruct(shape, BF16) for shape in shapes],
+        in_specs=[SCALARS] + [OUTSIDE] * (2 + len(before)),
+        out_specs=[INSIDE] * len(shapes),
+        scratch_shapes=[
+            pltpu.VMEM((len(steps), 4 * rows, depth), BF16),
+            pltpu.VMEM((len(steps), depth, cols), BF16),
+            pltpu.VMEM((4 * rows, cols), F32),
+            pltpu.SemaphoreType.DMA((len(steps) + 1, 2)),
+        ],
+        compiler_params=pltpu.CompilerParams(vmem_limit_bytes=40 * 1024 * 1024),
+    )(at, *in_hbm([act, weight, *before]))
 
 
 def fetch(sources, buffers, sems):
@@ -154,20 +189,22 @@
     return pltpu.make_async_copy(weight_ref.at[:, pl.ds(col, w_buf.shape[1])], w_buf, sem)
 
 
-def mix_kernel(at_ref, skip_ref, conv_hbm, *refs):
-    sources, weight_ref = (conv_hbm,) + refs[:8], refs[8]
-    home_ref, give_ref, conv_buf, vg_buf, w_buf, sem, sems = refs[9:]
+def mix_kernel(at_ref, skip_ref, weight_ref, conv_ref, value_ref, gate_ref, *refs):
+    sources, (home_ref, give_ref, w_buf, sem, vg_buf, sems) = refs[:6], refs[6:]
+    pieces = [vg_buf.at[at] for at in range(6)]
+    others = fetch(sources, pieces, sems)
+    values, gates = [value_ref] + pieces[:3], [gate_ref] + pieces[3:]
     own_x, own_c, own_z = at_ref[1], at_ref[2], at_ref[3]
-    copies = fetch(sources, [conv_buf] + [vg_buf.at[at] for at in range(8)], sems)
     copy = column_block(weight_ref, 2 * (1 - own_z) + 1 - own_c, w_buf, sem)
     copy.start()
     rows = home_ref.shape[0]
-    for other in copies:
-        other.wait()
     for step in range(4):
+        if step == 1:
+            for other in others:
+                other.wait()
         src = lax.rem(own_x + 4 - step, 4)
-        conv = conv_buf[:, src].astype(F32).reshape(256, rows)
-        value, gate = vg_buf[step].astype(F32), vg_buf[4 + step].astype(F32)
+        conv = conv_ref[:, src].astype(F32).reshape(256, rows)
+        value, gate = values[step][...].astype(F32), gates[step][...].astype(F32)
         mixed = gate * (conv + skip_ref[src] * value)
         col = pl.multiple_of(src * 256, 128)
         home_ref[:, pl.ds(col, 256)] = mixed.T.astype(BF16)
@@ -181,17 +218,22 @@
     return pl.pallas_call(
         mix_kernel,
         out_shape=(one, one),
-        in_specs=[SCALARS, INSIDE] + [OUTSIDE] * 10,
+        in_specs=[SCALARS, INSIDE, OUTSIDE] + [INSIDE] * 3 + [OUTSIDE] * 6,
         out_specs=(INSIDE, INSIDE),
         scratch_shapes=[
-            pltpu.VMEM(conv.shape, BF16),
-            pltpu.VMEM((8, 256, rows), BF16),
             pltpu.VMEM((1024, 1024), BF16),
             pltpu.SemaphoreType.DMA,
-            pltpu.SemaphoreType.DMA((9,)),
+            pltpu.VMEM((6, 256, rows), BF16),
+            pltpu.SemaphoreType.DMA((6,)),
         ],
         compiler_params=pltpu.CompilerParams(vmem_limit_bytes=32 * 1024 * 1024),
-    )(at, skip, *in_hbm([conv, *values, *gates, weight]))
+    )(
+        at,
+        skip,
+        *in_hbm([weight]),
+        *in_vmem([conv, values[0], gates[0]]),
+        *in_hbm([*values[1:], *gates[1:]]),
+    )
 
 
 def away_kernel(at_ref, home_ref, weight_ref, away_ref, w_buf, sem):
@@ -267,12 +309,9 @@
     return jnp.dot(left, right, preferred_element_type=F32)
 
 
-def filter_kernel(first, last, turn, *refs):
-    sources, out_ref, x_buf, h_buf = refs[:4], refs[4], refs[5], refs[6]
-    buffers, sems = refs[7:11], refs[11]
-    slab_ref, resp_ref, ahead, back = buffers
-    for copy in fetch(sources, buffers, sems):
-        copy.wait()
+def filter_kernel(first, last, turn, slab_ref, resp_ref, *refs):
+    sources, (out_ref, x_buf, h_buf, ahead, back, sems) = refs[:2], refs[2:]
+    copies = fetch(sources, (ahead, back), sems)
     rows = slab_ref.shape[1]
     for ref, buf in ((slab_ref, x_buf), (resp_ref, h_buf)):
         for part in range(buf.shape[0]):
@@ -282,6 +321,8 @@
         return jnp.concatenate([buf[part, pick, :] for part in range(buf.shape[0])], axis=1)
 
     t_cos, t_sin = turn[0], turn[1]
+    for copy in copies:
+        copy.wait()
     group = 4
     for start in range(0, 16, group):
         picks = [pl.ds(start + at, 64, stride=16) for at in range(group)]
@@ -318,19 +359,17 @@
     return pl.pallas_call(
         filter_kernel,
         out_shape=jax.ShapeDtypeStruct((count, rows), BF16),
-        in_specs=[INSIDE] * 3 + [OUTSIDE] * 4,
+        in_specs=[INSIDE] * 5 + [OUTSIDE] * 2,
         out_specs=INSIDE,
         scratch_shapes=[
             pltpu.VMEM((rows // 128, count, 128), F32),
             pltpu.VMEM((2 * rows // 128, count, 128), F32),
-            pltpu.VMEM((count, rows), BF16),
-            pltpu.VMEM((count, 2 * rows), BF16),
             pltpu.VMEM((2 * rows, 2 * rows), BF16),
             pltpu.VMEM((2 * rows, 2 * rows), BF16),
-            pltpu.SemaphoreType.DMA((4,)),
+            pltpu.SemaphoreType.DMA((2,)),
         ],
         compiler_params=pltpu.CompilerParams(vmem_limit_bytes=32 * 1024 * 1024),
-    )(first, last, turn, *in_hbm([slabs, resp, ahead, back]))
+    )(first, last, turn, *in_vmem([slabs, resp]), *in_hbm([ahead, back]))
 
 
 def along_x(pieces):
@@ -359,16 +398,17 @@
     w_y, g_x = tie(w_y, g_x)
     w_all = to_all(w_y, "y")
     (g_y,) = place(my_zh, to_all(g_x, "zh"), 1)
-    *w_all, resp, g_y = tie(*w_all, resp, g_y)
+    here = part_sum(at, act, [w_all[0], w_all[1], w_all[3]], (0, 1, 3))
+    w_far, resp, g_y, here = tie(w_all[2], resp, g_y, here)
     g_all = lax.all_gather(g_y, "y", axis=0, tiled=True)
-    *values, value = project(at, act, w_all, True)
+    *values, value = project(at, act, w_far, (2,), [here], True)
     slabs = lax.all_to_all(value, SLABS, 0, 0, tiled=True)
     values = along_x(values)
     slabs, *values = tie(slabs, *values)
     conv = filtered(slabs.reshape(1024, rows), resp.reshape(1024, 2 * rows))
     conv = conv.reshape(64, 16, rows)
     conv = lax.all_to_all(conv, SEQ, 0, 0, tiled=True).reshape(16, 4, 16, rows)
-    gates = along_x(project(at * jnp.array([0, 1, 0, 0], jnp.int32), act, [g_all], False))
+    gates = along_x(project(at, act, g_all, (0, 1, 2, 3), [], False))
 
     home, give = mix_and_give(
         at, conv, values, gates, skip_weight.reshape(4, 256, 1), output_proj

time: 192 us -> 186 us (0.969)
  starting transfers between devices: 85.2 us -> 78.8 us
  waiting for transfers between devices: 40.9 us -> 43.6 us
    all_to_all x1, starting transfers between devices: 14.6 us -> 7.5 us  [body(): conv = lax.all_to_all(conv, SEQ, 0, 0, tiled=True).reshape(16, 4, 16, rows)]
    ppermute x6, waiting for transfers between devices: 12.6 us -> 7.18 us  [along_x(): lax.ppermute(p, 'x', shift(step))]
    all_to_all x1, waiting for transfers between devices: 0.01 us -> 4.81 us  [body(): slabs = lax.all_to_all(value, SLABS, 0, 0, tiled=True)]
    ppermute x6, starting transfers between devices: 13.4 us -> 8.91 us  [along_x(): lax.ppermute(p, 'x', shift(step))]
    ppermute x1, starting transfers between devices: 1.1 us -> 5.07 us  [body(): got = lax.ppermute(give, 'c', SWAP)]
    pallas_call x3, Pallas kernels: 5.53 us -> 2.42 us  [place(): pl.pallas_call(place_kernel, out_shape=(one,) * count, in_specs=[pl.Block...]
    all_gather x1, waiting for transfers between devices: 0.02 us -> 2.8 us  [body(): g_all = lax.all_gather(g_y, 'y', axis=0, tiled=True)]
    ppermute x1, starting transfers between devices: 0.09 us -> 2.74 us  [body(): back = lax.ppermute(away, 'zl', SWAP)]
  transfers between devices with their start and end apart: 26 -> 26, of which waited for: 14 -> 15; matrix products, arithmetic and copies ran while one was open for 0% -> 0% of each run, Pallas kernels for 19% -> 19%
where the time goes in v3:
time: 186 us; the launch traced here: 185 us
  starting transfers between devices  78.8 us (42%)
  waiting for transfers between devices  43.6 us (23%)
  Pallas kernels  41.3 us (22%)
  between operations  13.6 us (7%)
  local copies, waits for them, and re-layouts  6.57 us (4%)
    ppermute x9, starting transfers between devices, to_all(): lax.ppermute(block, axis, shift(step))  25.4 us
    all_to_all x1, starting transfers between devices, body(): resp = lax.all_to_all(resp.reshape(64, 16, 2 * rows), SEQ, 0, 0, tiled=True)  15.4 us
    pallas_call x2, Pallas kernels, project(): pl.pallas_call(lambda *refs: finish_kernel(steps, whole, *refs), out_shap...  12.3 us
    ppermute x9, waiting for transfers between devices, to_all(): lax.ppermute(block, axis, shift(step))  12.2 us
    ppermute x6, starting transfers between devices, along_x(): lax.ppermute(p, 'x', shift(step))  8.91 us
    all_to_all x1, starting transfers between devices, body(): slabs = lax.all_to_all(value, SLABS, 0, 0, tiled=True)  8.75 us
    ppermute x1, waiting for transfers between devices, body(): back = lax.ppermute(away, 'zl', SWAP)  8.31 us
    ppermute x3, waiting for transfers between devices, body(): lax.ppermute(p, 'x', shift(step))  8.22 us
  transfers between devices with their start and end apart: 26, of which 15 were waited for; matrix products, arithmetic and copies ran while one was open for 0% of the time, Pallas kernels for 19%

profile of v3, /device:TPU:1, one launch (start us, length us, event | category | flops | bytes accessed | tf_op | source)
XLA Modules:
  0.0 185.0 jit_solution(12250999443624043600)
XLA Ops:
  6.5 2.7 %shard_map.109 = bf16[16,4,16,512]{3,2,1,0:T(8,128)(2,1)} custom-call(bf16[512,1024]{1,0:T(8,128)(2,1)} %bitcast.14), custom_call_target="tpu_custom_call" | custom-call | tf_op jit(solution)/shard_map/pallas_call | solution.py:46
  9.2 1.1 constant_dynamic-slice_fusion
  10.3 0.0 all-gather.3.cloned.1.call-update
  10.3 15.4 %all-to-all-start = ((bf16[64,16,512]{2,1,0:T(8,128)(2,1)}), bf16[64,16,512]{2,1,0:T(8,128)(2,1)}, u32[]{:S(2)}, u32[]{:S(2)}) async-start(bf16[64,16,512]{2,1,0:T(8,128)(2,1)} %bitcast.7), calls=%async_computation | async-start | bytes 2097152 | tf_op jit(solution)/shard_map/all_to_all | solution.py:387
  25.7 0.0 all-gather.5.cloned.1.call-start
  25.8 1.8 shard_map.110
  27.5 0.9 collective-permute-start
  28.5 2.4 %collective-permute-start.1 = (bf16[128,256]{1,0:T(8,128)(2,1)}, bf16[128,256]{1,0:T(8,128)(2,1)S(1)}, u32[]{:S(2)}, u32[]{:S(2)}) collective-permute-start(bf16[128,256]{1,0:T(8,128)(2,1)} %get-tuple-element.43), channel_id=1, source_target_pairs={{0,8},{4,12},{8,0},{12,4},{1,9},{5,13},{9,1},{13,5},{2,10},{6,14},... | collective-permute-start | bytes 196616 | tf_op jit(solution)/shard_map/ppermute | solution.py:390
  30.9 1.2 collective-permute-start.2
  32.1 4.3 %collective-permute-done.refs_1_ = bf16[128,256]{1,0:T(8,128)(2,1)S(1)} collective-permute-done((bf16[128,256]{1,0:T(8,128)(2,1)}, bf16[128,256]{1,0:T(8,128)(2,1)S(1)}, u32[]{:S(2)}, u32[]{:S(2)}) %collective-permute-start) | collective-permute-done | bytes 65568 | tf_op jit(solution)/shard_map/ppermute | solution.py:390
  36.4 3.5 %collective-permute-done.1.refs_2_ = bf16[128,256]{1,0:T(8,128)(2,1)S(1)} collective-permute-done((bf16[128,256]{1,0:T(8,128)(2,1)}, bf16[128,256]{1,0:T(8,128)(2,1)S(1)}, u32[]{:S(2)}, u32[]{:S(2)}) %collective-permute-start.1) | collective-permute-done | bytes 65568 | tf_op jit(solution)/shard_map/ppermute | solution.py:390
  39.9 0.3 collective-permute-done.2.refs_3_
  40.3 0.8 copy-done.5
  41.1 0.7 shard_map.111
  41.9 2.8 %collective-permute-start.3 = (bf16[256,256]{1,0:T(8,128)(2,1)}, bf16[256,256]{1,0:T(8,128)(2,1)S(1)}, u32[]{:S(2)}, u32[]{:S(2)}) collective-permute-start(bf16[256,256]{1,0:T(8,128)(2,1)} %get-tuple-element.45.refs_0_), channel_id=1, source_target_pairs={{0,16},{16,32},{32,48},{48,0},{1,17},{17,33},{33,49},{49,1},{2,18}... | collective-permute-start | bytes 393224 | tf_op jit(solution)/shard_map/ppermute | solution.py:95
  44.7 4.6 %collective-permute-start.4 = (bf16[256,256]{1,0:T(8,128)(2,1)}, bf16[256,256]{1,0:T(8,128)(2,1)S(1)}, u32[]{:S(2)}, u32[]{:S(2)}) collective-permute-start(bf16[256,256]{1,0:T(8,128)(2,1)} %get-tuple-element.45.refs_0_), channel_id=1, source_target_pairs={{0,32},{16,48},{32,0},{48,16},{1,33},{17,49},{33,1},{49,17},{2,34}... | collective-permute-start | bytes 393224 | tf_op jit(solution)/shard_map/ppermute | solution.py:95
  49.3 3.6 %collective-permute-start.5 = (bf16[256,256]{1,0:T(8,128)(2,1)}, bf16[256,256]{1,0:T(8,128)(2,1)S(1)}, u32[]{:S(2)}, u32[]{:S(2)}) collective-permute-start(bf16[256,256]{1,0:T(8,128)(2,1)} %get-tuple-element.45.refs_0_), channel_id=1, source_target_pairs={{0,48},{16,0},{32,16},{48,32},{1,49},{17,1},{33,17},{49,33},{2,50}... | collective-permute-start | bytes 393224 | tf_op jit(solution)/shard_map/ppermute | solution.py:95
  52.9 0.1 collective-permute-done.3.refs_1_
  52.9 5.3 %collective-permute-done.4.refs_2_ = bf16[256,256]{1,0:T(8,128)(2,1)S(1)} collective-permute-done((bf16[256,256]{1,0:T(8,128)(2,1)}, bf16[256,256]{1,0:T(8,128)(2,1)S(1)}, u32[]{:S(2)}, u32[]{:S(2)}) %collective-permute-start.4) | collective-permute-done | bytes 131104 | tf_op jit(solution)/shard_map/ppermute | solution.py:95
  58.2 0.9 copy-done.4
  59.1 0.8 shard_map.112.refs_2_
  60.0 3.0 %collective-permute-start.10 = (bf16[1024,256]{1,0:T(8,128)(2,1)}, bf16[1024,256]{1,0:T(8,128)(2,1)}, u32[]{:S(2)}, u32[]{:S(2)}) collective-permute-start(bf16[1024,256]{1,0:T(8,128)(2,1)} %shard_map.112.refs_2_), channel_id=1, source_target_pairs={{0,64},{64,128},{128,192},{192,0},{1,65},{65,129},{129,193},{193,1... | collective-permute-start | bytes 1572872 | tf_op jit(solution)/shard_map/ppermute | solution.py:95
  63.0 0.3 collective-permute-start.11
  63.3 2.0 %collective-permute-start.6 = (bf16[1024,256]{1,0:T(8,128)(2,1)}, bf16[1024,256]{1,0:T(8,128)(2,1)S(1)}, u32[]{:S(2)}, u32[]{:S(2)}) collective-permute-start(bf16[1024,256]{1,0:T(8,128)(2,1)} %shard_map.112.refs_2_), channel_id=1, source_target_pairs={{0,128},{64,192},{128,0},{192,64},{1,129},{65,193},{129,1},{193,65... | collective-permute-start | bytes 1572872 | tf_op jit(solution)/shard_map/ppermute | solution.py:95
  65.3 2.7 %collective-permute-start.7 = (bf16[256,256]{1,0:T(8,128)(2,1)}, bf16[256,256]{1,0:T(8,128)(2,1)S(1)}, u32[]{:S(2)}, u32[]{:S(2)}) collective-permute-start(bf16[256,256]{1,0:T(8,128)(2,1)} %get-tuple-element.49.refs_0_), channel_id=1, source_target_pairs={{0,16},{16,32},{32,48},{48,0},{1,17},{17,33},{33,49},{49,1},{2,18}... | collective-permute-start | bytes 393224 | tf_op jit(solution)/shard_map/ppermute | solution.py:95
  68.0 3.7 %collective-permute-start.8 = (bf16[256,256]{1,0:T(8,128)(2,1)}, bf16[256,256]{1,0:T(8,128)(2,1)S(1)}, u32[]{:S(2)}, u32[]{:S(2)}) collective-permute-start(bf16[256,256]{1,0:T(8,128)(2,1)} %get-tuple-element.49.refs_0_), channel_id=1, source_target_pairs={{0,32},{16,48},{32,0},{48,16},{1,33},{17,49},{33,1},{49,17},{2,34}... | collective-permute-start | bytes 393224 | tf_op jit(solution)/shard_map/ppermute | solution.py:95
  71.7 0.5 collective-permute-done.7.refs_1_
  72.2 2.7 %collective-permute-start.9 = (bf16[256,256]{1,0:T(8,128)(2,1)}, bf16[256,256]{1,0:T(8,128)(2,1)S(1)}, u32[]{:S(2)}, u32[]{:S(2)}) collective-permute-start(bf16[256,256]{1,0:T(8,128)(2,1)} %get-tuple-element.49.refs_0_), channel_id=1, source_target_pairs={{0,48},{16,0},{32,16},{48,32},{1,49},{17,1},{33,17},{49,33},{2,50}... | collective-permute-start | bytes 393224 | tf_op jit(solution)/shard_map/ppermute | solution.py:95
  74.9 0.1 pad_add_fusion.refs_0_.at_ref
  75.0 1.0 collective-permute-done.8.refs_2_
  76.0 5.3 %collective-permute-done.9.refs_3_ = bf16[256,256]{1,0:T(8,128)(2,1)S(1)} collective-permute-done((bf16[256,256]{1,0:T(8,128)(2,1)}, bf16[256,256]{1,0:T(8,128)(2,1)S(1)}, u32[]{:S(2)}, u32[]{:S(2)}) %collective-permute-start.9) | collective-permute-done | bytes 131104 | tf_op jit(solution)/shard_map/ppermute | solution.py:95
  81.4 0.9 copy-done.3
  82.3 0.8 shard_map.113
  83.1 5.4 %shard_map.114.refs_3_ = f32[1024,256]{1,0:T(8,128)S(1)} custom-call(s32[4]{0:T(128)S(1)} %pad_add_fusion.refs_0_.at_ref, bf16[1024,4096]{1,0:T(8,128)(2,1)} %all-gather.3.cloned.1.call-done.refs_1_, bf16[1024,256]{1,0:T(8,128)(2,1)} %shard_map.112.refs_2_, bf16[1024,256]{1,0:T(8,128)(2,1)} %collective-permute-done.10.refs_3_, ...), custom_call_target="tpu_custom_call" | custom-call | tf_op jit(solution)/shard_map/pallas_call | solution.py:116
  88.5 1.0 copy-done.1
  89.6 0.8 copy-done.8
  90.4 4.4 %shard_map.115 = (bf16[256,256]{1,0:T(8,128)(2,1)S(1)}, bf16[256,256]{1,0:T(8,128)(2,1)S(1)}, bf16[256,256]{1,0:T(8,128)(2,1)S(1)}, bf16[256,256]{1,0:T(8,128)(2,1)S(1)}, bf16[16,4,16,256]{3,2,1,0:T(8,128)(2,1)}) custom-call(s32[4]{0:T(128)S(1)} %pad_add_fusion.refs_0_.at_ref, bf16[1024,4096]{1,0:T(8,128)(2,1)} %all-gather.3.cloned.1.call-done.refs_1_, ...), custom_call_target="tpu_custom_call" | custom-call | tf_op jit(solution)/shard_map/pallas_call | solution.py:162
  94.8 8.8 %all-to-all-start.1 = ((bf16[16,4,16,256]{3,2,1,0:T(8,128)(2,1)}), bf16[16,4,16,256]{3,2,1,0:T(8,128)(2,1)S(1)}, u32[]{:S(2)}, u32[]{:S(2)}) async-start(bf16[16,4,16,256]{3,2,1,0:T(8,128)(2,1)} %get-tuple-element.52), calls=%async_computation.1 | async-start | bytes 1048576 | tf_op jit(solution)/shard_map/all_to_all | solution.py:405
  103.6 1.4 collective-permute-start.12
  105.0 1.9 %collective-permute-start.13 = (bf16[256,256]{1,0:T(8,128)(2,1)S(1)}, bf16[256,256]{1,0:T(8,128)(2,1)S(1)}, u32[]{:S(2)}, u32[]{:S(2)}) collective-permute-start(bf16[256,256]{1,0:T(8,128)(2,1)S(1)} %get-tuple-element.55), channel_id=1, source_target_pairs={{0,8},{4,12},{8,0},{12,4},{1,9},{5,13},{9,1},{13,5},{2,10},{6,14},... | collective-permute-start | bytes 393224 | tf_op jit(solution)/shard_map/ppermute | solution.py:376
  106.9 0.6 collective-permute-start.14
  107.5 1.2 collective-permute-done.12.refs_0_
  108.7 2.0 %collective-permute-done.13.refs_1_ = bf16[256,256]{1,0:T(8,128)(2,1)S(1)} collective-permute-done((bf16[256,256]{1,0:T(8,128)(2,1)S(1)}, bf16[256,256]{1,0:T(8,128)(2,1)S(1)}, u32[]{:S(2)}, u32[]{:S(2)}) %collective-permute-start.13) | collective-permute-done | bytes 131104 | tf_op jit(solution)/shard_map/ppermute | solution.py:376
  110.7 0.7 copy-done.10
  111.3 4.8 %all-to-all-done.1 = bf16[16,4,16,256]{3,2,1,0:T(8,128)(2,1)S(1)} async-done(((bf16[16,4,16,256]{3,2,1,0:T(8,128)(2,1)}), bf16[16,4,16,256]{3,2,1,0:T(8,128)(2,1)S(1)}, u32[]{:S(2)}, u32[]{:S(2)}) %all-to-all-start.1) | async-done | bytes 524320 | tf_op jit(solution)/shard_map/all_to_all | solution.py:405
  116.1 6.9 %shard_map.116 = bf16[1024,256]{1,0:T(8,128)(2,1)} custom-call(bf16[128,64]{1,0:T(8,128)(2,1)S(1)} %copy-done.6, bf16[64,128]{1,0:T(8,128)(2,1)S(1)} %copy-done.7, f32[2,64,256]{2,1,0:T(8,128)S(1)} %copy-done.2, bf16[1024,256]{1,0:T(8,128)(2,1)S(1)} %bitcast.12, bf16[1024,512]{1,0:T(8,128)(2,1)} %bitcast.9.resp_ref, ...), custom_call_target="tpu_custom_call" | custom-call | tf_op jit(solution)/shard_map/pallas_call | solution.py:359
  123.1 7.5 %all-to-all-start.2 = ((bf16[64,16,256]{2,1,0:T(8,128)(2,1)}), bf16[64,16,256]{2,1,0:T(8,128)(2,1)S(1)}, u32[]{:S(2)}, u32[]{:S(2)}) async-start(bf16[64,16,256]{2,1,0:T(8,128)(2,1)} %bitcast.10), calls=%async_computation.2 | async-start | bytes 1048576 | tf_op jit(solution)/shard_map/all_to_all | solution.py:410
  130.6 2.8 %all-gather.5.cloned.1.call-done.refs_2_ = bf16[4096,256]{1,0:T(8,128)(2,1)} async-done(((bf16[1024,256]{1,0:T(8,128)(2,1)}), bf16[4096,256]{1,0:T(8,128)(2,1)}) %all-gather.5.cloned.1.call-update) | async-done | bytes 2097168 | tf_op jit(solution)/shard_map/all_gather | solution.py:403
  133.4 8.0 %shard_map.117 = (bf16[256,256]{1,0:T(8,128)(2,1)S(1)}, bf16[256,256]{1,0:T(8,128)(2,1)}, bf16[256,256]{1,0:T(8,128)(2,1)}, bf16[256,256]{1,0:T(8,128)(2,1)S(1)}) custom-call(s32[4]{0:T(128)S(1)} %pad_add_fusion.refs_0_.at_ref, bf16[1024,4096]{1,0:T(8,128)(2,1)} %all-gather.3.cloned.1.call-done.refs_1_, bf16[4096,256]{1,0:T(8,128)(2,1)} %all-gather.5.cloned.1.call-done.refs_2_), custom_call_target="tpu_custom_call" | custom-call | tf_op jit(solution)/shard_map/pallas_call | solution.py:162
  141.4 1.3 collective-permute-start.15
  142.7 2.9 %collective-permute-start.16 = (bf16[256,256]{1,0:T(8,128)(2,1)}, bf16[256,256]{1,0:T(8,128)(2,1)}, u32[]{:S(2)}, u32[]{:S(2)}) collective-permute-start(bf16[256,256]{1,0:T(8,128)(2,1)} %get-tuple-element.66), channel_id=1, source_target_pairs={{0,8},{4,12},{8,0},{12,4},{1,9},{5,13},{9,1},{13,5},{2,10},{6,14},... | collective-permute-start | bytes 393224 | tf_op jit(solution)/shard_map/ppermute | solution.py:376
  145.6 0.8 collective-permute-start.17
  146.4 0.3 reshape.38.skip_ref
  146.8 1.4 collective-permute-done.15.refs_3_
  148.1 2.6 %collective-permute-done.16.refs_4_ = bf16[256,256]{1,0:T(8,128)(2,1)} collective-permute-done((bf16[256,256]{1,0:T(8,128)(2,1)}, bf16[256,256]{1,0:T(8,128)(2,1)}, u32[]{:S(2)}, u32[]{:S(2)}) %collective-permute-start.16) | collective-permute-done | bytes 131104 | tf_op jit(solution)/shard_map/ppermute | solution.py:376
  150.7 3.3 %shard_map.118 = (bf16[256,1024]{1,0:T(8,128)(2,1)S(1)}, bf16[256,1024]{1,0:T(8,128)(2,1)S(1)}) custom-call(s32[4]{0:T(128)S(1)} %pad_add_fusion.refs_0_.at_ref, f32[4,256,1]{2,1,0:T(8,128)S(1)} %reshape.38.skip_ref, bf16[1024,4096]{1,0:T(8,128)(2,1)} %weight_ref.5, bf16[16,4,16,256]{3,2,1,0:T(8,128)(2,1)S(1)} %bitcast.13, ...), custom_call_target="tpu_custom_call" | custom-call | tf_op jit(solution)/shard_map/pallas_call | solution.py:218
  154.0 5.1 %collective-permute-start.18 = (bf16[256,1024]{1,0:T(8,128)(2,1)S(1)}, bf16[256,1024]{1,0:T(8,128)(2,1)S(1)}, u32[]{:S(2)}, u32[]{:S(2)}) collective-permute-start(bf16[256,1024]{1,0:T(8,128)(2,1)S(1)} %get-tuple-element.69), channel_id=1, source_target_pairs={{0,1},{1,0},{2,3},{3,2},{4,5},{5,4},{6,7},{7,6},{8,9},{9,8},{10,11... | collective-permute-start | bytes 1572872 | tf_op jit(solution)/shard_map/ppermute | solution.py:416
  159.1 2.9 %shard_map.119 = f32[256,1024]{1,0:T(8,128)S(1)} custom-call(s32[4]{0:T(128)S(1)} %pad_add_fusion.refs_0_.at_ref, bf16[256,1024]{1,0:T(8,128)(2,1)S(1)} %get-tuple-element.70.home_ref, bf16[1024,4096]{1,0:T(8,128)(2,1)} %weight_ref.5), custom_call_target="tpu_custom_call" | custom-call | tf_op jit(solution)/shard_map/pallas_call | solution.py:247
  162.0 0.1 add_convert_fusion.1
  162.1 2.7 %collective-permute-start.20 = (bf16[256,1024]{1,0:T(8,128)(2,1)S(1)}, bf16[256,1024]{1,0:T(8,128)(2,1)S(1)}, u32[]{:S(2)}, u32[]{:S(2)}) collective-permute-start(bf16[256,1024]{1,0:T(8,128)(2,1)S(1)} %add_convert_fusion.1), channel_id=1, source_target_pairs={{0,2},{2,0},{1,3},{3,1},{4,6},{6,4},{5,7},{7,5},{8,10},{10,8},{9,1... | collective-permute-start | bytes 1572872 | tf_op jit(solution)/shard_map/ppermute | solution.py:419
  164.9 3.6 %shard_map.120 = (bf16[256,1024]{1,0:T(8,128)(2,1)S(1)}, f32[256,1024]{1,0:T(8,128)S(1)}) custom-call(s32[4]{0:T(128)S(1)} %pad_add_fusion.refs_0_.at_ref, bf16[256,1024]{1,0:T(8,128)(2,1)S(1)} %get-tuple-element.70.home_ref, bf16[1024,4096]{1,0:T(8,128)(2,1)} %weight_ref.5), custom_call_target="tpu_custom_call" | custom-call | tf_op jit(solution)/shard_map/pallas_call | solution.py:274
  168.5 0.4 collective-permute-start.19
  168.8 8.3 %collective-permute-done.20 = bf16[256,1024]{1,0:T(8,128)(2,1)S(1)} collective-permute-done((bf16[256,1024]{1,0:T(8,128)(2,1)S(1)}, bf16[256,1024]{1,0:T(8,128)(2,1)S(1)}, u32[]{:S(2)}, u32[]{:S(2)}) %collective-permute-start.20) | collective-permute-done | bytes 524320 | tf_op jit(solution)/shard_map/ppermute | solution.py:419
  177.2 1.0 add_convert_fusion
  (31 shorter events, 0.1 us)
Async XLA Ops:
  6.5 2.7 %copy-start = (bf16[256,4096]{1,0:T(8,128)(2,1)S(1)}, bf16[256,4096]{1,0:T(8,128)(2,1)}, u32[]{:S(2)}) copy-start(bf16[256,4096]{1,0:T(8,128)(2,1)} %param.11) | copy-start | bytes 6291460
  6.5 76.6 %all-gather.3.cloned.1.call-start = ((), (), s32[]{:S(2)}) async-start(), calls=%async_computation.3 | async-start | bytes 9437184 | tf_op jit(solution)/shard_map/all_gather | solution.py:395
  10.3 79.3 %all-to-all-start = ((bf16[64,16,512]{2,1,0:T(8,128)(2,1)}), bf16[64,16,512]{2,1,0:T(8,128)(2,1)}, u32[]{:S(2)}, u32[]{:S(2)}) async-start(bf16[64,16,512]{2,1,0:T(8,128)(2,1)} %bitcast.7), calls=%async_computation | async-start | bytes 2097152 | tf_op jit(solution)/shard_map/all_to_all | solution.py:387
  25.7 107.7 %all-gather.5.cloned.1.call-start = ((), (), s32[]{:S(2)}) async-start(), calls=%async_computation.4 | async-start | bytes 2621440 | tf_op jit(solution)/shard_map/all_gather | solution.py:403
  27.5 8.9 %collective-permute-start = (bf16[128,256]{1,0:T(8,128)(2,1)}, bf16[128,256]{1,0:T(8,128)(2,1)S(1)}, u32[]{:S(2)}, u32[]{:S(2)}) collective-permute-start(bf16[128,256]{1,0:T(8,128)(2,1)} %get-tuple-element.42), channel_id=1, source_target_pairs={{0,4},{4,8},{8,12},{12,0},{1,5},{5,9},{9,13},{13,1},{2,6},{6,10},{... | collective-permute-start | bytes 196616 | tf_op jit(solution)/shard_map/ppermute | solution.py:390
  28.5 11.5 %collective-permute-start.1 = (bf16[128,256]{1,0:T(8,128)(2,1)}, bf16[128,256]{1,0:T(8,128)(2,1)S(1)}, u32[]{:S(2)}, u32[]{:S(2)}) collective-permute-start(bf16[128,256]{1,0:T(8,128)(2,1)} %get-tuple-element.43), channel_id=1, source_target_pairs={{0,8},{4,12},{8,0},{12,4},{1,9},{5,13},{9,1},{13,5},{2,10},{6,14},... | collective-permute-start | bytes 196616 | tf_op jit(solution)/shard_map/ppermute | solution.py:390
  30.9 9.4 %collective-permute-start.2 = (bf16[128,256]{1,0:T(8,128)(2,1)}, bf16[128,256]{1,0:T(8,128)(2,1)S(1)}, u32[]{:S(2)}, u32[]{:S(2)}) collective-permute-start(bf16[128,256]{1,0:T(8,128)(2,1)} %get-tuple-element.44), channel_id=1, source_target_pairs={{0,12},{4,0},{8,4},{12,8},{1,13},{5,1},{9,5},{13,9},{2,14},{6,2},{... | collective-permute-start | bytes 196616 | tf_op jit(solution)/shard_map/ppermute | solution.py:390
  40.3 0.8 copy-start.5
  41.9 11.1 %collective-permute-start.3 = (bf16[256,256]{1,0:T(8,128)(2,1)}, bf16[256,256]{1,0:T(8,128)(2,1)S(1)}, u32[]{:S(2)}, u32[]{:S(2)}) collective-permute-start(bf16[256,256]{1,0:T(8,128)(2,1)} %get-tuple-element.45.refs_0_), channel_id=1, source_target_pairs={{0,16},{16,32},{32,48},{48,0},{1,17},{17,33},{33,49},{49,1},{2,18}... | collective-permute-start | bytes 393224 | tf_op jit(solution)/shard_map/ppermute | solution.py:95
  44.7 13.6 %collective-permute-start.4 = (bf16[256,256]{1,0:T(8,128)(2,1)}, bf16[256,256]{1,0:T(8,128)(2,1)S(1)}, u32[]{:S(2)}, u32[]{:S(2)}) collective-permute-start(bf16[256,256]{1,0:T(8,128)(2,1)} %get-tuple-element.45.refs_0_), channel_id=1, source_target_pairs={{0,32},{16,48},{32,0},{48,16},{1,33},{17,49},{33,1},{49,17},{2,34}... | collective-permute-start | bytes 393224 | tf_op jit(solution)/shard_map/ppermute | solution.py:95
  49.3 8.9 %collective-permute-start.5 = (bf16[256,256]{1,0:T(8,128)(2,1)}, bf16[256,256]{1,0:T(8,128)(2,1)S(1)}, u32[]{:S(2)}, u32[]{:S(2)}) collective-permute-start(bf16[256,256]{1,0:T(8,128)(2,1)} %get-tuple-element.45.refs_0_), channel_id=1, source_target_pairs={{0,48},{16,0},{32,16},{48,32},{1,49},{17,1},{33,17},{49,33},{2,50}... | collective-permute-start | bytes 393224 | tf_op jit(solution)/shard_map/ppermute | solution.py:95
  58.2 0.9 copy-start.4
  60.0 23.1 %collective-permute-start.10 = (bf16[1024,256]{1,0:T(8,128)(2,1)}, bf16[1024,256]{1,0:T(8,128)(2,1)}, u32[]{:S(2)}, u32[]{:S(2)}) collective-permute-start(bf16[1024,256]{1,0:T(8,128)(2,1)} %shard_map.112.refs_2_), channel_id=1, source_target_pairs={{0,64},{64,128},{128,192},{192,0},{1,65},{65,129},{129,193},{193,1... | collective-permute-start | bytes 1572872 | tf_op jit(solution)/shard_map/ppermute | solution.py:95
  63.0 20.1 %collective-permute-start.11 = (bf16[1024,256]{1,0:T(8,128)(2,1)}, bf16[1024,256]{1,0:T(8,128)(2,1)}, u32[]{:S(2)}, u32[]{:S(2)}) collective-permute-start(bf16[1024,256]{1,0:T(8,128)(2,1)} %shard_map.112.refs_2_), channel_id=1, source_target_pairs={{0,192},{64,0},{128,64},{192,128},{1,193},{65,1},{129,65},{193,129... | collective-permute-start | bytes 1572872 | tf_op jit(solution)/shard_map/ppermute | solution.py:95
  63.3 26.3 %collective-permute-start.6 = (bf16[1024,256]{1,0:T(8,128)(2,1)}, bf16[1024,256]{1,0:T(8,128)(2,1)S(1)}, u32[]{:S(2)}, u32[]{:S(2)}) collective-permute-start(bf16[1024,256]{1,0:T(8,128)(2,1)} %shard_map.112.refs_2_), channel_id=1, source_target_pairs={{0,128},{64,192},{128,0},{192,64},{1,129},{65,193},{129,1},{193,65... | collective-permute-start | bytes 1572872 | tf_op jit(solution)/shard_map/ppermute | solution.py:95
  65.3 6.9 %collective-permute-start.7 = (bf16[256,256]{1,0:T(8,128)(2,1)}, bf16[256,256]{1,0:T(8,128)(2,1)S(1)}, u32[]{:S(2)}, u32[]{:S(2)}) collective-permute-start(bf16[256,256]{1,0:T(8,128)(2,1)} %get-tuple-element.49.refs_0_), channel_id=1, source_target_pairs={{0,16},{16,32},{32,48},{48,0},{1,17},{17,33},{33,49},{49,1},{2,18}... | collective-permute-start | bytes 393224 | tf_op jit(solution)/shard_map/ppermute | solution.py:95
  68.0 8.0 %collective-permute-start.8 = (bf16[256,256]{1,0:T(8,128)(2,1)}, bf16[256,256]{1,0:T(8,128)(2,1)S(1)}, u32[]{:S(2)}, u32[]{:S(2)}) collective-permute-start(bf16[256,256]{1,0:T(8,128)(2,1)} %get-tuple-element.49.refs_0_), channel_id=1, source_target_pairs={{0,32},{16,48},{32,0},{48,16},{1,33},{17,49},{33,1},{49,17},{2,34}... | collective-permute-start | bytes 393224 | tf_op jit(solution)/shard_map/ppermute | solution.py:95
  72.2 9.1 %collective-permute-start.9 = (bf16[256,256]{1,0:T(8,128)(2,1)}, bf16[256,256]{1,0:T(8,128)(2,1)S(1)}, u32[]{:S(2)}, u32[]{:S(2)}) collective-permute-start(bf16[256,256]{1,0:T(8,128)(2,1)} %get-tuple-element.49.refs_0_), channel_id=1, source_target_pairs={{0,48},{16,0},{32,16},{48,32},{1,49},{17,1},{33,17},{49,33},{2,50}... | collective-permute-start | bytes 393224 | tf_op jit(solution)/shard_map/ppermute | solution.py:95
  81.4 0.9 copy-start.3
  88.5 1.0 copy-start.1
  89.6 0.8 copy-start.8
  90.4 25.7 %copy-start.2 = (f32[2,64,256]{2,1,0:T(8,128)S(1)}, f32[2,64,256]{2,1,0:T(8,128)}, u32[]{:S(2)}) copy-start(f32[2,64,256]{2,1,0:T(8,128)} %constant.37.clone.turn) | copy-start | bytes 393220
  90.4 25.7 %copy-start.6 = (bf16[128,64]{1,0:T(8,128)(2,1)S(1)}, bf16[128,64]{1,0:T(8,128)(2,1)}, u32[]{:S(2)}) copy-start(bf16[128,64]{1,0:T(8,128)(2,1)} %constant.35.clone.first) | copy-start | bytes 49156
  90.4 25.7 %copy-start.7 = (bf16[64,128]{1,0:T(8,128)(2,1)S(1)}, bf16[64,128]{1,0:T(8,128)(2,1)}, u32[]{:S(2)}) copy-start(bf16[64,128]{1,0:T(8,128)(2,1)} %constant.36.clone.last) | copy-start | bytes 49156
  94.8 21.3 %all-to-all-start.1 = ((bf16[16,4,16,256]{3,2,1,0:T(8,128)(2,1)}), bf16[16,4,16,256]{3,2,1,0:T(8,128)(2,1)S(1)}, u32[]{:S(2)}, u32[]{:S(2)}) async-start(bf16[16,4,16,256]{3,2,1,0:T(8,128)(2,1)} %get-tuple-element.52), calls=%async_computation.1 | async-start | bytes 1048576 | tf_op jit(solution)/shard_map/all_to_all | solution.py:405
  103.6 5.1 %collective-permute-start.12 = (bf16[256,256]{1,0:T(8,128)(2,1)S(1)}, bf16[256,256]{1,0:T(8,128)(2,1)S(1)}, u32[]{:S(2)}, u32[]{:S(2)}) collective-permute-start(bf16[256,256]{1,0:T(8,128)(2,1)S(1)} %get-tuple-element.54), channel_id=1, source_target_pairs={{0,4},{4,8},{8,12},{12,0},{1,5},{5,9},{9,13},{13,1},{2,6},{6,10},{... | collective-permute-start | bytes 393224 | tf_op jit(solution)/shard_map/ppermute | solution.py:376
  105.0 5.7 %collective-permute-start.13 = (bf16[256,256]{1,0:T(8,128)(2,1)S(1)}, bf16[256,256]{1,0:T(8,128)(2,1)S(1)}, u32[]{:S(2)}, u32[]{:S(2)}) collective-permute-start(bf16[256,256]{1,0:T(8,128)(2,1)S(1)} %get-tuple-element.55), channel_id=1, source_target_pairs={{0,8},{4,12},{8,0},{12,4},{1,9},{5,13},{9,1},{13,5},{2,10},{6,14},... | collective-permute-start | bytes 393224 | tf_op jit(solution)/shard_map/ppermute | solution.py:376
  106.9 4.4 %collective-permute-start.14 = (bf16[256,256]{1,0:T(8,128)(2,1)S(1)}, bf16[256,256]{1,0:T(8,128)(2,1)}, u32[]{:S(2)}, u32[]{:S(2)}) collective-permute-start(bf16[256,256]{1,0:T(8,128)(2,1)S(1)} %get-tuple-element.56), channel_id=1, source_target_pairs={{0,12},{4,0},{8,4},{12,8},{1,13},{5,1},{9,5},{13,9},{2,14},{6,2},{... | collective-permute-start | bytes 393224 | tf_op jit(solution)/shard_map/ppermute | solution.py:376
  108.7 2.0 %copy-start.9 = (bf16[256,256]{1,0:T(8,128)(2,1)}, bf16[256,256]{1,0:T(8,128)(2,1)S(1)}, u32[]{:S(2)}) copy-start(bf16[256,256]{1,0:T(8,128)(2,1)S(1)} %collective-permute-done.12.refs_0_) | copy-start | bytes 393220
  110.7 0.7 copy-start.10
  123.1 23.7 %all-to-all-start.2 = ((bf16[64,16,256]{2,1,0:T(8,128)(2,1)}), bf16[64,16,256]{2,1,0:T(8,128)(2,1)S(1)}, u32[]{:S(2)}, u32[]{:S(2)}) async-start(bf16[64,16,256]{2,1,0:T(8,128)(2,1)} %bitcast.10), calls=%async_computation.2 | async-start | bytes 1048576 | tf_op jit(solution)/shard_map/all_to_all | solution.py:410
  130.6 15.8 %copy-start.11 = (f32[1024]{0:T(1024)S(1)}, f32[1024]{0:T(1024)}, u32[]{:S(2)}) copy-start(f32[1024]{0:T(1024)} %param.15) | copy-start | bytes 12292
  141.4 6.7 %collective-permute-start.15 = (bf16[256,256]{1,0:T(8,128)(2,1)}, bf16[256,256]{1,0:T(8,128)(2,1)}, u32[]{:S(2)}, u32[]{:S(2)}) collective-permute-start(bf16[256,256]{1,0:T(8,128)(2,1)} %get-tuple-element.65), channel_id=1, source_target_pairs={{0,4},{4,8},{8,12},{12,0},{1,5},{5,9},{9,13},{13,1},{2,6},{6,10},{... | collective-permute-start | bytes 393224 | tf_op jit(solution)/shard_map/ppermute | solution.py:376
  142.7 8.0 %collective-permute-start.16 = (bf16[256,256]{1,0:T(8,128)(2,1)}, bf16[256,256]{1,0:T(8,128)(2,1)}, u32[]{:S(2)}, u32[]{:S(2)}) collective-permute-start(bf16[256,256]{1,0:T(8,128)(2,1)} %get-tuple-element.66), channel_id=1, source_target_pairs={{0,8},{4,12},{8,0},{12,4},{1,9},{5,13},{9,1},{13,5},{2,10},{6,14},... | collective-permute-start | bytes 393224 | tf_op jit(solution)/shard_map/ppermute | solution.py:376
  145.6 5.1 %collective-permute-start.17 = (bf16[256,256]{1,0:T(8,128)(2,1)S(1)}, bf16[256,256]{1,0:T(8,128)(2,1)}, u32[]{:S(2)}, u32[]{:S(2)}) collective-permute-start(bf16[256,256]{1,0:T(8,128)(2,1)S(1)} %get-tuple-element.67), channel_id=1, source_target_pairs={{0,12},{4,0},{8,4},{12,8},{1,13},{5,1},{9,5},{13,9},{2,14},{6,2},{... | collective-permute-start | bytes 393224 | tf_op jit(solution)/shard_map/ppermute | solution.py:376
  154.0 7.9 %collective-permute-start.18 = (bf16[256,1024]{1,0:T(8,128)(2,1)S(1)}, bf16[256,1024]{1,0:T(8,128)(2,1)S(1)}, u32[]{:S(2)}, u32[]{:S(2)}) collective-permute-start(bf16[256,1024]{1,0:T(8,128)(2,1)S(1)} %get-tuple-element.69), channel_id=1, source_target_pairs={{0,1},{1,0},{2,3},{3,2},{4,5},{5,4},{6,7},{7,6},{8,9},{9,8},{10,11... | collective-permute-start | bytes 1572872 | tf_op jit(solution)/shard_map/ppermute | solution.py:416
  162.1 15.0 %collective-permute-start.20 = (bf16[256,1024]{1,0:T(8,128)(2,1)S(1)}, bf16[256,1024]{1,0:T(8,128)(2,1)S(1)}, u32[]{:S(2)}, u32[]{:S(2)}) collective-permute-start(bf16[256,1024]{1,0:T(8,128)(2,1)S(1)} %add_convert_fusion.1), channel_id=1, source_target_pairs={{0,2},{2,0},{1,3},{3,1},{4,6},{6,4},{5,7},{7,5},{8,10},{10,8},{9,1... | collective-permute-start | bytes 1572872 | tf_op jit(solution)/shard_map/ppermute | solution.py:419
  168.5 8.7 %collective-permute-start.19 = (bf16[256,1024]{1,0:T(8,128)(2,1)S(1)}, bf16[256,1024]{1,0:T(8,128)(2,1)S(1)}, u32[]{:S(2)}, u32[]{:S(2)}) collective-permute-start(bf16[256,1024]{1,0:T(8,128)(2,1)S(1)} %get-tuple-element.72), channel_id=1, source_target_pairs={{0,1},{1,0},{2,3},{3,2},{4,5},{5,4},{6,7},{7,6},{8,9},{9,8},{10,11... | collective-permute-start | bytes 1572872 | tf_op jit(solution)/shard_map/ppermute | solution.py:422
Sparse Core Ops, SparseCore 0:
  10.4 68.1 all-gather.2
  90.5 42.8 all-gather.4

commit v4 on v3

--- a/solution.py
+++ b/solution.py
@@ -96,7 +96,7 @@
 
 
 def sum_kernel(steps, at_ref, act_ref, *refs):
-    w_refs, (total, a_buf, w_buf, sems) = refs[: len(steps)], refs[len(steps) :]
+    w_refs, (total, mark, a_buf, w_buf, sems) = refs[: len(steps)], refs[len(steps) :]
     depth = w_buf.shape[1]
     copies = []
     for at, step in enumerate(steps):
@@ -108,6 +108,7 @@
             copy.wait()
         prod = jnp.dot(a_buf[at], w_buf[at], preferred_element_type=F32)
         total[...] = prod if at == 0 else total[...] + prod
+    mark[...] = total[:8, :128]
 
 
 def part_sum(at, act, weights, steps):
@@ -115,9 +116,12 @@
     cols = weights[0].shape[1]
     return pl.pallas_call(
         lambda *refs: sum_kernel(steps, *refs),
-        out_shape=jax.ShapeDtypeStruct((rows, cols), F32),
+        out_shape=(
+            jax.ShapeDtypeStruct((rows, cols), F32),
+            jax.ShapeDtypeStruct((8, 128), F32),
+        ),
         in_specs=[SCALARS] + [OUTSIDE] * (len(steps) + 1),
-        out_specs=INSIDE,
+        out_specs=(INSIDE, INSIDE),
         scratch_shapes=[
             pltpu.VMEM((len(steps), rows, depth), BF16),
             pltpu.VMEM((len(steps), depth, cols), BF16),
@@ -135,17 +139,19 @@
     copies = []
     for at, step in enumerate(steps):
         first = pl.multiple_of(lax.rem(own_y + 4 - step, 4) * depth, depth)
-        source = w_ref if len(steps) == 1 else w_ref.at[pl.ds(first, depth)]
-        pair = (source, act_ref.at[:, pl.ds(first, depth)])
-        copies.append(fetch(pair, (w_buf.at[at], a_buf.at[at]), sems.at[at]))
-    has_sum = len(refs) > len(outs) + 4
-    if has_sum:
-        copies[0] += fetch(refs[:1], (total,), sems.at[len(steps)])
+        pair = [(act_ref.at[:, pl.ds(first, depth)], a_buf.at[at])]
+        if len(steps) > 1:
+            pair.append((w_ref.at[pl.ds(first, depth)], w_buf.at[at]))
+        copies.append(fetch(*zip(*pair), sems.at[at]))
     for at, pair in enumerate(copies):
         for copy in pair:
             copy.wait()
-        prod = jnp.dot(a_buf[at], w_buf[at], preferred_element_type=F32)
-        total[...] = total[...] + prod if at or has_sum else prod
+        weight = w_buf[at] if len(steps) > 1 else w_ref[...]
+        prod = jnp.dot(a_buf[at], weight, preferred_element_type=F32)
+        if at:
+            total[...] += prod
+        else:
+            total[...] = prod if len(steps) > 1 else refs[0][...] + prod
     for step in range(4):
         part = lax.rem(own_x + step, 4)
         row = pl.multiple_of(part * rows, 8)
@@ -162,16 +168,16 @@
     return pl.pallas_call(
         lambda *refs: finish_kernel(steps, whole, *refs),
         out_shape=[jax.ShapeDtypeStruct(shape, BF16) for shape in shapes],
-        in_specs=[SCALARS] + [OUTSIDE] * (2 + len(before)),
+        in_specs=[SCALARS, OUTSIDE] + ([INSIDE] * 3 if before else [OUTSIDE]),
         out_specs=[INSIDE] * len(shapes),
         scratch_shapes=[
             pltpu.VMEM((len(steps), 4 * rows, depth), BF16),
             pltpu.VMEM((len(steps), depth, cols), BF16),
             pltpu.VMEM((4 * rows, cols), F32),
-            pltpu.SemaphoreType.DMA((len(steps) + 1, 2)),
+            pltpu.SemaphoreType.DMA((len(steps), 2)),
         ],
         compiler_params=pltpu.CompilerParams(vmem_limit_bytes=40 * 1024 * 1024),
-    )(at, *in_hbm([act, weight, *before]))
+    )(at, *in_hbm([act]), *(in_vmem([weight, *before]) if before else in_hbm([weight])))
 
 
 def fetch(sources, buffers, sems):
@@ -323,7 +329,7 @@
     t_cos, t_sin = turn[0], turn[1]
     for copy in copies:
         copy.wait()
-    group = 4
+    group = 8
     for start in range(0, 16, group):
         picks = [pl.ds(start + at, 64, stride=16) for at in range(group)]
         turned = []
@@ -398,10 +404,10 @@
     w_y, g_x = tie(w_y, g_x)
     w_all = to_all(w_y, "y")
     (g_y,) = place(my_zh, to_all(g_x, "zh"), 1)
-    here = part_sum(at, act, [w_all[0], w_all[1], w_all[3]], (0, 1, 3))
-    w_far, resp, g_y, here = tie(w_all[2], resp, g_y, here)
+    here, mark = part_sum(at, act, [w_all[0], w_all[1], w_all[3]], (0, 1, 3))
+    w_far, resp, g_y, mark = tie(w_all[2], resp, g_y, mark)
     g_all = lax.all_gather(g_y, "y", axis=0, tiled=True)
-    *values, value = project(at, act, w_far, (2,), [here], True)
+    *values, value = project(at, act, w_far, (2,), [here, mark], True)
     slabs = lax.all_to_all(value, SLABS, 0, 0, tiled=True)
     values = along_x(values)
     slabs, *values = tie(slabs, *values)

time: 186 us -> 186 us (level)
  starting transfers between devices: 78.8 us -> 86.7 us
  waiting for transfers between devices: 43.6 us -> 36.5 us
    all_to_all x1, waiting for transfers between devices: 4.81 us -> 0.01 us  [body(): slabs = lax.all_to_all(value, SLABS, 0, 0, tiled=True)]
    ppermute x6, starting transfers between devices: 8.91 us -> 13.7 us  [along_x(): lax.ppermute(p, 'x', shift(step))]
    all_to_all x1, starting transfers between devices: 7.5 us -> 12.2 us  [body(): conv = lax.all_to_all(conv, SEQ, 0, 0, tiled=True).reshape(16, 4, 16, rows)]
    all_to_all x1, starting transfers between devices: 8.75 us -> 12.2 us  [body(): slabs = lax.all_to_all(value, SLABS, 0, 0, tiled=True)]
    all_to_all x1, waiting for transfers between devices: 0.01 us -> 3.05 us  [body(): conv = lax.all_to_all(conv, SEQ, 0, 0, tiled=True).reshape(16, 4, 16, rows)]
    all_gather x1, waiting for transfers between devices: 2.8 us -> 0.02 us  [body(): g_all = lax.all_gather(g_y, 'y', axis=0, tiled=True)]
    ppermute x9, waiting for transfers between devices: 12.2 us -> 9.73 us  [to_all(): lax.ppermute(block, axis, shift(step))]
    ppermute x9, starting transfers between devices: 25.4 us -> 23.2 us  [to_all(): lax.ppermute(block, axis, shift(step))]
  transfers between devices with their start and end apart: 26 -> 26, of which waited for: 15 -> 11; matrix products, arithmetic and copies ran while one was open for 0% -> 0% of each run, Pallas kernels for 19% -> 18%
where the time goes in v4:
time: 186 us; the launch traced here: 185 us
  starting transfers between devices  86.7 us (47%)
  Pallas kernels  39.8 us (21%)
  waiting for transfers between devices  36.5 us (20%)
  between operations  13.6 us (7%)
  local copies, waits for them, and re-layouts  6.96 us (4%)
    ppermute x9, starting transfers between devices, to_all(): lax.ppermute(block, axis, shift(step))  23.2 us
    all_to_all x1, starting transfers between devices, body(): resp = lax.all_to_all(resp.reshape(64, 16, 2 * rows), SEQ, 0, 0, tiled=True)  15.4 us
    ppermute x6, starting transfers between devices, along_x(): lax.ppermute(p, 'x', shift(step))  13.7 us
    all_to_all x1, starting transfers between devices, body(): slabs = lax.all_to_all(value, SLABS, 0, 0, tiled=True)  12.2 us
    all_to_all x1, starting transfers between devices, body(): conv = lax.all_to_all(conv, SEQ, 0, 0, tiled=True).reshape(16, 4, 16, rows)  12.2 us
    pallas_call x2, Pallas kernels, project(): pl.pallas_call(lambda *refs: finish_kernel(steps, whole, *refs), out_shap...  11.8 us
    ppermute x9, waiting for transfers between devices, to_all(): lax.ppermute(block, axis, shift(step))  9.73 us
    ppermute x1, waiting for transfers between devices, body(): back = lax.ppermute(away, 'zl', SWAP)  9.2 us
  transfers between devices with their start and end apart: 26, of which 11 were waited for; matrix products, arithmetic and copies ran while one was open for 0% of the time, Pallas kernels for 18%

profile of v4, /device:TPU:1, one launch (start us, length us, event | category | flops | bytes accessed | tf_op | source)
XLA Modules:
  0.0 184.8 jit_solution(11287339188386759688)
XLA Ops:
  6.5 2.7 %shard_map.109 = bf16[16,4,16,512]{3,2,1,0:T(8,128)(2,1)} custom-call(bf16[512,1024]{1,0:T(8,128)(2,1)} %bitcast.14), custom_call_target="tpu_custom_call" | custom-call | tf_op jit(solution)/shard_map/pallas_call | solution.py:46
  9.2 1.1 constant_dynamic-slice_fusion
  10.3 0.0 all-gather.3.cloned.1.call-update
  10.3 15.4 %all-to-all-start = ((bf16[64,16,512]{2,1,0:T(8,128)(2,1)}), bf16[64,16,512]{2,1,0:T(8,128)(2,1)}, u32[]{:S(2)}, u32[]{:S(2)}) async-start(bf16[64,16,512]{2,1,0:T(8,128)(2,1)} %bitcast.7), calls=%async_computation | async-start | bytes 2097152 | tf_op jit(solution)/shard_map/all_to_all | solution.py:393
  25.7 0.0 all-gather.5.cloned.1.call-start
  25.7 1.7 shard_map.110
  27.5 0.9 collective-permute-start
  28.4 2.4 %collective-permute-start.1 = (bf16[128,256]{1,0:T(8,128)(2,1)}, bf16[128,256]{1,0:T(8,128)(2,1)S(1)}, u32[]{:S(2)}, u32[]{:S(2)}) collective-permute-start(bf16[128,256]{1,0:T(8,128)(2,1)} %get-tuple-element.45), channel_id=1, source_target_pairs={{0,8},{4,12},{8,0},{12,4},{1,9},{5,13},{9,1},{13,5},{2,10},{6,14},... | collective-permute-start | bytes 196616 | tf_op jit(solution)/shard_map/ppermute | solution.py:396
  30.8 1.2 collective-permute-start.2
  32.0 4.4 %collective-permute-done.refs_1_ = bf16[128,256]{1,0:T(8,128)(2,1)S(1)} collective-permute-done((bf16[128,256]{1,0:T(8,128)(2,1)}, bf16[128,256]{1,0:T(8,128)(2,1)S(1)}, u32[]{:S(2)}, u32[]{:S(2)}) %collective-permute-start) | collective-permute-done | bytes 65568 | tf_op jit(solution)/shard_map/ppermute | solution.py:396
  36.4 3.5 %collective-permute-done.1.refs_2_ = bf16[128,256]{1,0:T(8,128)(2,1)S(1)} collective-permute-done((bf16[128,256]{1,0:T(8,128)(2,1)}, bf16[128,256]{1,0:T(8,128)(2,1)S(1)}, u32[]{:S(2)}, u32[]{:S(2)}) %collective-permute-start.1) | collective-permute-done | bytes 65568 | tf_op jit(solution)/shard_map/ppermute | solution.py:396
  39.9 0.4 collective-permute-done.2.refs_3_
  40.2 0.8 copy-done.6
  41.1 0.7 shard_map.111
  41.8 3.9 %collective-permute-start.5 = (bf16[256,256]{1,0:T(8,128)(2,1)}, bf16[256,256]{1,0:T(8,128)(2,1)S(1)}, u32[]{:S(2)}, u32[]{:S(2)}) collective-permute-start(bf16[256,256]{1,0:T(8,128)(2,1)} %get-tuple-element.47.refs_0_), channel_id=1, source_target_pairs={{0,48},{16,0},{32,16},{48,32},{1,49},{17,1},{33,17},{49,33},{2,50}... | collective-permute-start | bytes 393224 | tf_op jit(solution)/shard_map/ppermute | solution.py:95
  45.7 3.6 %collective-permute-start.4 = (bf16[256,256]{1,0:T(8,128)(2,1)}, bf16[256,256]{1,0:T(8,128)(2,1)S(1)}, u32[]{:S(2)}, u32[]{:S(2)}) collective-permute-start(bf16[256,256]{1,0:T(8,128)(2,1)} %get-tuple-element.47.refs_0_), channel_id=1, source_target_pairs={{0,32},{16,48},{32,0},{48,16},{1,33},{17,49},{33,1},{49,17},{2,34}... | collective-permute-start | bytes 393224 | tf_op jit(solution)/shard_map/ppermute | solution.py:95
  49.3 2.4 %collective-permute-start.3 = (bf16[256,256]{1,0:T(8,128)(2,1)}, bf16[256,256]{1,0:T(8,128)(2,1)S(1)}, u32[]{:S(2)}, u32[]{:S(2)}) collective-permute-start(bf16[256,256]{1,0:T(8,128)(2,1)} %get-tuple-element.47.refs_0_), channel_id=1, source_target_pairs={{0,16},{16,32},{32,48},{48,0},{1,17},{17,33},{33,49},{49,1},{2,18}... | collective-permute-start | bytes 393224 | tf_op jit(solution)/shard_map/ppermute | solution.py:95
  51.6 6.5 %collective-permute-done.5.refs_3_ = bf16[256,256]{1,0:T(8,128)(2,1)S(1)} collective-permute-done((bf16[256,256]{1,0:T(8,128)(2,1)}, bf16[256,256]{1,0:T(8,128)(2,1)S(1)}, u32[]{:S(2)}, u32[]{:S(2)}) %collective-permute-start.5) | collective-permute-done | bytes 131104 | tf_op jit(solution)/shard_map/ppermute | solution.py:95
  58.1 0.9 copy-done.5
  59.0 0.8 shard_map.112.refs_2_
  59.9 3.4 %collective-permute-start.11 = (bf16[1024,256]{1,0:T(8,128)(2,1)}, bf16[1024,256]{1,0:T(8,128)(2,1)}, u32[]{:S(2)}, u32[]{:S(2)}) collective-permute-start(bf16[1024,256]{1,0:T(8,128)(2,1)} %shard_map.112.refs_2_), channel_id=1, source_target_pairs={{0,192},{64,0},{128,64},{192,128},{1,193},{65,1},{129,65},{193,129... | collective-permute-start | bytes 1572872 | tf_op jit(solution)/shard_map/ppermute | solution.py:95
  63.3 0.0 collective-permute-start.10
  63.3 1.5 collective-permute-start.6
  64.8 0.3 collective-permute-start.9
  65.1 5.2 %collective-permute-start.8 = (bf16[256,256]{1,0:T(8,128)(2,1)}, bf16[256,256]{1,0:T(8,128)(2,1)S(1)}, u32[]{:S(2)}, u32[]{:S(2)}) collective-permute-start(bf16[256,256]{1,0:T(8,128)(2,1)} %get-tuple-element.51.refs_0_), channel_id=1, source_target_pairs={{0,32},{16,48},{32,0},{48,16},{1,33},{17,49},{33,1},{49,17},{2,34}... | collective-permute-start | bytes 393224 | tf_op jit(solution)/shard_map/ppermute | solution.py:95
  70.3 2.9 %collective-permute-start.7 = (bf16[256,256]{1,0:T(8,128)(2,1)}, bf16[256,256]{1,0:T(8,128)(2,1)S(1)}, u32[]{:S(2)}, u32[]{:S(2)}) collective-permute-start(bf16[256,256]{1,0:T(8,128)(2,1)} %get-tuple-element.51.refs_0_), channel_id=1, source_target_pairs={{0,16},{16,32},{32,48},{48,0},{1,17},{17,33},{33,49},{49,1},{2,18}... | collective-permute-start | bytes 393224 | tf_op jit(solution)/shard_map/ppermute | solution.py:95
  73.2 0.1 pad_add_fusion.refs_0_.at_ref
  73.3 0.0 collective-permute-done.8.refs_2_
  73.3 3.2 %collective-permute-done.7.refs_1_ = bf16[256,256]{1,0:T(8,128)(2,1)S(1)} collective-permute-done((bf16[256,256]{1,0:T(8,128)(2,1)}, bf16[256,256]{1,0:T(8,128)(2,1)S(1)}, u32[]{:S(2)}, u32[]{:S(2)}) %collective-permute-start.7) | collective-permute-done | bytes 131104 | tf_op jit(solution)/shard_map/ppermute | solution.py:95
  76.5 0.9 copy-done.4
  77.4 0.8 shard_map.113
  78.3 0.4 all-gather.3.cloned.1.call-done.refs_1_
  78.7 5.4 %shard_map.114 = (f32[1024,256]{1,0:T(8,128)S(1)}, f32[8,128]{1,0:T(8,128)S(1)}) custom-call(s32[4]{0:T(128)S(1)} %pad_add_fusion.refs_0_.at_ref, bf16[1024,4096]{1,0:T(8,128)(2,1)} %all-gather.3.cloned.1.call-done.refs_1_, bf16[1024,256]{1,0:T(8,128)(2,1)} %shard_map.112.refs_2_, bf16[1024,256]{1,0:T(8,128)(2,1)} %collective-permute-done.10.refs_3_, ...), custom_call_target="tpu_custom_call" | custom-call | tf_op jit(solution)/shard_map/pallas_call | solution.py:117
  84.1 1.0 copy-done.1
  85.1 0.0 all-to-all-done
  85.1 0.0 all-gather.5.cloned.1.call-update
  85.2 1.2 copy-done.2
  86.4 3.9 %shard_map.115 = (bf16[256,256]{1,0:T(8,128)(2,1)S(1)}, bf16[256,256]{1,0:T(8,128)(2,1)S(1)}, bf16[256,256]{1,0:T(8,128)(2,1)S(1)}, bf16[256,256]{1,0:T(8,128)(2,1)S(1)}, bf16[16,4,16,256]{3,2,1,0:T(8,128)(2,1)}) custom-call(s32[4]{0:T(128)S(1)} %pad_add_fusion.refs_0_.at_ref, bf16[1024,4096]{1,0:T(8,128)(2,1)} %all-gather.3.cloned.1.call-done.refs_1_, ...), custom_call_target="tpu_custom_call" | custom-call | tf_op jit(solution)/shard_map/pallas_call | solution.py:168
  90.3 12.2 %all-to-all-start.1 = ((bf16[16,4,16,256]{3,2,1,0:T(8,128)(2,1)}), bf16[16,4,16,256]{3,2,1,0:T(8,128)(2,1)S(1)}, u32[]{:S(2)}, u32[]{:S(2)}) async-start(bf16[16,4,16,256]{3,2,1,0:T(8,128)(2,1)} %get-tuple-element.56), calls=%async_computation.1 | async-start | bytes 1048576 | tf_op jit(solution)/shard_map/all_to_all | solution.py:411
  102.5 6.3 %collective-permute-start.12 = (bf16[256,256]{1,0:T(8,128)(2,1)S(1)}, bf16[256,256]{1,0:T(8,128)(2,1)S(1)}, u32[]{:S(2)}, u32[]{:S(2)}) collective-permute-start(bf16[256,256]{1,0:T(8,128)(2,1)S(1)} %get-tuple-element.58), channel_id=1, source_target_pairs={{0,4},{4,8},{8,12},{12,0},{1,5},{5,9},{9,13},{13,1},{2,6},{6,10},{... | collective-permute-start | bytes 393224 | tf_op jit(solution)/shard_map/ppermute | solution.py:382
  108.9 2.7 %collective-permute-start.13 = (bf16[256,256]{1,0:T(8,128)(2,1)S(1)}, bf16[256,256]{1,0:T(8,128)(2,1)S(1)}, u32[]{:S(2)}, u32[]{:S(2)}) collective-permute-start(bf16[256,256]{1,0:T(8,128)(2,1)S(1)} %get-tuple-element.59), channel_id=1, source_target_pairs={{0,8},{4,12},{8,0},{12,4},{1,9},{5,13},{9,1},{13,5},{2,10},{6,14},... | collective-permute-start | bytes 393224 | tf_op jit(solution)/shard_map/ppermute | solution.py:382
  111.6 1.2 collective-permute-done.12.refs_0_
  112.7 3.2 %collective-permute-done.13.refs_1_ = bf16[256,256]{1,0:T(8,128)(2,1)S(1)} collective-permute-done((bf16[256,256]{1,0:T(8,128)(2,1)S(1)}, bf16[256,256]{1,0:T(8,128)(2,1)S(1)}, u32[]{:S(2)}, u32[]{:S(2)}) %collective-permute-start.13) | collective-permute-done | bytes 131104 | tf_op jit(solution)/shard_map/ppermute | solution.py:382
  115.9 0.6 copy-done.10
  116.6 6.1 %shard_map.116 = bf16[1024,256]{1,0:T(8,128)(2,1)} custom-call(bf16[128,64]{1,0:T(8,128)(2,1)S(1)} %copy-done.7, bf16[64,128]{1,0:T(8,128)(2,1)S(1)} %copy-done.8, f32[2,64,256]{2,1,0:T(8,128)S(1)} %copy-done.3, bf16[1024,256]{1,0:T(8,128)(2,1)S(1)} %bitcast.12, bf16[1024,512]{1,0:T(8,128)(2,1)} %bitcast.9.resp_ref, ...), custom_call_target="tpu_custom_call" | custom-call | tf_op jit(solution)/shard_map/pallas_call | solution.py:365
  122.7 12.2 %all-to-all-start.2 = ((bf16[64,16,256]{2,1,0:T(8,128)(2,1)}), bf16[64,16,256]{2,1,0:T(8,128)(2,1)S(1)}, u32[]{:S(2)}, u32[]{:S(2)}) async-start(bf16[64,16,256]{2,1,0:T(8,128)(2,1)} %bitcast.10), calls=%async_computation.2 | async-start | bytes 1048576 | tf_op jit(solution)/shard_map/all_to_all | solution.py:416
  134.9 0.0 copy-start.11
  134.9 0.0 all-gather.5.cloned.1.call-done.refs_2_
  135.0 7.9 %shard_map.117 = (bf16[256,256]{1,0:T(8,128)(2,1)S(1)}, bf16[256,256]{1,0:T(8,128)(2,1)}, bf16[256,256]{1,0:T(8,128)(2,1)}, bf16[256,256]{1,0:T(8,128)(2,1)S(1)}) custom-call(s32[4]{0:T(128)S(1)} %pad_add_fusion.refs_0_.at_ref, bf16[1024,4096]{1,0:T(8,128)(2,1)} %all-gather.3.cloned.1.call-done.refs_1_, bf16[4096,256]{1,0:T(8,128)(2,1)} %all-gather.5.cloned.1.call-done.refs_2_), custom_call_target="tpu_custom_call" | custom-call | tf_op jit(solution)/shard_map/pallas_call | solution.py:168
  142.8 1.1 collective-permute-start.15
  143.9 2.6 %collective-permute-start.16 = (bf16[256,256]{1,0:T(8,128)(2,1)}, bf16[256,256]{1,0:T(8,128)(2,1)}, u32[]{:S(2)}, u32[]{:S(2)}) collective-permute-start(bf16[256,256]{1,0:T(8,128)(2,1)} %get-tuple-element.70), channel_id=1, source_target_pairs={{0,8},{4,12},{8,0},{12,4},{1,9},{5,13},{9,1},{13,5},{2,10},{6,14},... | collective-permute-start | bytes 393224 | tf_op jit(solution)/shard_map/ppermute | solution.py:382
  146.5 1.0 collective-permute-start.17
  147.5 0.3 reshape.38.skip_ref
  147.8 3.0 %all-to-all-done.2 = bf16[64,16,256]{2,1,0:T(8,128)(2,1)S(1)} async-done(((bf16[64,16,256]{2,1,0:T(8,128)(2,1)}), bf16[64,16,256]{2,1,0:T(8,128)(2,1)S(1)}, u32[]{:S(2)}, u32[]{:S(2)}) %all-to-all-start.2) | async-done | bytes 524320 | tf_op jit(solution)/shard_map/all_to_all | solution.py:416
  150.9 1.5 collective-permute-done.16.refs_4_
  152.4 3.3 %shard_map.118 = (bf16[256,1024]{1,0:T(8,128)(2,1)S(1)}, bf16[256,1024]{1,0:T(8,128)(2,1)S(1)}) custom-call(s32[4]{0:T(128)S(1)} %pad_add_fusion.refs_0_.at_ref, f32[4,256,1]{2,1,0:T(8,128)S(1)} %reshape.38.skip_ref, bf16[1024,4096]{1,0:T(8,128)(2,1)} %weight_ref.5, bf16[16,4,16,256]{3,2,1,0:T(8,128)(2,1)S(1)} %bitcast.13, ...), custom_call_target="tpu_custom_call" | custom-call | tf_op jit(solution)/shard_map/pallas_call | solution.py:224
  155.7 4.6 %collective-permute-start.18 = (bf16[256,1024]{1,0:T(8,128)(2,1)S(1)}, bf16[256,1024]{1,0:T(8,128)(2,1)S(1)}, u32[]{:S(2)}, u32[]{:S(2)}) collective-permute-start(bf16[256,1024]{1,0:T(8,128)(2,1)S(1)} %get-tuple-element.73), channel_id=1, source_target_pairs={{0,1},{1,0},{2,3},{3,2},{4,5},{5,4},{6,7},{7,6},{8,9},{9,8},{10,11... | collective-permute-start | bytes 1572872 | tf_op jit(solution)/shard_map/ppermute | solution.py:422
  160.3 2.9 %shard_map.119 = f32[256,1024]{1,0:T(8,128)S(1)} custom-call(s32[4]{0:T(128)S(1)} %pad_add_fusion.refs_0_.at_ref, bf16[256,1024]{1,0:T(8,128)(2,1)S(1)} %get-tuple-element.74.home_ref, bf16[1024,4096]{1,0:T(8,128)(2,1)} %weight_ref.5), custom_call_target="tpu_custom_call" | custom-call | tf_op jit(solution)/shard_map/pallas_call | solution.py:253
  163.2 0.1 add_convert_fusion.1
  163.3 0.5 collective-permute-start.20
  163.8 3.6 %shard_map.120 = (bf16[256,1024]{1,0:T(8,128)(2,1)S(1)}, f32[256,1024]{1,0:T(8,128)S(1)}) custom-call(s32[4]{0:T(128)S(1)} %pad_add_fusion.refs_0_.at_ref, bf16[256,1024]{1,0:T(8,128)(2,1)S(1)} %get-tuple-element.74.home_ref, bf16[1024,4096]{1,0:T(8,128)(2,1)} %weight_ref.5), custom_call_target="tpu_custom_call" | custom-call | tf_op jit(solution)/shard_map/pallas_call | solution.py:280
  167.4 0.4 collective-permute-start.19
  167.8 9.2 %collective-permute-done.20 = bf16[256,1024]{1,0:T(8,128)(2,1)S(1)} collective-permute-done((bf16[256,1024]{1,0:T(8,128)(2,1)S(1)}, bf16[256,1024]{1,0:T(8,128)(2,1)S(1)}, u32[]{:S(2)}, u32[]{:S(2)}) %collective-permute-start.20) | collective-permute-done | bytes 524320 | tf_op jit(solution)/shard_map/ppermute | solution.py:425
  177.0 1.0 add_convert_fusion
  (31 shorter events, 0.1 us)
Async XLA Ops:
  6.5 2.7 %copy-start = (bf16[256,4096]{1,0:T(8,128)(2,1)S(1)}, bf16[256,4096]{1,0:T(8,128)(2,1)}, u32[]{:S(2)}) copy-start(bf16[256,4096]{1,0:T(8,128)(2,1)} %param.11) | copy-start | bytes 6291460
  6.5 72.1 %all-gather.3.cloned.1.call-start = ((), (), s32[]{:S(2)}) async-start(), calls=%async_computation.3 | async-start | bytes 9437184 | tf_op jit(solution)/shard_map/all_gather | solution.py:401
  10.3 74.8 %all-to-all-start = ((bf16[64,16,512]{2,1,0:T(8,128)(2,1)}), bf16[64,16,512]{2,1,0:T(8,128)(2,1)}, u32[]{:S(2)}, u32[]{:S(2)}) async-start(bf16[64,16,512]{2,1,0:T(8,128)(2,1)} %bitcast.7), calls=%async_computation | async-start | bytes 2097152 | tf_op jit(solution)/shard_map/all_to_all | solution.py:393
  25.7 109.3 %all-gather.5.cloned.1.call-start = ((), (), s32[]{:S(2)}) async-start(), calls=%async_computation.4 | async-start | bytes 2621440 | tf_op jit(solution)/shard_map/all_gather | solution.py:409
  27.5 8.9 %collective-permute-start = (bf16[128,256]{1,0:T(8,128)(2,1)}, bf16[128,256]{1,0:T(8,128)(2,1)S(1)}, u32[]{:S(2)}, u32[]{:S(2)}) collective-permute-start(bf16[128,256]{1,0:T(8,128)(2,1)} %get-tuple-element.44), channel_id=1, source_target_pairs={{0,4},{4,8},{8,12},{12,0},{1,5},{5,9},{9,13},{13,1},{2,6},{6,10},{... | collective-permute-start | bytes 196616 | tf_op jit(solution)/shard_map/ppermute | solution.py:396
  28.4 11.4 %collective-permute-start.1 = (bf16[128,256]{1,0:T(8,128)(2,1)}, bf16[128,256]{1,0:T(8,128)(2,1)S(1)}, u32[]{:S(2)}, u32[]{:S(2)}) collective-permute-start(bf16[128,256]{1,0:T(8,128)(2,1)} %get-tuple-element.45), channel_id=1, source_target_pairs={{0,8},{4,12},{8,0},{12,4},{1,9},{5,13},{9,1},{13,5},{2,10},{6,14},... | collective-permute-start | bytes 196616 | tf_op jit(solution)/shard_map/ppermute | solution.py:396
  30.8 9.4 %collective-permute-start.2 = (bf16[128,256]{1,0:T(8,128)(2,1)}, bf16[128,256]{1,0:T(8,128)(2,1)S(1)}, u32[]{:S(2)}, u32[]{:S(2)}) collective-permute-start(bf16[128,256]{1,0:T(8,128)(2,1)} %get-tuple-element.46), channel_id=1, source_target_pairs={{0,12},{4,0},{8,4},{12,8},{1,13},{5,1},{9,5},{13,9},{2,14},{6,2},{... | collective-permute-start | bytes 196616 | tf_op jit(solution)/shard_map/ppermute | solution.py:396
  40.2 0.8 copy-start.6
  41.8 16.3 %collective-permute-start.5 = (bf16[256,256]{1,0:T(8,128)(2,1)}, bf16[256,256]{1,0:T(8,128)(2,1)S(1)}, u32[]{:S(2)}, u32[]{:S(2)}) collective-permute-start(bf16[256,256]{1,0:T(8,128)(2,1)} %get-tuple-element.47.refs_0_), channel_id=1, source_target_pairs={{0,48},{16,0},{32,16},{48,32},{1,49},{17,1},{33,17},{49,33},{2,50}... | collective-permute-start | bytes 393224 | tf_op jit(solution)/shard_map/ppermute | solution.py:95
  45.7 12.4 %collective-permute-start.4 = (bf16[256,256]{1,0:T(8,128)(2,1)}, bf16[256,256]{1,0:T(8,128)(2,1)S(1)}, u32[]{:S(2)}, u32[]{:S(2)}) collective-permute-start(bf16[256,256]{1,0:T(8,128)(2,1)} %get-tuple-element.47.refs_0_), channel_id=1, source_target_pairs={{0,32},{16,48},{32,0},{48,16},{1,33},{17,49},{33,1},{49,17},{2,34}... | collective-permute-start | bytes 393224 | tf_op jit(solution)/shard_map/ppermute | solution.py:95
  49.3 8.9 %collective-permute-start.3 = (bf16[256,256]{1,0:T(8,128)(2,1)}, bf16[256,256]{1,0:T(8,128)(2,1)S(1)}, u32[]{:S(2)}, u32[]{:S(2)}) collective-permute-start(bf16[256,256]{1,0:T(8,128)(2,1)} %get-tuple-element.47.refs_0_), channel_id=1, source_target_pairs={{0,16},{16,32},{32,48},{48,0},{1,17},{17,33},{33,49},{49,1},{2,18}... | collective-permute-start | bytes 393224 | tf_op jit(solution)/shard_map/ppermute | solution.py:95
  58.1 0.9 copy-start.5
  59.9 18.4 %collective-permute-start.11 = (bf16[1024,256]{1,0:T(8,128)(2,1)}, bf16[1024,256]{1,0:T(8,128)(2,1)}, u32[]{:S(2)}, u32[]{:S(2)}) collective-permute-start(bf16[1024,256]{1,0:T(8,128)(2,1)} %shard_map.112.refs_2_), channel_id=1, source_target_pairs={{0,192},{64,0},{128,64},{192,128},{1,193},{65,1},{129,65},{193,129... | collective-permute-start | bytes 1572872 | tf_op jit(solution)/shard_map/ppermute | solution.py:95
  63.3 15.0 %collective-permute-start.10 = (bf16[1024,256]{1,0:T(8,128)(2,1)}, bf16[1024,256]{1,0:T(8,128)(2,1)}, u32[]{:S(2)}, u32[]{:S(2)}) collective-permute-start(bf16[1024,256]{1,0:T(8,128)(2,1)} %shard_map.112.refs_2_), channel_id=1, source_target_pairs={{0,64},{64,128},{128,192},{192,0},{1,65},{65,129},{129,193},{193,1... | collective-permute-start | bytes 1572872 | tf_op jit(solution)/shard_map/ppermute | solution.py:95
  63.3 21.9 %collective-permute-start.6 = (bf16[1024,256]{1,0:T(8,128)(2,1)}, bf16[1024,256]{1,0:T(8,128)(2,1)S(1)}, u32[]{:S(2)}, u32[]{:S(2)}) collective-permute-start(bf16[1024,256]{1,0:T(8,128)(2,1)} %shard_map.112.refs_2_), channel_id=1, source_target_pairs={{0,128},{64,192},{128,0},{192,64},{1,129},{65,193},{129,1},{193,65... | collective-permute-start | bytes 1572872 | tf_op jit(solution)/shard_map/ppermute | solution.py:95
  64.8 5.5 %collective-permute-start.9 = (bf16[256,256]{1,0:T(8,128)(2,1)}, bf16[256,256]{1,0:T(8,128)(2,1)S(1)}, u32[]{:S(2)}, u32[]{:S(2)}) collective-permute-start(bf16[256,256]{1,0:T(8,128)(2,1)} %get-tuple-element.51.refs_0_), channel_id=1, source_target_pairs={{0,48},{16,0},{32,16},{48,32},{1,49},{17,1},{33,17},{49,33},{2,50}... | collective-permute-start | bytes 393224 | tf_op jit(solution)/shard_map/ppermute | solution.py:95
  65.1 8.2 %collective-permute-start.8 = (bf16[256,256]{1,0:T(8,128)(2,1)}, bf16[256,256]{1,0:T(8,128)(2,1)S(1)}, u32[]{:S(2)}, u32[]{:S(2)}) collective-permute-start(bf16[256,256]{1,0:T(8,128)(2,1)} %get-tuple-element.51.refs_0_), channel_id=1, source_target_pairs={{0,32},{16,48},{32,0},{48,16},{1,33},{17,49},{33,1},{49,17},{2,34}... | collective-permute-start | bytes 393224 | tf_op jit(solution)/shard_map/ppermute | solution.py:95
  70.3 6.2 %collective-permute-start.7 = (bf16[256,256]{1,0:T(8,128)(2,1)}, bf16[256,256]{1,0:T(8,128)(2,1)S(1)}, u32[]{:S(2)}, u32[]{:S(2)}) collective-permute-start(bf16[256,256]{1,0:T(8,128)(2,1)} %get-tuple-element.51.refs_0_), channel_id=1, source_target_pairs={{0,16},{16,32},{32,48},{48,0},{1,17},{17,33},{33,49},{49,1},{2,18}... | collective-permute-start | bytes 393224 | tf_op jit(solution)/shard_map/ppermute | solution.py:95
  76.5 0.9 copy-start.4
  84.1 1.0 copy-start.1
  85.2 1.2 copy-start.2
  86.4 30.2 %copy-start.3 = (f32[2,64,256]{2,1,0:T(8,128)S(1)}, f32[2,64,256]{2,1,0:T(8,128)}, u32[]{:S(2)}) copy-start(f32[2,64,256]{2,1,0:T(8,128)} %constant.37.clone.turn) | copy-start | bytes 393220
  86.4 30.2 %copy-start.7 = (bf16[128,64]{1,0:T(8,128)(2,1)S(1)}, bf16[128,64]{1,0:T(8,128)(2,1)}, u32[]{:S(2)}) copy-start(bf16[128,64]{1,0:T(8,128)(2,1)} %constant.35.clone.first) | copy-start | bytes 49156
  86.4 30.2 %copy-start.8 = (bf16[64,128]{1,0:T(8,128)(2,1)S(1)}, bf16[64,128]{1,0:T(8,128)(2,1)}, u32[]{:S(2)}) copy-start(bf16[64,128]{1,0:T(8,128)(2,1)} %constant.36.clone.last) | copy-start | bytes 49156
  90.3 26.2 %all-to-all-start.1 = ((bf16[16,4,16,256]{3,2,1,0:T(8,128)(2,1)}), bf16[16,4,16,256]{3,2,1,0:T(8,128)(2,1)S(1)}, u32[]{:S(2)}, u32[]{:S(2)}) async-start(bf16[16,4,16,256]{3,2,1,0:T(8,128)(2,1)} %get-tuple-element.56), calls=%async_computation.1 | async-start | bytes 1048576 | tf_op jit(solution)/shard_map/all_to_all | solution.py:411
  102.5 10.2 %collective-permute-start.12 = (bf16[256,256]{1,0:T(8,128)(2,1)S(1)}, bf16[256,256]{1,0:T(8,128)(2,1)S(1)}, u32[]{:S(2)}, u32[]{:S(2)}) collective-permute-start(bf16[256,256]{1,0:T(8,128)(2,1)S(1)} %get-tuple-element.58), channel_id=1, source_target_pairs={{0,4},{4,8},{8,12},{12,0},{1,5},{5,9},{9,13},{13,1},{2,6},{6,10},{... | collective-permute-start | bytes 393224 | tf_op jit(solution)/shard_map/ppermute | solution.py:382
  108.9 7.0 %collective-permute-start.13 = (bf16[256,256]{1,0:T(8,128)(2,1)S(1)}, bf16[256,256]{1,0:T(8,128)(2,1)S(1)}, u32[]{:S(2)}, u32[]{:S(2)}) collective-permute-start(bf16[256,256]{1,0:T(8,128)(2,1)S(1)} %get-tuple-element.59), channel_id=1, source_target_pairs={{0,8},{4,12},{8,0},{12,4},{1,9},{5,13},{9,1},{13,5},{2,10},{6,14},... | collective-permute-start | bytes 393224 | tf_op jit(solution)/shard_map/ppermute | solution.py:382
  111.6 5.0 %collective-permute-start.14 = (bf16[256,256]{1,0:T(8,128)(2,1)S(1)}, bf16[256,256]{1,0:T(8,128)(2,1)}, u32[]{:S(2)}, u32[]{:S(2)}) collective-permute-start(bf16[256,256]{1,0:T(8,128)(2,1)S(1)} %get-tuple-element.60), channel_id=1, source_target_pairs={{0,12},{4,0},{8,4},{12,8},{1,13},{5,1},{9,5},{13,9},{2,14},{6,2},{... | collective-permute-start | bytes 393224 | tf_op jit(solution)/shard_map/ppermute | solution.py:382
  112.7 3.2 %copy-start.9 = (bf16[256,256]{1,0:T(8,128)(2,1)}, bf16[256,256]{1,0:T(8,128)(2,1)S(1)}, u32[]{:S(2)}) copy-start(bf16[256,256]{1,0:T(8,128)(2,1)S(1)} %collective-permute-done.12.refs_0_) | copy-start | bytes 393220
  115.9 0.6 copy-start.10
  122.7 28.2 %all-to-all-start.2 = ((bf16[64,16,256]{2,1,0:T(8,128)(2,1)}), bf16[64,16,256]{2,1,0:T(8,128)(2,1)S(1)}, u32[]{:S(2)}, u32[]{:S(2)}) async-start(bf16[64,16,256]{2,1,0:T(8,128)(2,1)} %bitcast.10), calls=%async_computation.2 | async-start | bytes 1048576 | tf_op jit(solution)/shard_map/all_to_all | solution.py:416
  134.9 12.6 %copy-start.11 = (f32[1024]{0:T(1024)S(1)}, f32[1024]{0:T(1024)}, u32[]{:S(2)}) copy-start(f32[1024]{0:T(1024)} %param.15) | copy-start | bytes 12292
  142.8 8.1 %collective-permute-start.15 = (bf16[256,256]{1,0:T(8,128)(2,1)}, bf16[256,256]{1,0:T(8,128)(2,1)}, u32[]{:S(2)}, u32[]{:S(2)}) collective-permute-start(bf16[256,256]{1,0:T(8,128)(2,1)} %get-tuple-element.69), channel_id=1, source_target_pairs={{0,4},{4,8},{8,12},{12,0},{1,5},{5,9},{9,13},{13,1},{2,6},{6,10},{... | collective-permute-start | bytes 393224 | tf_op jit(solution)/shard_map/ppermute | solution.py:382
  143.9 8.5 %collective-permute-start.16 = (bf16[256,256]{1,0:T(8,128)(2,1)}, bf16[256,256]{1,0:T(8,128)(2,1)}, u32[]{:S(2)}, u32[]{:S(2)}) collective-permute-start(bf16[256,256]{1,0:T(8,128)(2,1)} %get-tuple-element.70), channel_id=1, source_target_pairs={{0,8},{4,12},{8,0},{12,4},{1,9},{5,13},{9,1},{13,5},{2,10},{6,14},... | collective-permute-start | bytes 393224 | tf_op jit(solution)/shard_map/ppermute | solution.py:382
  146.5 5.9 %collective-permute-start.17 = (bf16[256,256]{1,0:T(8,128)(2,1)S(1)}, bf16[256,256]{1,0:T(8,128)(2,1)}, u32[]{:S(2)}, u32[]{:S(2)}) collective-permute-start(bf16[256,256]{1,0:T(8,128)(2,1)S(1)} %get-tuple-element.71), channel_id=1, source_target_pairs={{0,12},{4,0},{8,4},{12,8},{1,13},{5,1},{9,5},{13,9},{2,14},{6,2},{... | collective-permute-start | bytes 393224 | tf_op jit(solution)/shard_map/ppermute | solution.py:382
  155.7 7.5 %collective-permute-start.18 = (bf16[256,1024]{1,0:T(8,128)(2,1)S(1)}, bf16[256,1024]{1,0:T(8,128)(2,1)S(1)}, u32[]{:S(2)}, u32[]{:S(2)}) collective-permute-start(bf16[256,1024]{1,0:T(8,128)(2,1)S(1)} %get-tuple-element.73), channel_id=1, source_target_pairs={{0,1},{1,0},{2,3},{3,2},{4,5},{5,4},{6,7},{7,6},{8,9},{9,8},{10,11... | collective-permute-start | bytes 1572872 | tf_op jit(solution)/shard_map/ppermute | solution.py:422
  163.3 13.6 %collective-permute-start.20 = (bf16[256,1024]{1,0:T(8,128)(2,1)S(1)}, bf16[256,1024]{1,0:T(8,128)(2,1)S(1)}, u32[]{:S(2)}, u32[]{:S(2)}) collective-permute-start(bf16[256,1024]{1,0:T(8,128)(2,1)S(1)} %add_convert_fusion.1), channel_id=1, source_target_pairs={{0,2},{2,0},{1,3},{3,1},{4,6},{6,4},{5,7},{7,5},{8,10},{10,8},{9,1... | collective-permute-start | bytes 1572872 | tf_op jit(solution)/shard_map/ppermute | solution.py:425
  167.4 9.6 %collective-permute-start.19 = (bf16[256,1024]{1,0:T(8,128)(2,1)S(1)}, bf16[256,1024]{1,0:T(8,128)(2,1)S(1)}, u32[]{:S(2)}, u32[]{:S(2)}) collective-permute-start(bf16[256,1024]{1,0:T(8,128)(2,1)S(1)} %get-tuple-element.76), channel_id=1, source_target_pairs={{0,1},{1,0},{2,3},{3,2},{4,5},{5,4},{6,7},{7,6},{8,9},{9,8},{10,11... | collective-permute-start | bytes 1572872 | tf_op jit(solution)/shard_map/ppermute | solution.py:428
Sparse Core Ops, SparseCore 0:
  10.4 68.1 all-gather.2
  85.3 47.5 all-gather.4
